TPU v7x, 512 devices: a whole 4x4x16 slice. The times are simulated.
512 devices in a mesh: grp: 16 (over z_lo, x), fsdp: 4 (over y), tp: 8 (over z_hi, core).
Axes of the slice: x: 4, y: 4, z: 16 (z_hi: 4, z_lo: 4; z = z_hi * 4 + z_lo), core: 2. Of those that a mesh axis runs over, the one named last changes fastest.
Arguments:
- frames: bfloat16 [3072, 5120], P('fsdp', 'grp'), may hold values from -6 to 6
- projector: bfloat16 [5120, 8192], P('grp', 'tp'), may hold values from -0.078125 to 0.078125
- text_token_embedding: bfloat16 [16384, 8192], P(('grp', 'fsdp'), 'tp'), may hold values from -6 to 6
- norm_gain_vector: float32 [8192], replicated, may hold values from 0.1 to 1.9
- frozen: bfloat16 [8192, 1024], P('fsdp', 'tp'), may hold values from -0.0625 to 0.0625
- adapter_down_map: bfloat16 [8192, 64], P('fsdp'), may hold values from -0.0625 to 0.0625
- adapter_up_map: bfloat16 [64, 1024], P(None, 'tp'), may hold values from -0.75 to 0.75
- clip_frame_length: int32 [4, 16, 16], P('fsdp'), may hold values from 1 to 6, as said below
- audio_first_token: int32 [4, 16, 16], P('fsdp'), may hold values from 0 to 255, as said below
- segment_document_index: int32 [16384], P(('grp', 'fsdp')), may hold values from 0 to 255, never falling along the last dimension, each value on 1 to 256 neighbouring positions
- keep_document_flags: int32 [256], replicated, may hold values 0 or 1
- cotangent: bfloat16 [16384, 1024], P(('grp', 'fsdp'), 'tp'), may hold values from -0.046875 to 0.046875
Outputs:
- value_output: bfloat16 [16384, 1024], P(('grp', 'fsdp'), 'tp')
- projector_grad: float32 [5120, 8192], P('grp', 'tp')
- down_map_gradient: float32 [8192, 64], P('tp')
- up_map_gradient: float32 [64, 1024], P(None, 'tp')
Inputs may be any that keep to these rules, and one draw needn't show every extreme that they name: `clip_frame_length`: entry [f, g, k] is the length of clip k of frame block f * 16 + g; the 16 clips of a block sum to 48, and one of them has exactly 6 frames. `audio_first_token`: entry [f, g, k] is the first token, among the 256 tokens of block k * 4 + f, of the audio slots of clip k of frame block f * 16 + g; the 16 clips that one token block takes lie in distinct aligned windows of 16 tokens.
All inputs are finite; a program needn't handle non-finite values.
Results may differ from a plain program's by a relative error of at most 0.018.
Values may be sent and summed in bfloat16 or wider, within the bound.
No kernel may reach another device: no remote copies, remote signals or barrier semaphores. Data moves between devices by JAX's collectives and lax.ppermute only.
A program may use at most 128 MiB of HBM per device.

v0:
```python
import jax
import jax.numpy as jnp
from jax import lax
from jax.sharding import PartitionSpec as P

adapter_scale = 2.0
norm_eps = 1e-05


def in_blocks(x, dim, length):
    shape = x.shape
    blocks = x.reshape(*shape[:dim], length, shape[dim] // length, *shape[dim + 1 :])
    return jnp.moveaxis(blocks, dim, 0)


def sent_and_summed(x, axis, dim):
    length = lax.axis_size(axis)
    blocks = lax.all_to_all(in_blocks(x, dim, length), axis, 0, 0, tiled=True)
    return jnp.sum(blocks.astype(jnp.float32), axis=0)


def side_by_side(arrays, axis, dim, along):
    ends, at = ([], 0)
    for a in arrays[:-1]:
        at += a.shape[along]
        ends.append(at)
    both = jnp.concatenate(arrays, axis=along)
    return tuple(jnp.split(lax.all_gather(both, axis, axis=dim, tiled=True), ends, axis=along))


def copy_for_each(x, axis):
    copies = jnp.broadcast_to(x, (lax.axis_size(axis), *x.shape))
    return lax.all_to_all(copies, axis, split_axis=0, concat_axis=0, tiled=True)


def over_copies(x, axis):
    return copy_for_each(x, axis).astype(jnp.float32).sum(axis=0)


def rows_for(lines, length):
    spare = -len(lines) % length
    return jnp.pad(lines, [(0, spare)] + [(0, 0)] * (lines.ndim - 1))


def in_order(blocks, dim):
    shape = list(blocks.shape[1:])
    shape[dim] *= blocks.shape[0]
    return jnp.moveaxis(blocks, 0, dim).reshape(shape)


def collect(x, axis, dim):
    return in_order(copy_for_each(x, axis), dim)


def sum_at_owner(x, axis, dim):
    blocks = in_blocks(x, dim, lax.axis_size(axis))
    arrived = lax.all_to_all(blocks, axis, split_axis=0, concat_axis=0, tiled=True)
    return arrived.sum(axis=0)


def total_of(x, axes):
    padded = rows_for(x, lax.axis_size(axes))
    whole = collect(sum_at_owner(padded, axes, 0), axes, 0)
    return lax.slice_in_dim(whole, 0, len(x)).reshape(x.shape)


def together(arrays, axis):
    flat, at, outs = (jnp.concatenate([a.reshape(-1) for a in arrays]), 0, [])
    so_far = total_of(flat, axis)
    for a in arrays:
        outs.append(so_far[at : at + a.size].reshape(a.shape))
        at += a.size
    return tuple(outs)


def pick_entry(grid_in, position, which_axis):
    matches = lax.broadcasted_iota(jnp.int32, grid_in.shape, which_axis) == position
    return jnp.sum(jnp.where(matches, grid_in, 0), axis=which_axis)


def contract_leading(left_side, right_side):
    return lax.dot_general(
        left_side, right_side, (((0,), (0,)), ((), ())), preferred_element_type=jnp.float32
    )


def contract_trailing(left_side, right_side):
    return lax.dot_general(
        left_side, right_side, (((1,), (1,)), ((), ())), preferred_element_type=jnp.float32
    )


def shards(
    frames,
    projector,
    text_token_embedding,
    norm_gain_vector,
    frozen,
    adapter_down_map,
    adapter_up_map,
    clip_frame_length,
    audio_first_token,
    segment_document_index,
    keep_document_flags,
    cotangent,
):
    grp_index = lax.axis_index("grp")
    tensor_shard_index = lax.axis_index("tp")
    tok_count, tensor_shard_width = text_token_embedding.shape
    group_count = clip_frame_length.shape[1]
    frame_count = frames.shape[0] // group_count
    slot_cap = 2 * frame_count // group_count
    slot_total = group_count * slot_cap
    full_width = tensor_shard_width * lax.axis_size("tp")
    own_sizes = pick_entry(clip_frame_length[0], grp_index, 0)
    own_starts = jnp.cumsum(own_sizes) - own_sizes
    slot_offset = lax.broadcasted_iota(jnp.int32, (group_count, slot_cap), 1)
    frame_slot = own_starts[:, None] + slot_offset
    slot_live = slot_offset < own_sizes[:, None]
    frame_iota = lax.broadcasted_iota(jnp.int32, (group_count, slot_cap, frame_count), 2)
    sender = (
        ((frame_iota == frame_slot[:, :, None]) & slot_live[:, :, None])
        .astype(jnp.bfloat16)
        .reshape(slot_total, frame_count)
    )
    in_sizes = pick_entry(clip_frame_length[0], grp_index, 1)
    arrive_at = pick_entry(audio_first_token[0], grp_index, 1)
    token_iota = lax.broadcasted_iota(jnp.int32, (tok_count, group_count, slot_cap), 0)
    receive_mask = (token_iota == (arrive_at[:, None] + slot_offset)[None]) & (
        slot_offset < in_sizes[:, None]
    )[None]
    receiving_device = receive_mask.astype(jnp.bfloat16).reshape(tok_count, slot_total)
    is_audio = jnp.any(receive_mask, axis=(1, 2))
    embedded = sent_and_summed(
        jnp.dot(frames, projector, preferred_element_type=jnp.float32).astype(jnp.bfloat16),
        "grp",
        0,
    ).astype(jnp.bfloat16)
    outgoing = (
        jnp.dot(sender, embedded, preferred_element_type=jnp.float32)
        .astype(jnp.bfloat16)
        .reshape(group_count, slot_cap, tensor_shard_width)
    )
    incoming = lax.all_to_all(outgoing, "grp", split_axis=0, concat_axis=0, tiled=True).reshape(
        slot_total, tensor_shard_width
    )
    audio_part = jnp.dot(receiving_device, incoming, preferred_element_type=jnp.float32).astype(
        jnp.bfloat16
    )
    inputs = jnp.where(is_audio[:, None], audio_part, text_token_embedding)
    gathered = lax.all_gather(inputs, "tp", axis=1, tiled=True)
    widened = gathered.astype(jnp.float32)
    mean_sq = jnp.mean(widened * widened, axis=1)
    inv_rms = lax.rsqrt(mean_sq + norm_eps)
    normalized_input = (widened * inv_rms[:, None] * norm_gain_vector[None, :]).astype(jnp.bfloat16)
    frozen_complete, adapter_complete = side_by_side((frozen, adapter_down_map), "fsdp", 0, 1)
    base_output = jnp.dot(normalized_input, frozen_complete, preferred_element_type=jnp.float32)
    lower_rank_rows = jnp.dot(
        normalized_input, adapter_complete, preferred_element_type=jnp.float32
    )
    lower_halfway = lower_rank_rows.astype(jnp.bfloat16)
    value_output = (
        base_output
        + adapter_scale * jnp.dot(lower_halfway, adapter_up_map, preferred_element_type=jnp.float32)
    ).astype(jnp.bfloat16)
    doc_iota = lax.broadcasted_iota(jnp.int32, (tok_count, keep_document_flags.shape[0]), 1)
    weight_tok = jnp.sum(
        jnp.where(segment_document_index[:, None] == doc_iota, keep_document_flags[None, :], 0),
        axis=1,
    )
    output_gradient = cotangent * weight_tok.astype(jnp.bfloat16)[:, None]
    adapter_portion = adapter_scale * contract_trailing(output_gradient, adapter_up_map)
    dot_portion = jnp.sum(output_gradient.astype(jnp.float32) * base_output, axis=1) + jnp.sum(
        adapter_portion * lower_rank_rows, axis=1
    )
    adapter_gradient, row_dot_products = (
        over_copies(adapter_portion.astype(jnp.bfloat16), "tp").astype(jnp.float32),
        over_copies(dot_portion.astype(jnp.bfloat16), "tp").astype(jnp.float32),
    )
    adapter_halfway = adapter_gradient.astype(jnp.bfloat16)
    up_portion = adapter_scale * contract_leading(lower_halfway, output_gradient)
    local_normalized = lax.dynamic_slice_in_dim(
        normalized_input, tensor_shard_index * tensor_shard_width, tensor_shard_width, 1
    )
    down_portion = contract_leading(local_normalized, adapter_halfway)
    down_map_gradient, up_map_gradient = together((down_portion, up_portion), ("grp", "fsdp"))
    slot_grad = contract_leading(receiving_device, output_gradient).astype(jnp.bfloat16)
    slot_adapter = contract_leading(receiving_device, adapter_halfway).astype(jnp.bfloat16)
    slot_stats = lax.dot_general(
        receiving_device.astype(jnp.float32),
        jnp.stack([inv_rms, row_dot_products], axis=1),
        (((0,), (0,)), ((), ())),
        precision=lax.Precision.HIGHEST,
        preferred_element_type=jnp.float32,
    )
    spread_rows = contract_trailing(slot_grad, frozen_complete)
    reduced_result = lax.psum_scatter(
        spread_rows.astype(jnp.bfloat16), "tp", scatter_dimension=1, tiled=True
    ).astype(jnp.float32)
    local_adapter = lax.dynamic_slice_in_dim(
        adapter_complete, tensor_shard_index * tensor_shard_width, tensor_shard_width, 0
    )
    gradient_norm = reduced_result + contract_trailing(slot_adapter, local_adapter)
    own_gain = lax.dynamic_slice_in_dim(
        norm_gain_vector, tensor_shard_index * tensor_shard_width, tensor_shard_width, 0
    )
    slot_inv = slot_stats[:, 0:1]
    slot_dot = slot_stats[:, 1:2]
    grad_rows = (
        slot_inv * own_gain[None, :] * gradient_norm
        - incoming.astype(jnp.float32) * (slot_inv * slot_inv * slot_dot / full_width)
    ).astype(jnp.bfloat16)
    returned = lax.all_to_all(
        grad_rows.reshape(group_count, slot_cap, tensor_shard_width),
        "grp",
        split_axis=0,
        concat_axis=0,
        tiled=True,
    ).reshape(slot_total, tensor_shard_width)
    frame_grad = contract_leading(sender, returned).astype(jnp.bfloat16)
    proj_part = contract_leading(frames, collect(frame_grad, "grp", 0))
    projector_grad = over_copies(proj_part.astype(jnp.bfloat16), "fsdp").astype(jnp.float32)
    return (value_output, projector_grad, down_map_gradient, up_map_gradient)


def solution(mesh):
    in_specs = (
        P("fsdp", "grp"),
        P("grp", "tp"),
        P(("grp", "fsdp"), "tp"),
        P(),
        P("fsdp", "tp"),
        P("fsdp", None),
        P(None, "tp"),
        P("fsdp", None, None),
        P("fsdp", None, None),
        P(("grp", "fsdp")),
        P(),
        P(("grp", "fsdp"), "tp"),
    )
    out_specs = (P(("grp", "fsdp"), "tp"), P("grp", "tp"), P("tp", None), P(None, "tp"))
    return jax.shard_map(shards, mesh=mesh, in_specs=in_specs, out_specs=out_specs, check_vma=False)
```

profile of v0, /device:TPU:8, one launch (start us, length us, event | category | flops | bytes accessed | tf_op | source)
XLA Modules:
  0.0 395.0 jit_solution(4861010309446714678)
XLA Ops:
  8.3 3.2 convolution_convert_fusion.1
  11.5 8.6 %all-to-all-start = ((bf16[16,48,1024]{2,1,0:T(8,128)(2,1)}), bf16[16,48,1024]{2,1,0:T(8,128)(2,1)S(1)}, u32[]{:S(2)}, u32[]{:S(2)}) async-start(bf16[16,48,1024]{2,1,0:T(8,128)(2,1)} %bitcast.51), calls=%async_computation | async-start | bytes 3145728 | tf_op jit(solution)/shard_map/all_to_all | solution.py:18
  23.1 30.8 %all-to-all-done = bf16[16,48,1024]{2,1,0:T(8,128)(2,1)S(1)} async-done(((bf16[16,48,1024]{2,1,0:T(8,128)(2,1)}), bf16[16,48,1024]{2,1,0:T(8,128)(2,1)S(1)}, u32[]{:S(2)}, u32[]{:S(2)}) %all-to-all-start) | async-done | bytes 1572896 | tf_op jit(solution)/shard_map/all_to_all | solution.py:18
  55.3 8.3 %all-to-all-start.1 = ((bf16[16,6,1024]{2,1,0:T(8,128)(2,1)}), bf16[16,6,1024]{2,1,0:T(8,128)(2,1)S(1)}, u32[]{:S(2)}, u32[]{:S(2)}) async-start(bf16[16,6,1024]{2,1,0:T(8,128)(2,1)} %reshape.193), calls=%async_computation.1 | async-start | bytes 524288 | tf_op jit(solution)/shard_map/all_to_all | solution.py:144
  63.8 9.8 %all-to-all-done.1 = bf16[16,6,1024]{2,1,0:T(8,128)(2,1)S(1)} async-done(((bf16[16,6,1024]{2,1,0:T(8,128)(2,1)}), bf16[16,6,1024]{2,1,0:T(8,128)(2,1)S(1)}, u32[]{:S(2)}, u32[]{:S(2)}) %all-to-all-start.1) | async-done | bytes 196640 | tf_op jit(solution)/shard_map/all_to_all | solution.py:144
  76.2 4.8 %all-gather.5.cloned.1.call-done = bf16[8192,192]{1,0:T(8,128)(2,1)} async-done(((bf16[2048,192]{1,0:T(8,128)(2,1)}), bf16[8192,192]{1,0:T(8,128)(2,1)}) %all-gather.5.cloned.1.call-update) | async-done | bytes 3145744 | tf_op jit(solution)/shard_map/all_gather | solution.py:28
  81.0 3.8 convolution_convert_fusion
  84.9 96.2 %all-gather.3.cloned.1.call-done = bf16[256,8192]{1,0:T(8,128)(2,1)} async-done(((bf16[256,1024]{1,0:T(8,128)(2,1)}), bf16[256,8192]{1,0:T(8,128)(2,1)}) %all-gather.3.cloned.1.call-update) | async-done | bytes 4194320 | tf_op jit(solution)/shard_map/all_gather | solution.py:151
  181.0 3.3 fusion
  191.4 18.8 %all_to_all.51 = bf16[8,2,128]{2,1,0:T(2,128)(2,1)S(1)} all-to-all(bf16[8,2,128]{2,1,0:T(2,128)(2,1)S(1)} %reshape.203), channel_id=1, replica_groups=mesh['grp'=16,'fsdp'=4,'tp'=8] {'tp'}, dimensions={0} | all-to-all | bytes 8192 | tf_op jit(solution)/shard_map/all_to_all | solution.py:33
  210.9 4.0 %all-to-all-start.3 = ((bf16[8,256,64]{1,2,0:T(8,128)(2,1)}), bf16[8,256,64]{1,2,0:T(8,128)(2,1)}, u32[]{:S(2)}, u32[]{:S(2)}) async-start(bf16[8,256,64]{1,2,0:T(8,128)(2,1)} %broadcast_in_dim.61), calls=%async_computation.4 | async-start | bytes 524288 | tf_op jit(solution)/shard_map/all_to_all | solution.py:33
  217.3 21.4 %all-to-all-done.3 = bf16[8,256,64]{1,2,0:T(8,128)(2,1)} async-done(((bf16[8,256,64]{1,2,0:T(8,128)(2,1)}), bf16[8,256,64]{1,2,0:T(8,128)(2,1)}, u32[]{:S(2)}, u32[]{:S(2)}) %all-to-all-start.3) | async-done | bytes 262176 | tf_op jit(solution)/shard_map/all_to_all | solution.py:33
  241.9 7.1 %reduce-scatter.2.cloned.1.call-done = bf16[96,1024]{1,0:T(8,128)(2,1)} async-done(((bf16[96,8192]{1,0:T(8,128)(2,1)}), bf16[96,1024]{1,0:T(8,128)(2,1)}) %reduce-scatter.2.cloned.1.call-update) | async-done | bytes 196624 | tf_op jit(solution)/shard_map/reduce_scatter | solution.py:197
  251.4 7.9 %all-to-all-start.4 = ((bf16[16,6,1024]{2,1,0:T(8,128)(2,1)}), bf16[16,6,1024]{2,1,0:T(8,128)(2,1)S(1)}, u32[]{:S(2)}, u32[]{:S(2)}) async-start(bf16[16,6,1024]{2,1,0:T(8,128)(2,1)} %reshape.194), calls=%async_computation.5 | async-start | bytes 524288 | tf_op jit(solution)/shard_map/all_to_all | solution.py:213
  261.0 10.2 %all-to-all-done.4 = bf16[16,6,1024]{2,1,0:T(8,128)(2,1)S(1)} async-done(((bf16[16,6,1024]{2,1,0:T(8,128)(2,1)}), bf16[16,6,1024]{2,1,0:T(8,128)(2,1)S(1)}, u32[]{:S(2)}, u32[]{:S(2)}) %all-to-all-start.4) | async-done | bytes 196640 | tf_op jit(solution)/shard_map/all_to_all | solution.py:213
  271.1 6.9 %all-to-all-start.7 = ((f32[64,1,1152]{2,1,0:T(1,128)}), f32[64,1,1152]{2,1,0:T(1,128)S(1)}, u32[]{:S(2)}, u32[]{:S(2)}) async-start(f32[64,1,1152]{2,1,0:T(1,128)} %bitcast.13), calls=%async_computation.8 | async-start | bytes 589824 | tf_op jit(solution)/shard_map/all_to_all | solution.py:57
  278.7 12.1 %all-to-all-done.7 = f32[64,1,1152]{2,1,0:T(1,128)S(1)} async-done(((f32[64,1,1152]{2,1,0:T(1,128)}), f32[64,1,1152]{2,1,0:T(1,128)S(1)}, u32[]{:S(2)}, u32[]{:S(2)}) %all-to-all-start.7) | async-done | bytes 294944 | tf_op jit(solution)/shard_map/all_to_all | solution.py:57
  292.2 3.9 all-to-all-start.5
  296.3 32.3 %all-to-all-done.5 = bf16[16,48,1024]{2,1,0:T(8,128)(2,1)S(1)} async-done(((bf16[16,48,1024]{2,1,0:T(8,128)(2,1)}), bf16[16,48,1024]{2,1,0:T(8,128)(2,1)S(1)}, u32[]{:S(2)}, u32[]{:S(2)}) %all-to-all-start.5) | async-done | bytes 1572896 | tf_op jit(solution)/shard_map/all_to_all | solution.py:33
  329.5 11.2 %all-to-all-start.8 = ((f32[64,1,1152]{2,1,0:T(1,128)}), f32[64,1,1152]{2,1,0:T(1,128)S(1)}, u32[]{:S(2)}, u32[]{:S(2)}) async-start(f32[64,1,1152]{2,1,0:T(1,128)} %broadcast_in_dim.64), calls=%async_computation.9 | async-start | bytes 589824 | tf_op jit(solution)/shard_map/all_to_all | solution.py:33
  342.3 9.6 %all-to-all-done.8 = f32[64,1,1152]{2,1,0:T(1,128)S(1)} async-done(((f32[64,1,1152]{2,1,0:T(1,128)}), f32[64,1,1152]{2,1,0:T(1,128)S(1)}, u32[]{:S(2)}, u32[]{:S(2)}) %all-to-all-start.8) | async-done | bytes 294944 | tf_op jit(solution)/shard_map/all_to_all | solution.py:33
  353.8 5.1 %all-to-all-start.6 = ((bf16[4,320,1024]{2,1,0:T(8,128)(2,1)}), bf16[4,320,1024]{2,1,0:T(8,128)(2,1)S(1)}, u32[]{:S(2)}, u32[]{:S(2)}) async-start(bf16[4,320,1024]{2,1,0:T(8,128)(2,1)} %broadcast_in_dim.63), calls=%async_computation.7 | async-start | bytes 5242880 | tf_op jit(solution)/shard_map/all_to_all | solution.py:33
  359.8 2.4 reduce.5
  369.3 17.7 %all-to-all-done.6 = bf16[4,320,1024]{2,1,0:T(8,128)(2,1)S(1)} async-done(((bf16[4,320,1024]{2,1,0:T(8,128)(2,1)}), bf16[4,320,1024]{2,1,0:T(8,128)(2,1)S(1)}, u32[]{:S(2)}, u32[]{:S(2)}) %all-to-all-start.6) | async-done | bytes 2621472 | tf_op jit(solution)/shard_map/all_to_all | solution.py:33
  (119 shorter events, 41.6 us)
Async XLA Ops:
  7.2 13.0 %copy-start.6 = (bf16[2048,64]{0,1:T(8,128)(2,1)S(1)}, bf16[2048,64]{0,1:T(8,128)(2,1)}, u32[]{:S(2)}) copy-start(bf16[2048,64]{0,1:T(8,128)(2,1)} %param.17) | copy-start | bytes 786436
  7.2 13.2 %copy-start.5 = (bf16[2048,128]{1,0:T(8,128)(2,1)S(1)}, bf16[2048,128]{1,0:T(8,128)(2,1)}, u32[]{:S(2)}) copy-start(bf16[2048,128]{1,0:T(8,128)(2,1)} %param.16) | copy-start | bytes 1572868
  11.5 10.2 %copy-start.12 = (s32[1,16,16]{2,1,0:T(8,128)S(1)}, s32[1,16,16]{2,1,0:T(8,128)}, u32[]{:S(2)}) copy-start(s32[1,16,16]{2,1,0:T(8,128)} %param.19) | copy-start | bytes 3076
  11.5 10.2 %copy-start.13 = (s32[1,16,16]{2,1,0:T(8,128)S(1)}, s32[1,16,16]{2,1,0:T(8,128)}, u32[]{:S(2)}) copy-start(s32[1,16,16]{2,1,0:T(8,128)} %param.20) | copy-start | bytes 3076
  11.5 42.5 %all-to-all-start = ((bf16[16,48,1024]{2,1,0:T(8,128)(2,1)}), bf16[16,48,1024]{2,1,0:T(8,128)(2,1)S(1)}, u32[]{:S(2)}, u32[]{:S(2)}) async-start(bf16[16,48,1024]{2,1,0:T(8,128)(2,1)} %bitcast.51), calls=%async_computation | async-start | bytes 3145728 | tf_op jit(solution)/shard_map/all_to_all | solution.py:18
  20.1 61.0 %all-gather.5.cloned.1.call-start = ((), (), s32[]{:S(2)}) async-start(), calls=%async_computation.11 | async-start | bytes 5242880 | tf_op jit(solution)/shard_map/all_gather | solution.py:28
  21.6 54.2 %copy-start.7 = (bf16[256,128]{1,0:T(8,128)(2,1)S(1)}, bf16[256,128]{1,0:T(8,128)(2,1)}, u32[]{:S(2)}) copy-start(bf16[256,128]{1,0:T(8,128)(2,1)} %param.23) | copy-start | bytes 196612
  21.6 54.4 %copy-start.18 = (s32[256]{0:T(256)S(1)}, s32[256]{0:T(256)}, u32[]{:S(2)}) copy-start(s32[256]{0:T(256)} %param.22) | copy-start | bytes 3076
  21.6 54.4 %copy-start.19 = (s32[256]{0:T(256)S(1)}, s32[256]{0:T(256)}, u32[]{:S(2)}) copy-start(s32[256]{0:T(256)} %param.21) | copy-start | bytes 3076
  23.1 193.5 %copy-start.14 = (s32[96]{0:T(128)}, s32[96]{0:T(128)S(1)}, u32[]{:S(2)}) copy-start(s32[96]{0:T(128)S(1)} %get-tuple-element.41) | copy-start | bytes 1156
  23.1 193.4 %copy-start.15 = (pred[96]{0:T(512)(128)(4,1)}, pred[96]{0:T(512)(128)(4,1)S(1)}, u32[]{:S(2)}) copy-start(pred[96]{0:T(512)(128)(4,1)S(1)} %get-tuple-element.39) | copy-start | bytes 292
  55.3 18.3 %all-to-all-start.1 = ((bf16[16,6,1024]{2,1,0:T(8,128)(2,1)}), bf16[16,6,1024]{2,1,0:T(8,128)(2,1)S(1)}, u32[]{:S(2)}, u32[]{:S(2)}) async-start(bf16[16,6,1024]{2,1,0:T(8,128)(2,1)} %reshape.193), calls=%async_computation.1 | async-start | bytes 524288 | tf_op jit(solution)/shard_map/all_to_all | solution.py:144
  63.6 117.5 %all-gather.3.cloned.1.call-start = ((), (), s32[]{:S(2)}) async-start(), calls=%async_computation.10 | async-start | bytes 4718592 | tf_op jit(solution)/shard_map/all_gather | solution.py:151
  75.8 173.2 %reduce-scatter.2.cloned.1.call-start = ((), (), s32[]{:S(2)}) async-start(), calls=%async_computation.12 | async-start | bytes 1769472 | tf_op jit(solution)/shard_map/reduce_scatter | solution.py:197
  84.8 99.5 %copy-start.9 = (f32[8192]{0:T(1024)S(1)}, f32[8192]{0:T(1024)}, u32[]{:S(2)}) copy-start(f32[8192]{0:T(1024)} %param.15) | copy-start | bytes 98308
  210.9 27.8 %all-to-all-start.3 = ((bf16[8,256,64]{1,2,0:T(8,128)(2,1)}), bf16[8,256,64]{1,2,0:T(8,128)(2,1)}, u32[]{:S(2)}, u32[]{:S(2)}) async-start(bf16[8,256,64]{1,2,0:T(8,128)(2,1)} %broadcast_in_dim.61), calls=%async_computation.4 | async-start | bytes 524288 | tf_op jit(solution)/shard_map/all_to_all | solution.py:33
  215.6 33.5 %slice-start = ((bf16[8192,192]{1,0:T(8,128)(2,1)}), bf16[8192,64]{1,0:T(8,128)(2,1)S(1)}, s32[]{:S(2)}) async-start(bf16[8192,192]{1,0:T(8,128)(2,1)} %all-gather.5.cloned.1.call-done), calls=%async_computation.13 | async-start | bytes 4194304 | tf_op jit(solution)/shard_map/split | solution.py:28
  241.9 36.2 %copy-start.17 = (s32[16]{0:T(128)S(1)}, s32[16]{0:T(128)}, u32[]{:S(2)}) copy-start(s32[16]{0:T(128)} %copy-done.16) | copy-start | bytes 196
  241.9 36.4 %copy-start.11 = (s32[16]{0:T(128)S(1)}, s32[16]{0:T(128)}, u32[]{:S(2)}) copy-start(s32[16]{0:T(128)} %copy-done.10) | copy-start | bytes 196
  251.4 19.8 %all-to-all-start.4 = ((bf16[16,6,1024]{2,1,0:T(8,128)(2,1)}), bf16[16,6,1024]{2,1,0:T(8,128)(2,1)S(1)}, u32[]{:S(2)}, u32[]{:S(2)}) async-start(bf16[16,6,1024]{2,1,0:T(8,128)(2,1)} %reshape.194), calls=%async_computation.5 | async-start | bytes 524288 | tf_op jit(solution)/shard_map/all_to_all | solution.py:213
  271.1 19.7 %all-to-all-start.7 = ((f32[64,1,1152]{2,1,0:T(1,128)}), f32[64,1,1152]{2,1,0:T(1,128)S(1)}, u32[]{:S(2)}, u32[]{:S(2)}) async-start(f32[64,1,1152]{2,1,0:T(1,128)} %bitcast.13), calls=%async_computation.8 | async-start | bytes 589824 | tf_op jit(solution)/shard_map/all_to_all | solution.py:57
  292.2 36.4 %all-to-all-start.5 = ((bf16[16,48,1024]{2,1,0:T(8,128)(2,1)}), bf16[16,48,1024]{2,1,0:T(8,128)(2,1)S(1)}, u32[]{:S(2)}, u32[]{:S(2)}) async-start(bf16[16,48,1024]{2,1,0:T(8,128)(2,1)} %broadcast_in_dim.62), calls=%async_computation.6 | async-start | bytes 3145728 | tf_op jit(solution)/shard_map/all_to_all | solution.py:33
  329.5 22.5 %all-to-all-start.8 = ((f32[64,1,1152]{2,1,0:T(1,128)}), f32[64,1,1152]{2,1,0:T(1,128)S(1)}, u32[]{:S(2)}, u32[]{:S(2)}) async-start(f32[64,1,1152]{2,1,0:T(1,128)} %broadcast_in_dim.64), calls=%async_computation.9 | async-start | bytes 589824 | tf_op jit(solution)/shard_map/all_to_all | solution.py:33
  353.8 33.2 %all-to-all-start.6 = ((bf16[4,320,1024]{2,1,0:T(8,128)(2,1)}), bf16[4,320,1024]{2,1,0:T(8,128)(2,1)S(1)}, u32[]{:S(2)}, u32[]{:S(2)}) async-start(bf16[4,320,1024]{2,1,0:T(8,128)(2,1)} %broadcast_in_dim.63), calls=%async_computation.7 | async-start | bytes 5242880 | tf_op jit(solution)/shard_map/all_to_all | solution.py:33
  (8 other events, 13.8 us)
Sparse Core Ops, SparseCore 0:
  23.6 57.3 all-gather.4
  83.2 97.8 all-gather.2
  183.9 65.0 reduce-scatter.1
where the time goes:
time: 397 us; the launch traced here: 395 us
  waiting for transfers between devices  252 us (63%)
  starting transfers between devices  56 us (14%)
  local copies, waits for them, and re-layouts  21.2 us (5%)
  blocking collectives  18.8 us (5%)
  matrix products  18 us (5%)
  other arithmetic  14.8 us (4%)
  between operations  14.2 us (4%)
    all_gather x1, waiting for transfers between devices, shards(): gathered = lax.all_gather(inputs, 'tp', axis=1, tiled=True)  96.2 us
    all_to_all x4, waiting for transfers between devices, copy_for_each(): return lax.all_to_all(copies, axis, split_axis=0, concat_axis=0, tiled=True)  81 us
    all_to_all x1, waiting for transfers between devices, sent_and_summed(): blocks = lax.all_to_all(in_blocks(x, dim, length), axis, 0, 0, tiled=True)  30.8 us
    all_to_all x4, starting transfers between devices, copy_for_each(): return lax.all_to_all(copies, axis, split_axis=0, concat_axis=0, tiled=True)  24.2 us
    all_to_all x1, blocking collectives, copy_for_each(): return lax.all_to_all(copies, axis, split_axis=0, concat_axis=0, tiled=True)  18.8 us
    all_to_all x1, waiting for transfers between devices, sum_at_owner(): lax.all_to_all(blocks, axis, split_axis=0, concat_axis=0, tiled=True)  12.1 us
    all_to_all x1, waiting for transfers between devices, shards(): lax.all_to_all(grad_rows.reshape(group_count, slot_cap, tensor_shard_widt...  10.2 us
    all_to_all x1, waiting for transfers between devices, shards(): lax.all_to_all(outgoing, 'grp', split_axis=0, concat_axis=0, tiled=True)  9.8 us
  transfers between devices with their start and end apart: 11, of which 11 were waited for; matrix products, arithmetic and copies ran while one was open for 10% of the time, Pallas kernels for 0%

commit v1 on v0

v1 whole, which is shorter than its diff:
```python
import jax
import jax.numpy as jnp
from jax import lax
from jax.sharding import Mesh, PartitionSpec as P

adapter_scale = 2.0
norm_eps = 1e-05
GRP = ("zl", "x")
TP = ("zh", "c")
bf16, f32 = jnp.bfloat16, jnp.float32


def dot(a, b, ca, cb):
    return lax.dot_general(a, b, (((ca,), (cb,)), ((), ())), preferred_element_type=f32)


def exchange(blocks, axis):
    return lax.all_to_all(blocks, axis, split_axis=0, concat_axis=0, tiled=True)


def pick_entry(grid_in, position, which_axis):
    matches = lax.broadcasted_iota(jnp.int32, grid_in.shape, which_axis) == position
    return jnp.sum(jnp.where(matches, grid_in, 0), axis=which_axis)


def copies(x, n):
    return jnp.broadcast_to(x[None], (n, *x.shape))


def two_halves(v):
    hi = lax.reduce_precision(v, 8, 7)
    return hi.astype(bf16), (v - hi).astype(bf16)


def shards(
    frames,
    projector,
    text,
    gain_all,
    frozen,
    down,
    up,
    clip_len,
    first_token,
    segment,
    keep,
    cotangent,
):
    nx, ny, ng, nt = (lax.axis_size(a) for a in ("x", "y", GRP, TP))
    grp_index, tp_index = lax.axis_index(GRP), lax.axis_index(TP)
    x_index = lax.axis_index("x")
    toks, width = text.shape
    cols, rank = frozen.shape[1], down.shape[1]
    n_frames = frames.shape[0] // ng
    full_width = width * nt
    cap = 2 * n_frames // ng
    slots = ng * cap
    rows = toks + n_frames
    gain = lax.dynamic_slice_in_dim(gain_all, tp_index * width, width, 0)

    partial = dot(frames, projector, 1, 0).astype(bf16)

    own_sizes = pick_entry(clip_len[0], grp_index, 0)
    before = lax.broadcasted_iota(jnp.int32, (ng, ng), 1) < lax.broadcasted_iota(jnp.int32, (ng, ng), 0)
    own_starts = jnp.sum(jnp.where(before, own_sizes[None, :], 0), axis=1)
    slot_offset = lax.broadcasted_iota(jnp.int32, (ng, cap), 1)
    frame_slot = own_starts[:, None] + slot_offset
    slot_live = slot_offset < own_sizes[:, None]
    frame_iota = lax.broadcasted_iota(jnp.int32, (ng, cap, n_frames), 2)
    sender = (
        ((frame_iota == frame_slot[:, :, None]) & slot_live[:, :, None])
        .astype(bf16)
        .reshape(slots, n_frames)
    )
    in_sizes = pick_entry(clip_len[0], grp_index, 1)
    arrive_at = pick_entry(first_token[0], grp_index, 1)
    token_iota = lax.broadcasted_iota(jnp.int32, (toks, ng, cap), 0)
    receive_mask = (token_iota == (arrive_at[:, None] + slot_offset)[None]) & (
        slot_offset < in_sizes[:, None]
    )[None]
    receiver = receive_mask.astype(bf16).reshape(toks, slots)
    is_audio = jnp.any(receive_mask, axis=(1, 2))

    doc_iota = lax.broadcasted_iota(jnp.int32, (toks, keep.shape[0]), 1)
    kept = jnp.sum(jnp.where(segment[:, None] == doc_iota, keep[None, :], 0), axis=1)
    grad_tok = cotangent * kept.astype(bf16)[:, None]
    grad_slots = exchange(dot(receiver, grad_tok, 0, 0).astype(bf16).reshape(ng, cap, cols), GRP)
    grad_frames = dot(sender, grad_slots.reshape(slots, cols), 0, 0).astype(bf16)
    grad_text = jnp.where(is_audio[:, None], jnp.zeros_like(grad_tok), grad_tok)
    grad_rows = jnp.concatenate([grad_text, grad_frames], axis=0)

    piece = width // (ny * nx)
    w_piece = lax.dynamic_index_in_dim(frozen.reshape(2, ny, nx, piece, cols), x_index, 2, False)
    a_rows = piece // nt
    a_piece = lax.dynamic_index_in_dim(down.reshape(2, ny, nx, nt, a_rows, rank), x_index, 2, False)
    a_piece = lax.dynamic_index_in_dim(a_piece, tp_index, 2, False)
    a_piece = jnp.pad(a_piece, ((0, 0), (0, 0), (0, 0), (0, cols - rank)))
    wa = jnp.moveaxis(jnp.concatenate([w_piece, a_piece], axis=2), 0, 1)
    wa = exchange(wa.reshape(ny, 2 * (piece + a_rows), cols), "y")
    wa = wa.reshape(nt, piece + a_rows, cols)
    lanes = -(-rows // cols) * cols
    padded_grad = jnp.pad(grad_rows, ((0, lanes - rows), (0, 0)))
    lora_part = (adapter_scale * dot(up, padded_grad, 1, 1)).astype(bf16)
    n_l = lanes // cols
    lora_part = jnp.moveaxis(lora_part.reshape(rank, n_l, cols), 1, 0).reshape(n_l * rank, cols)
    sent = jnp.concatenate([wa, copies(jnp.concatenate([grad_frames, lora_part], axis=0), nt)], axis=1)
    came = exchange(sent, TP)
    at = piece + a_rows
    w_rows = jnp.moveaxis(came[:, :piece], 0, 1).reshape(piece, nt * cols)
    weights = jnp.concatenate([w_rows, came[:, piece:at].reshape(piece, cols)], axis=1)
    weights = lax.all_gather(weights, "x", axis=0, tiled=True)
    weights = lax.all_gather(weights, "y", axis=0, tiled=True)
    grad_full = jnp.moveaxis(came[:, at : at + n_frames], 0, 1).reshape(n_frames, nt * cols)
    lora = jnp.sum(came[:, at + n_frames :].astype(f32), axis=0).astype(bf16)
    lora_t = jnp.moveaxis(lora.reshape(n_l, rank, cols), 0, 1).reshape(rank, lanes)[:, :rows]

    blocks = exchange(partial.reshape(ng, n_frames, width), GRP)
    embedded = jnp.sum(blocks.astype(f32), axis=0).astype(bf16)
    inputs = jnp.concatenate([text, embedded], axis=0)
    wide = inputs.astype(f32)
    scaled = wide * gain[None, :]
    sq_part = jnp.sum(wide * wide, axis=1)

    lora_frames = jnp.pad(lora_t[:, toks:].T, ((0, 0), (0, cols - rank)))
    grad_norm = dot(jnp.concatenate([grad_full, lora_frames], axis=1), weights, 1, 1)
    dots_part = jnp.sum(scaled[toks:] * grad_norm, axis=1)
    product = dot(scaled.astype(bf16), weights, 1, 0)
    low_part = product[:, nt * cols : nt * cols + rank].astype(bf16)
    low_part = jnp.pad(low_part.T, ((0, 0), (0, lanes - rows)))
    low_part = jnp.moveaxis(low_part.reshape(rank, n_l, cols), 1, 0).reshape(n_l * rank, cols)
    sums = jnp.pad(jnp.concatenate([sq_part, dots_part]), (0, lanes - rows - n_frames))
    hi, lo = two_halves(sums.reshape(n_l, cols))
    stats = jnp.concatenate([low_part, hi, lo, jnp.zeros((8 - 2 * n_l, cols), bf16)], axis=0)
    stats = jnp.sum(exchange(copies(stats, nt), TP).astype(f32), axis=0)
    sums = (stats[n_l * rank : n_l * rank + n_l] + stats[n_l * rank + n_l : n_l * rank + 2 * n_l]).reshape(lanes)
    inv_rms = lax.rsqrt(sums[:rows] / full_width + norm_eps)
    low = jnp.moveaxis(stats[: n_l * rank].reshape(n_l, rank, cols), 0, 1).reshape(rank, lanes)[:, :rows]
    low_half_t = (low * inv_rms[None, :]).astype(bf16)

    base = jnp.moveaxis(product[:, : nt * cols].astype(bf16).reshape(rows, nt, cols), 1, 0)
    base = lax.psum_scatter(base.reshape(nt * rows, cols), TP, scatter_dimension=0, tiled=True)
    values = base.astype(f32) * inv_rms[:, None] + adapter_scale * dot(low_half_t, up, 0, 0)
    values = values.astype(bf16)

    normed = (scaled * inv_rms[:, None]).astype(bf16)
    down_t = dot(lora_t, normed, 1, 0)
    up_part = adapter_scale * dot(low_half_t, grad_rows, 1, 0)
    adapters = jnp.concatenate(
        [
            down_t.astype(bf16).reshape(ng, rank // ng, width),
            jnp.pad(up_part.astype(bf16), ((0, 0), (0, width - cols))).reshape(ng, rank // ng, width),
        ],
        axis=1,
    )

    inv_f = inv_rms[toks:, None]
    dots = inv_f * sums[rows : rows + n_frames, None]
    frame_grad = (inv_f * gain[None, :] * grad_norm - wide[toks:] * (inv_f * inv_f * dots / full_width)).astype(bf16)
    came = exchange(jnp.concatenate([copies(frame_grad, ng), adapters], axis=1), GRP)
    all_grad = came[:, :n_frames].reshape(ng * n_frames, width)
    adapters = jnp.sum(came[:, n_frames:].astype(f32), axis=0).astype(bf16)
    proj_part = dot(frames, all_grad, 0, 0).astype(bf16)
    third = frames.shape[1] // ny
    came = exchange(
        jnp.concatenate([proj_part.reshape(ny, third, width), copies(adapters, ny)], axis=1), "y"
    )
    came = jnp.sum(came.astype(f32), axis=0)
    projector_grad = lax.all_gather(came[:third].astype(bf16), "y", axis=0, tiled=True).astype(f32)

    k = rank // ng
    own = jnp.concatenate([came[third : third + k].reshape(k * width // cols, cols), came[third + k :, :cols]], axis=0)
    out_slots = dot(sender, values[toks:], 1, 0).reshape(ng, cap, cols)
    last = exchange(jnp.concatenate([copies(own, ng), out_slots], axis=1), GRP)
    n_d = k * width // cols
    down_grad = last[:, :n_d].reshape(rank, width).T
    up_grad = last[:, n_d : n_d + k].reshape(rank, cols)
    in_slots = last[:, n_d + k :].astype(bf16).reshape(slots, cols)
    audio_values = dot(receiver, in_slots, 1, 0).astype(bf16)
    value_output = jnp.where(is_audio[:, None], audio_values, values[:toks])
    return value_output, projector_grad, down_grad, up_grad


def solution(mesh):
    sizes = dict(zip(mesh.axis_names, mesh.devices.shape))
    half = sizes["grp"] // 4
    mesh = Mesh(
        mesh.devices.reshape(half, 4, sizes["fsdp"], sizes["tp"] // 2, 2),
        ("zl", "x", "y", "zh", "c"),
    )
    rows = ("zl", "x", "y")
    in_specs = (
        P("y", GRP),
        P(GRP, TP),
        P(rows, TP),
        P(),
        P("y", TP),
        P("y", None),
        P(None, TP),
        P("y", None, None),
        P("y", None, None),
        P(rows),
        P(),
        P(rows, TP),
    )
    out_specs = (P(rows, TP), P(GRP, TP), P(TP, None), P(None, TP))
    return jax.shard_map(shards, mesh=mesh, in_specs=in_specs, out_specs=out_specs, check_vma=False)
```

time: 397 us -> 308 us (0.78)
  the two profiles are of different devices: /device:TPU:8 before, /device:TPU:2 now
where the time goes in v1:
time: 308 us; the launch traced here: 307 us
  waiting for transfers between devices  149 us (48%)
  starting transfers between devices  70.4 us (23%)
  blocking collectives  34.5 us (11%)
  between operations  14.8 us (5%)
  local copies, waits for them, and re-layouts  14 us (5%)
  matrix products  12.5 us (4%)
  other arithmetic  12 us (4%)
    all_to_all x8, waiting for transfers between devices, exchange(): return lax.all_to_all(blocks, axis, split_axis=0, concat_axis=0, tiled=True)  125 us
    all_to_all x8, starting transfers between devices, exchange(): return lax.all_to_all(blocks, axis, split_axis=0, concat_axis=0, tiled=True)  70.4 us
    all_gather x1, waiting for transfers between devices, shards(): weights = lax.all_gather(weights, 'y', axis=0, tiled=True)  23.8 us
    all_gather x1, blocking collectives, shards(): weights = lax.all_gather(weights, 'x', axis=0, tiled=True)  21.5 us
    all_gather x1, blocking collectives, shards(): lax.all_gather(came[:third].astype(bf16), 'y', axis=0, tiled=True)  13 us
    dot_general x12, matrix products, dot(): lax.dot_general(a, b, (((ca,), (cb,)), ((), ())), preferred_element_type=...  12.5 us
  transfers between devices with their start and end apart: 10, of which 8 were waited for; matrix products, arithmetic and copies ran while one was open for 6% of the time, Pallas kernels for 0%

profile of v1, /device:TPU:2, one launch (start us, length us, event | category | flops | bytes accessed | tf_op | source)
XLA Modules:
  0.0 307.2 jit_solution(1258214904756837706)
XLA Ops:
  11.3 9.2 %all-to-all-start.2 = ((bf16[16,6,128]{2,1,0:T(8,128)(2,1)}), bf16[16,6,128]{2,1,0:T(8,128)(2,1)S(1)}, u32[]{:S(2)}, u32[]{:S(2)}) async-start(bf16[16,6,128]{2,1,0:T(8,128)(2,1)} %reshape.220), calls=%async_computation.2 | async-start | bytes 65536 | tf_op jit(solution)/shard_map/all_to_all | solution.py:18
  24.7 2.6 all-to-all-done.2
  27.3 4.1 %all-to-all-start.1 = ((bf16[4,144,128]{2,1,0:T(8,128)(2,1)}), bf16[4,144,128]{2,1,0:T(8,128)(2,1)S(1)}, u32[]{:S(2)}, u32[]{:S(2)}) async-start(bf16[4,144,128]{2,1,0:T(8,128)(2,1)} %bitcast.8), calls=%async_computation.1 | async-start | bytes 294912 | tf_op jit(solution)/shard_map/all_to_all | solution.py:18
  31.9 5.5 %all-to-all-done.1 = bf16[4,144,128]{2,1,0:T(8,128)(2,1)S(1)} async-done(((bf16[4,144,128]{2,1,0:T(8,128)(2,1)}), bf16[4,144,128]{2,1,0:T(8,128)(2,1)S(1)}, u32[]{:S(2)}, u32[]{:S(2)}) %all-to-all-start.1) | async-done | bytes 147488 | tf_op jit(solution)/shard_map/all_to_all | solution.py:18
  38.5 12.4 %all-to-all-start.3 = ((bf16[8,312,128]{2,1,0:T(8,128)(2,1)}), bf16[8,312,128]{2,1,0:T(8,128)(2,1)S(1)}, u32[]{:S(2)}, u32[]{:S(2)}) async-start(bf16[8,312,128]{2,1,0:T(8,128)(2,1)} %pad_maximum_fusion.2), calls=%async_computation.3 | async-start | bytes 1277952 | tf_op jit(solution)/shard_map/all_to_all | solution.py:18
  50.9 2.2 convolution_convert_fusion.1
  53.0 34.7 %all-to-all-done.3 = bf16[8,312,128]{2,1,0:T(8,128)(2,1)S(1)} async-done(((bf16[8,312,128]{2,1,0:T(8,128)(2,1)}), bf16[8,312,128]{2,1,0:T(8,128)(2,1)S(1)}, u32[]{:S(2)}, u32[]{:S(2)}) %all-to-all-start.3) | async-done | bytes 639008 | tf_op jit(solution)/shard_map/all_to_all | solution.py:18
  87.7 6.5 %all-to-all-start = ((bf16[16,48,1024]{2,1,0:T(8,128)(2,1)}), bf16[16,48,1024]{2,1,0:T(8,128)(2,1)S(1)}, u32[]{:S(2)}, u32[]{:S(2)}) async-start(bf16[16,48,1024]{2,1,0:T(8,128)(2,1)} %bitcast.108), calls=%async_computation | async-start | bytes 3145728 | tf_op jit(solution)/shard_map/all_to_all | solution.py:18
  94.3 21.5 %all_gather.9 = bf16[256,1152]{1,0:T(8,128)(2,1)} all-gather(bf16[64,1152]{1,0:T(8,128)(2,1)S(1)} %pad_maximum_fusion.4), channel_id=1, replica_groups=mesh['zl'=4,'x'=4,'y'=4,'zh'=4,'c'=2] {'x'}, dimensions={0}, use_global_device_ids=true | all-gather | bytes 737280 | tf_op jit(solution)/shard_map/all_gather | solution.py:111
  119.3 4.3 %all-to-all-done = bf16[16,48,1024]{2,1,0:T(8,128)(2,1)S(1)} async-done(((bf16[16,48,1024]{2,1,0:T(8,128)(2,1)}), bf16[16,48,1024]{2,1,0:T(8,128)(2,1)S(1)}, u32[]{:S(2)}, u32[]{:S(2)}) %all-to-all-start) | async-done | bytes 1572896 | tf_op jit(solution)/shard_map/all_to_all | solution.py:18
  123.9 1.8 multiply_reduce_fusion
  125.7 23.8 %all-gather.2.cloned.1.call-done = bf16[1024,1152]{1,0:T(8,128)(2,1)} async-done(((bf16[256,1152]{1,0:T(8,128)(2,1)}), bf16[1024,1152]{1,0:T(8,128)(2,1)}) %all-gather.2.cloned.1.call-update) | async-done | bytes 2359312 | tf_op jit(solution)/shard_map/all_gather | solution.py:112
  149.5 2.8 convolution_convert_fusion
  153.9 1.6 copy.63
  155.5 2.6 fusion.14
  159.1 12.2 %all-to-all-start.4 = ((bf16[8,200,128]{2,1,0:T(8,128)(2,1)}), bf16[8,200,128]{2,1,0:T(8,128)(2,1)S(1)}, u32[]{:S(2)}, u32[]{:S(2)}) async-start(bf16[8,200,128]{2,1,0:T(8,128)(2,1)} %broadcast_in_dim.61), calls=%async_computation.4 | async-start | bytes 819200 | tf_op jit(solution)/shard_map/all_to_all | solution.py:18
  171.5 27.0 %all-to-all-done.4 = bf16[8,200,128]{2,1,0:T(8,128)(2,1)S(1)} async-done(((bf16[8,200,128]{2,1,0:T(8,128)(2,1)}), bf16[8,200,128]{2,1,0:T(8,128)(2,1)S(1)}, u32[]{:S(2)}, u32[]{:S(2)}) %all-to-all-start.4) | async-done | bytes 409632 | tf_op jit(solution)/shard_map/all_to_all | solution.py:18
  199.9 1.6 pad_maximum_fusion
  201.4 7.3 %all-to-all-start.5 = ((bf16[16,56,1024]{2,1,0:T(8,128)(2,1)}), bf16[16,56,1024]{2,1,0:T(8,128)(2,1)S(1)}, u32[]{:S(2)}, u32[]{:S(2)}) async-start(bf16[16,56,1024]{2,1,0:T(8,128)(2,1)} %pad_maximum_fusion), calls=%async_computation.5 | async-start | bytes 3670016 | tf_op jit(solution)/shard_map/all_to_all | solution.py:18
  210.0 43.2 %all-to-all-done.5 = bf16[16,56,1024]{2,1,0:T(8,128)(2,1)S(1)} async-done(((bf16[16,56,1024]{2,1,0:T(8,128)(2,1)}), bf16[16,56,1024]{2,1,0:T(8,128)(2,1)S(1)}, u32[]{:S(2)}, u32[]{:S(2)}) %all-to-all-start.5) | async-done | bytes 1835040 | tf_op jit(solution)/shard_map/all_to_all | solution.py:18
  255.0 3.5 %all-to-all-start.6 = ((bf16[4,88,1024]{2,1,0:T(8,128)(2,1)}), bf16[4,88,1024]{2,1,0:T(8,128)(2,1)S(1)}, u32[]{:S(2)}, u32[]{:S(2)}) async-start(bf16[4,88,1024]{2,1,0:T(8,128)(2,1)} %pad_maximum_fusion.1), calls=%async_computation.6 | async-start | bytes 1441792 | tf_op jit(solution)/shard_map/all_to_all | solution.py:18
  259.9 7.7 %all-to-all-done.6 = bf16[4,88,1024]{2,1,0:T(8,128)(2,1)S(1)} async-done(((bf16[4,88,1024]{2,1,0:T(8,128)(2,1)}), bf16[4,88,1024]{2,1,0:T(8,128)(2,1)S(1)}, u32[]{:S(2)}, u32[]{:S(2)}) %all-to-all-start.6) | async-done | bytes 720928 | tf_op jit(solution)/shard_map/all_to_all | solution.py:18
  268.6 15.1 %all-to-all-start.7 = ((f32[16,42,128]{2,1,0:T(8,128)}), f32[16,42,128]{2,1,0:T(8,128)S(1)}, u32[]{:S(2)}, u32[]{:S(2)}) async-start(f32[16,42,128]{2,1,0:T(8,128)} %pad_maximum_fusion.3), calls=%async_computation.8 | async-start | bytes 786432 | tf_op jit(solution)/shard_map/all_to_all | solution.py:18
  283.8 13.0 %all_gather.11 = bf16[320,1024]{1,0:T(8,128)(2,1)S(1)} all-gather(bf16[80,1024]{1,0:T(8,128)(2,1)S(1)} %slice.171), channel_id=1, replica_groups=mesh['zl'=4,'x'=4,'y'=4,'zh'=4,'c'=2] {'y'}, dimensions={0}, use_global_device_ids=true | all-gather | bytes 819200 | tf_op jit(solution)/shard_map/all_gather | solution.py:168
  (157 shorter events, 26.1 us)
Async XLA Ops:
  7.2 43.7 %copy-start = (bf16[320,1024]{1,0:T(8,128)(2,1)S(1)}, bf16[320,1024]{1,0:T(8,128)(2,1)}, u32[]{:S(2)}) copy-start(bf16[320,1024]{1,0:T(8,128)(2,1)} %param.13) | copy-start | bytes 1966084
  7.2 24.5 %copy-start.13 = (bf16[64,128]{1,0:T(8,128)(2,1)S(1)}, bf16[64,128]{1,0:T(8,128)(2,1)}, u32[]{:S(2)}) copy-start(bf16[64,128]{1,0:T(8,128)(2,1)} %param.18) | copy-start | bytes 49156
  11.3 16.1 %all-to-all-start.2 = ((bf16[16,6,128]{2,1,0:T(8,128)(2,1)}), bf16[16,6,128]{2,1,0:T(8,128)(2,1)S(1)}, u32[]{:S(2)}, u32[]{:S(2)}) async-start(bf16[16,6,128]{2,1,0:T(8,128)(2,1)} %reshape.220), calls=%async_computation.2 | async-start | bytes 65536 | tf_op jit(solution)/shard_map/all_to_all | solution.py:18
  20.6 17.0 %copy-start.30 = (pred[16,6]{0,1:T(8,128)(4,1)}, pred[16,6]{0,1:T(8,128)(4,1)S(1)}, u32[]{:S(2)}) copy-start(pred[16,6]{0,1:T(8,128)(4,1)S(1)} %iota_compare_fusion.7) | copy-start | bytes 292
  20.6 16.9 %copy-start.21 = (s32[16,6]{0,1:T(8,128)}, s32[16,6]{0,1:T(8,128)S(1)}, u32[]{:S(2)}) copy-start(s32[16,6]{0,1:T(8,128)S(1)} %iota_add_fusion) | copy-start | bytes 1156
  21.7 15.8 %copy-start.8 = (bf16[256,128]{1,0:T(8,128)(2,1)}, bf16[256,128]{1,0:T(8,128)(2,1)S(1)}, u32[]{:S(2)}) copy-start(bf16[256,128]{1,0:T(8,128)(2,1)S(1)} %broadcast_select_fusion) | copy-start | bytes 196612
  27.3 10.2 %all-to-all-start.1 = ((bf16[4,144,128]{2,1,0:T(8,128)(2,1)}), bf16[4,144,128]{2,1,0:T(8,128)(2,1)S(1)}, u32[]{:S(2)}, u32[]{:S(2)}) async-start(bf16[4,144,128]{2,1,0:T(8,128)(2,1)} %bitcast.8), calls=%async_computation.1 | async-start | bytes 294912 | tf_op jit(solution)/shard_map/all_to_all | solution.py:18
  37.6 13.3 %copy-start.28 = (bf16[768,320]{0,1:T(8,128)(2,1)S(1)}, bf16[768,320]{0,1:T(8,128)(2,1)}, u32[]{:S(2)}) copy-start(bf16[768,320]{0,1:T(8,128)(2,1)} %param.12) | copy-start | bytes 1474564
  38.5 49.3 %all-to-all-start.3 = ((bf16[8,312,128]{2,1,0:T(8,128)(2,1)}), bf16[8,312,128]{2,1,0:T(8,128)(2,1)S(1)}, u32[]{:S(2)}, u32[]{:S(2)}) async-start(bf16[8,312,128]{2,1,0:T(8,128)(2,1)} %pad_maximum_fusion.2), calls=%async_computation.3 | async-start | bytes 1277952 | tf_op jit(solution)/shard_map/all_to_all | solution.py:18
  87.7 35.9 %all-to-all-start = ((bf16[16,48,1024]{2,1,0:T(8,128)(2,1)}), bf16[16,48,1024]{2,1,0:T(8,128)(2,1)S(1)}, u32[]{:S(2)}, u32[]{:S(2)}) async-start(bf16[16,48,1024]{2,1,0:T(8,128)(2,1)} %bitcast.108), calls=%async_computation | async-start | bytes 3145728 | tf_op jit(solution)/shard_map/all_to_all | solution.py:18
  94.2 55.3 %all-gather.2.cloned.1.call-start = ((), (), s32[]{:S(2)}) async-start(), calls=%async_computation.9 | async-start | bytes 2949120 | tf_op jit(solution)/shard_map/all_gather | solution.py:112
  115.8 8.1 %copy-start.2 = (bf16[256,1024]{1,0:T(8,128)(2,1)S(1)}, bf16[256,1024]{1,0:T(8,128)(2,1)}, u32[]{:S(2)}) copy-start(bf16[256,1024]{1,0:T(8,128)(2,1)} %param.14) | copy-start | bytes 1572868
  118.0 7.7 %copy-start.11 = (bf16[64,3,128]{0,2,1:T(8,128)(2,1)}, bf16[64,3,128]{0,2,1:T(8,128)(2,1)S(1)}, u32[]{:S(2)}) copy-start(bf16[64,3,128]{0,2,1:T(8,128)(2,1)S(1)} %copy.65) | copy-start | bytes 147460
  158.1 13.2 %copy-start.4 = (bf16[48,1024]{1,0:T(8,128)(2,1)S(1)}, bf16[48,1024]{1,0:T(8,128)(2,1)}, u32[]{:S(2)}) copy-start(bf16[48,1024]{1,0:T(8,128)(2,1)} %copy-done.3) | copy-start | bytes 294916
  159.1 39.4 %all-to-all-start.4 = ((bf16[8,200,128]{2,1,0:T(8,128)(2,1)}), bf16[8,200,128]{2,1,0:T(8,128)(2,1)S(1)}, u32[]{:S(2)}, u32[]{:S(2)}) async-start(bf16[8,200,128]{2,1,0:T(8,128)(2,1)} %broadcast_in_dim.61), calls=%async_computation.4 | async-start | bytes 819200 | tf_op jit(solution)/shard_map/all_to_all | solution.py:18
  171.3 27.3 %copy-start.12 = (bf16[64,3,128]{0,2,1:T(8,128)(2,1)S(1)}, bf16[64,3,128]{0,2,1:T(8,128)(2,1)}, u32[]{:S(2)}) copy-start(bf16[64,3,128]{0,2,1:T(8,128)(2,1)} %copy-done.11) | copy-start | bytes 147460
  171.3 27.3 %copy-start.17 = (f32[1024]{0:T(1024)S(1)}, f32[1024]{0:T(1024)}, u32[]{:S(2)}) copy-start(f32[1024]{0:T(1024)} %dynamic_slice.13) | copy-start | bytes 12292
  171.5 27.6 %copy-start.9 = (bf16[256,128]{1,0:T(8,128)(2,1)S(1)}, bf16[256,128]{1,0:T(8,128)(2,1)}, u32[]{:S(2)}) copy-start(bf16[256,128]{1,0:T(8,128)(2,1)} %copy-done.8) | copy-start | bytes 196612
  171.5 27.6 %copy-start.15 = (bf16[48,128]{1,0:T(8,128)(2,1)S(1)}, bf16[48,128]{1,0:T(8,128)(2,1)}, u32[]{:S(2)}) copy-start(bf16[48,128]{1,0:T(8,128)(2,1)} %copy-done.14) | copy-start | bytes 36868
  201.4 51.7 %all-to-all-start.5 = ((bf16[16,56,1024]{2,1,0:T(8,128)(2,1)}), bf16[16,56,1024]{2,1,0:T(8,128)(2,1)S(1)}, u32[]{:S(2)}, u32[]{:S(2)}) async-start(bf16[16,56,1024]{2,1,0:T(8,128)(2,1)} %pad_maximum_fusion), calls=%async_computation.5 | async-start | bytes 3670016 | tf_op jit(solution)/shard_map/all_to_all | solution.py:18
  208.8 49.7 %reduce-scatter.2.cloned.1.call-start = ((), (), s32[]{:S(2)}) async-start(), calls=%async_computation.10 | async-start | bytes 700416 | tf_op jit(solution)/shard_map/reduce_scatter | solution.py:141
  210.0 43.4 %copy-start.29 = (bf16[768,320]{0,1:T(8,128)(2,1)S(1)}, bf16[768,320]{0,1:T(8,128)(2,1)}, u32[]{:S(2)}) copy-start(bf16[768,320]{0,1:T(8,128)(2,1)} %param.12) | copy-start | bytes 1474564
  255.0 12.6 %all-to-all-start.6 = ((bf16[4,88,1024]{2,1,0:T(8,128)(2,1)}), bf16[4,88,1024]{2,1,0:T(8,128)(2,1)S(1)}, u32[]{:S(2)}, u32[]{:S(2)}) async-start(bf16[4,88,1024]{2,1,0:T(8,128)(2,1)} %pad_maximum_fusion.1), calls=%async_computation.6 | async-start | bytes 1441792 | tf_op jit(solution)/shard_map/all_to_all | solution.py:18
  268.6 29.4 %all-to-all-start.7 = ((f32[16,42,128]{2,1,0:T(8,128)}), f32[16,42,128]{2,1,0:T(8,128)S(1)}, u32[]{:S(2)}, u32[]{:S(2)}) async-start(f32[16,42,128]{2,1,0:T(8,128)} %pad_maximum_fusion.3), calls=%async_computation.8 | async-start | bytes 786432 | tf_op jit(solution)/shard_map/all_to_all | solution.py:18
  (18 other events, 61.1 us)
Sparse Core Ops, SparseCore 0:
  116.0 33.5 all-gather.1
  212.4 45.1 reduce-scatter.1

commit v2 on v1

v2 whole, which is shorter than its diff:
```python
import jax
import jax.numpy as jnp
from jax import lax
from jax.sharding import Mesh, PartitionSpec as P

adapter_scale = 2.0
norm_eps = 1e-05
GRP = ("zl", "x")
TP = ("zh", "c")
bf16, f32 = jnp.bfloat16, jnp.float32


def dot(a, b, ca, cb):
    return lax.dot_general(a, b, (((ca,), (cb,)), ((), ())), preferred_element_type=f32)


def exchange(blocks, axis):
    return lax.all_to_all(blocks, axis, split_axis=0, concat_axis=0, tiled=True)


def pick_entry(grid_in, position, which_axis):
    matches = lax.broadcasted_iota(jnp.int32, grid_in.shape, which_axis) == position
    return jnp.sum(jnp.where(matches, grid_in, 0), axis=which_axis)


def copies(x, n):
    return jnp.broadcast_to(x[None], (n, *x.shape))


def two_halves(v):
    hi = lax.reduce_precision(v, 8, 7)
    return hi.astype(bf16), (v - hi).astype(bf16)


def from_peers(x, axis):
    n = lax.axis_size(axis)
    return [x] + [lax.ppermute(x, axis, [(i, (i + k) % n) for i in range(n)]) for k in range(1, n)]


def placed(blocks, dim, axis):
    n, me, size = len(blocks), lax.axis_index(axis), blocks[0].shape[dim]
    shape = list(blocks[0].shape)
    shape[dim] *= n
    out = jnp.zeros(shape, blocks[0].dtype)
    for k, block in enumerate(blocks):
        out = lax.dynamic_update_slice_in_dim(out, block, lax.rem(me - k + n, n) * size, dim)
    return out


def shards(
    frames,
    projector,
    text,
    gain_all,
    frozen,
    down,
    up,
    clip_len,
    first_token,
    segment,
    keep,
    cotangent,
):
    nx, ny, nzl, ng, nt = (lax.axis_size(a) for a in ("x", "y", "zl", GRP, TP))
    grp_index, tp_index = lax.axis_index(GRP), lax.axis_index(TP)
    x_index, y_index = lax.axis_index("x"), lax.axis_index("y")
    toks, width = text.shape
    cols, rank = frozen.shape[1], down.shape[1]
    n_frames = frames.shape[0] // ng
    full_width = width * nt
    cap = 2 * n_frames // ng
    slots = ng * cap
    rows = toks + n_frames
    gain = lax.dynamic_slice_in_dim(gain_all, tp_index * width, width, 0)

    by_x = frames.reshape(nzl, nx, n_frames, frames.shape[1])

    def block_for(k):
        part = lax.dynamic_index_in_dim(by_x, lax.rem(x_index + k, nx), 1, False)
        part = part.reshape(nzl * n_frames, frames.shape[1])
        return dot(part, projector, 1, 0).astype(bf16)

    x_parts = [
        lax.ppermute(block_for(k), "x", [(i, (i + k) % nx) for i in range(nx)]) for k in range(1, nx)
    ]
    x_sum = block_for(0).astype(f32)
    for part in x_parts:
        x_sum = x_sum + part.astype(f32)

    own_sizes = pick_entry(clip_len[0], grp_index, 0)
    before = lax.broadcasted_iota(jnp.int32, (ng, ng), 1) < lax.broadcasted_iota(jnp.int32, (ng, ng), 0)
    own_starts = jnp.sum(jnp.where(before, own_sizes[None, :], 0), axis=1)
    slot_offset = lax.broadcasted_iota(jnp.int32, (ng, cap), 1)
    frame_slot = own_starts[:, None] + slot_offset
    slot_live = slot_offset < own_sizes[:, None]
    frame_iota = lax.broadcasted_iota(jnp.int32, (ng, cap, n_frames), 2)
    sender = (
        ((frame_iota == frame_slot[:, :, None]) & slot_live[:, :, None])
        .astype(bf16)
        .reshape(slots, n_frames)
    )
    in_sizes = pick_entry(clip_len[0], grp_index, 1)
    arrive_at = pick_entry(first_token[0], grp_index, 1)
    token_iota = lax.broadcasted_iota(jnp.int32, (toks, ng, cap), 0)
    receive_mask = (token_iota == (arrive_at[:, None] + slot_offset)[None]) & (
        slot_offset < in_sizes[:, None]
    )[None]
    receiver = receive_mask.astype(bf16).reshape(toks, slots)
    is_audio = jnp.any(receive_mask, axis=(1, 2))

    doc_iota = lax.broadcasted_iota(jnp.int32, (toks, keep.shape[0]), 1)
    kept = jnp.sum(jnp.where(segment[:, None] == doc_iota, keep[None, :], 0), axis=1)
    grad_tok = cotangent * kept.astype(bf16)[:, None]
    grad_slots = exchange(dot(receiver, grad_tok, 0, 0).astype(bf16).reshape(ng, cap, cols), GRP)
    grad_frames = dot(sender, grad_slots.reshape(slots, cols), 0, 0).astype(bf16)
    grad_text = jnp.where(is_audio[:, None], jnp.zeros_like(grad_tok), grad_tok)
    grad_rows = jnp.concatenate([grad_text, grad_frames], axis=0)

    piece = width // (ny * nx)
    w_piece = lax.dynamic_index_in_dim(frozen.reshape(2, ny, nx, piece, cols), x_index, 2, False)
    down_half = lax.dynamic_slice_in_dim(down.T, lax.rem(tp_index, 2) * width, width, 1)
    down_half = jnp.moveaxis(down_half.reshape(rank, nt, cols), 1, 0).reshape(nt * rank, cols)

    def for_y(k):
        w = lax.dynamic_index_in_dim(w_piece, lax.rem(y_index + k, ny), 1, False)
        return jnp.concatenate([w.reshape(2 * piece, cols), down_half], axis=0)

    y_parts = [for_y(0)] + [
        lax.ppermute(for_y(k), "y", [(i, (i + k) % ny) for i in range(ny)]) for k in range(1, ny)
    ]
    y_parts = jnp.stack([lax.select_n(lax.rem(y_index - j + ny, ny), *y_parts) for j in range(ny)])
    wa = y_parts[:, : 2 * piece].reshape(nt, piece, cols)
    down_t = lax.dynamic_index_in_dim(y_parts[:, 2 * piece :], tp_index // 2, 0, False)
    down_t = jnp.moveaxis(down_t.reshape(nt, rank, cols), 0, 1).reshape(rank, width)
    up_rows = rank // nx
    up_piece = lax.dynamic_slice_in_dim(up, x_index * up_rows, up_rows, 0)
    sent = jnp.concatenate(
        [wa, copies(jnp.concatenate([up_piece, grad_frames], axis=0), nt)], axis=1
    )
    came = exchange(sent, TP)
    at = piece + up_rows
    weights = jnp.moveaxis(came[:, :at], 0, 1).reshape(at, nt * cols)
    weights = lax.all_gather(weights, "x")
    up_full = weights[:, piece:].reshape(rank, nt * cols)
    weights = from_peers(weights[:, :piece].reshape(nx * piece, nt * cols), "y")
    grad_full = jnp.moveaxis(came[:, at:], 0, 1).reshape(n_frames, nt * cols)
    lora_frames = (adapter_scale * dot(grad_full, up_full, 1, 1)).astype(bf16)

    text_wide = text.astype(f32)
    text_scaled = text_wide * gain[None, :]
    pair = jnp.concatenate(
        [
            (adapter_scale * dot(grad_text, up, 1, 1)).astype(bf16),
            dot(text_scaled.astype(bf16), down_t, 1, 1).astype(bf16),
        ],
        axis=1,
    )
    pair = lax.psum_scatter(pair, TP, scatter_dimension=0, tiled=True)
    sq_text = dot(jnp.ones((8, width), bf16), (text_wide * text_wide).astype(bf16), 1, 1)[0]

    blocks = exchange(x_sum.astype(bf16).reshape(nzl, n_frames, width), "zl")
    embedded = jnp.sum(blocks.astype(f32), axis=0).astype(bf16)
    wide = embedded.astype(f32)
    scaled = wide * gain[None, :]

    grad_norm = placed([dot(grad_full, w, 1, 1) for w in weights], 1, "y")
    grad_norm = grad_norm + dot(lora_frames, down_t, 1, 0)
    sq_hi, sq_lo = two_halves(jnp.sum(wide * wide, axis=1, keepdims=True))
    d_hi, d_lo = two_halves(jnp.sum(scaled * grad_norm, axis=1, keepdims=True))
    low_frames = dot(scaled.astype(bf16), down_t, 1, 1).astype(bf16)
    spare = jnp.zeros((n_frames, cols - rank - 4), bf16)
    of_frames = jnp.concatenate([low_frames, sq_hi, sq_lo, d_hi, d_lo, spare], axis=1)
    n_l = toks // cols
    t_hi, t_lo = two_halves(sq_text.reshape(n_l, cols))
    spare = jnp.zeros((8 - 2 * n_l, cols), bf16)
    stats = jnp.concatenate([of_frames, t_hi, t_lo, spare, pair], axis=0)
    stats = exchange(copies(stats, nt), TP)
    pair = stats[:, n_frames + 8 :].reshape(toks, cols)
    stats = jnp.sum(stats[:, : n_frames + 8].astype(f32), axis=0)
    sq_frames = stats[:n_frames, rank : rank + 1] + stats[:n_frames, rank + 1 : rank + 2]
    dots = stats[:n_frames, rank + 2 : rank + 3] + stats[:n_frames, rank + 3 : rank + 4]
    sq_text = (stats[n_frames : n_frames + n_l] + stats[n_frames + n_l : n_frames + 2 * n_l]).reshape(toks, 1)
    inv_text = lax.rsqrt(sq_text / full_width + norm_eps)
    inv_f = lax.rsqrt(sq_frames / full_width + norm_eps)
    inv_rms = jnp.concatenate([inv_text, inv_f], axis=0)
    lora = jnp.concatenate([pair[:, :rank], lora_frames], axis=0)
    low = jnp.concatenate([pair[:, rank:].astype(f32), stats[:n_frames, :rank]], axis=0)
    low_half = (low * inv_rms).astype(bf16)

    all_scaled = jnp.concatenate([text_scaled, scaled], axis=0)
    quarter = width // ny
    base = jnp.zeros((rows, nt * cols), f32)
    for j, w in enumerate(weights):
        at = lax.rem(y_index - j + ny, ny) * quarter
        base = base + dot(lax.dynamic_slice_in_dim(all_scaled, at, quarter, 1).astype(bf16), w, 1, 0)
    base = base.astype(bf16)
    base = jnp.moveaxis(base.reshape(rows, nt, cols), 1, 0)
    base = lax.psum_scatter(base.reshape(nt * rows, cols), TP, scatter_dimension=0, tiled=True)
    values = base.astype(f32) * inv_rms + adapter_scale * dot(low_half, up, 1, 0)
    values = values.astype(bf16)

    normed = (all_scaled * inv_rms).astype(bf16)
    k = rank // ng
    down_part = dot(lora, normed, 0, 0).astype(bf16).reshape(nzl, nx, k, width)
    up_part = (adapter_scale * dot(low_half, grad_rows, 0, 0)).astype(bf16)
    up_part = jnp.pad(up_part, ((0, 0), (0, width - cols))).reshape(nzl, nx, k, width)
    adapters = jnp.concatenate([down_part, up_part], axis=2).reshape(nzl, nx * 2 * k, width)

    frame_grad = (
        inv_f * gain[None, :] * grad_norm - wide * (inv_f * inv_f * inv_f * dots / full_width)
    ).astype(bf16)
    came = exchange(jnp.concatenate([copies(frame_grad, nzl), adapters], axis=1), "zl")
    adapters = jnp.sum(came[:, n_frames:].astype(f32), axis=0).astype(bf16).reshape(nx, 2 * k, width)
    frame_grad = came[:, :n_frames].reshape(nzl * n_frames, width)
    came = exchange(jnp.concatenate([copies(frame_grad, nx), adapters], axis=1), "x")
    adapters = jnp.sum(came[:, nzl * n_frames :].astype(f32), axis=0).astype(bf16)
    all_grad = came[:, : nzl * n_frames].reshape(nx, nzl, n_frames, width)
    all_grad = jnp.moveaxis(all_grad, 0, 1).reshape(ng * n_frames, width)
    proj_part = dot(frames, all_grad, 0, 0).astype(bf16)
    part = frames.shape[1] // ny
    came = exchange(
        jnp.concatenate([proj_part.reshape(ny, part, width), copies(adapters, ny)], axis=1), "y"
    )
    came = jnp.sum(came.astype(f32), axis=0)
    projector_grad = placed([b.astype(f32) for b in from_peers(came[:part].astype(bf16), "y")], 0, "y")

    n_d = k * width // cols
    own = jnp.concatenate([came[part : part + k].reshape(n_d, cols), came[part + k :, :cols]], axis=0)
    out_slots = dot(sender, values[toks:], 1, 0).reshape(ng, cap, cols)
    last = exchange(jnp.concatenate([copies(own, ng), out_slots], axis=1), GRP)
    down_grad = last[:, :n_d].reshape(rank, width).T
    up_grad = last[:, n_d : n_d + k].reshape(rank, cols)
    in_slots = last[:, n_d + k :].astype(bf16).reshape(slots, cols)
    audio_values = dot(receiver, in_slots, 1, 0).astype(bf16)
    value_output = jnp.where(is_audio[:, None], audio_values, values[:toks])
    return value_output, projector_grad, down_grad, up_grad


def solution(mesh):
    sizes = dict(zip(mesh.axis_names, mesh.devices.shape))
    half = sizes["grp"] // 4
    mesh = Mesh(
        mesh.devices.reshape(half, 4, sizes["fsdp"], sizes["tp"] // 2, 2),
        ("zl", "x", "y", "zh", "c"),
    )
    rows = ("zl", "x", "y")
    in_specs = (
        P("y", GRP),
        P(GRP, TP),
        P(rows, TP),
        P(),
        P("y", TP),
        P("y", None),
        P(None, TP),
        P("y", None, None),
        P("y", None, None),
        P(rows),
        P(),
        P(rows, TP),
    )
    out_specs = (P(rows, TP), P(GRP, TP), P(TP, None), P(None, TP))
    return jax.shard_map(shards, mesh=mesh, in_specs=in_specs, out_specs=out_specs, check_vma=False)
```

time: 308 us -> 280 us (0.909)
  the two profiles are of different devices: /device:TPU:2 before, /device:TPU:11 now
where the time goes in v2:
time: 280 us; the launch traced here: 279 us
  starting transfers between devices  103 us (37%)
  waiting for transfers between devices  103 us (37%)
  matrix products  23.9 us (9%)
  between operations  15.3 us (5%)
  local copies, waits for them, and re-layouts  12.6 us (4%)
  other arithmetic  10.4 us (4%)
  blocking collectives  10.4 us (4%)
    all_to_all x8, starting transfers between devices, exchange(): return lax.all_to_all(blocks, axis, split_axis=0, concat_axis=0, tiled=True)  64.5 us
    all_to_all x8, waiting for transfers between devices, exchange(): return lax.all_to_all(blocks, axis, split_axis=0, concat_axis=0, tiled=True)  55.8 us
    reduce_scatter x1, waiting for transfers between devices, shards(): lax.psum_scatter(base.reshape(nt * rows, cols), TP, scatter_dimension=0,...  24 us
    dot_general x26, matrix products, dot(): lax.dot_general(a, b, (((ca,), (cb,)), ((), ())), preferred_element_type=...  23.9 us
    ppermute x6, starting transfers between devices, from_peers(): lax.ppermute(x, axis, [(i, (i + k) % n) for i in range(n)])  19.6 us
    ppermute x6, waiting for transfers between devices, from_peers(): lax.ppermute(x, axis, [(i, (i + k) % n) for i in range(n)])  15.3 us
    all_gather x1, blocking collectives, shards(): weights = lax.all_gather(weights, 'x')  10.4 us
    ppermute x3, starting transfers between devices, shards(): lax.ppermute(block_for(k), 'x', [(i, (i + k) % nx) for i in range(nx)])  9.69 us
  transfers between devices with their start and end apart: 22, of which 10 were waited for; matrix products, arithmetic and copies ran while one was open for 11% of the time, Pallas kernels for 0%

profile of v2, /device:TPU:11, one launch (start us, length us, event | category | flops | bytes accessed | tf_op | source)
XLA Modules:
  0.0 278.6 jit_solution(10985576280237337929)
XLA Ops:
  11.3 8.3 %all-to-all-start.1 = ((bf16[16,6,128]{2,1,0:T(8,128)(2,1)}), bf16[16,6,128]{2,1,0:T(8,128)(2,1)S(1)}, u32[]{:S(2)}, u32[]{:S(2)}) async-start(bf16[16,6,128]{2,1,0:T(8,128)(2,1)} %reshape.328), calls=%async_computation.1 | async-start | bytes 65536 | tf_op jit(solution)/shard_map/all_to_all | solution.py:18
  22.3 3.9 %collective-permute-start.4 = (bf16[640,128]{1,0:T(8,128)(2,1)}, bf16[640,128]{1,0:T(8,128)(2,1)S(1)}, u32[]{:S(2)}, u32[]{:S(2)}) collective-permute-start(bf16[640,128]{1,0:T(8,128)(2,1)} %get-tuple-element.26), channel_id=1, source_target_pairs={{0,16},{8,24},{16,0},{24,8},{1,17},{9,25},{17,1},{25,9},{2,18},{10... | collective-permute-start | bytes 491528 | tf_op jit(solution)/shard_map/ppermute | solution.py:129
  26.2 3.0 %collective-permute-start.5 = (bf16[640,128]{1,0:T(8,128)(2,1)}, bf16[640,128]{1,0:T(8,128)(2,1)S(1)}, u32[]{:S(2)}, u32[]{:S(2)}) collective-permute-start(bf16[640,128]{1,0:T(8,128)(2,1)} %get-tuple-element.27), channel_id=1, source_target_pairs={{0,24},{8,0},{16,8},{24,16},{1,25},{9,1},{17,9},{25,17},{2,26},{10... | collective-permute-start | bytes 491528 | tf_op jit(solution)/shard_map/ppermute | solution.py:129
  36.4 4.1 %collective-permute-start.1 = (bf16[192,1024]{1,0:T(8,128)(2,1)}, bf16[192,1024]{1,0:T(8,128)(2,1)}, u32[]{:S(2)}, u32[]{:S(2)}) collective-permute-start(bf16[192,1024]{1,0:T(8,128)(2,1)} %convolution_convert_fusion.2), channel_id=1, source_target_pairs={{0,64},{32,96},{64,0},{96,32},{1,65},{33,97},{65,1},{97,33},{2,66}... | collective-permute-start | bytes 1179656 | tf_op jit(solution)/shard_map/ppermute | solution.py:84
  43.5 3.4 %collective-permute-start = (bf16[192,1024]{1,0:T(8,128)(2,1)}, bf16[192,1024]{1,0:T(8,128)(2,1)}, u32[]{:S(2)}, u32[]{:S(2)}) collective-permute-start(bf16[192,1024]{1,0:T(8,128)(2,1)} %convolution_convert_fusion.3), channel_id=1, source_target_pairs={{0,32},{32,64},{64,96},{96,0},{1,33},{33,65},{65,97},{97,1},{2,34}... | collective-permute-start | bytes 1179656 | tf_op jit(solution)/shard_map/ppermute | solution.py:84
  48.0 15.3 %all-to-all-start.2 = ((bf16[8,128,128]{2,1,0:T(8,128)(2,1)}), bf16[8,128,128]{2,1,0:T(8,128)(2,1)S(1)}, u32[]{:S(2)}, u32[]{:S(2)}) async-start(bf16[8,128,128]{2,1,0:T(8,128)(2,1)} %pad_maximum_fusion.6), calls=%async_computation.2 | async-start | bytes 524288 | tf_op jit(solution)/shard_map/all_to_all | solution.py:18
  66.5 13.7 %all-to-all-done.2 = bf16[8,128,128]{2,1,0:T(8,128)(2,1)S(1)} async-done(((bf16[8,128,128]{2,1,0:T(8,128)(2,1)}), bf16[8,128,128]{2,1,0:T(8,128)(2,1)S(1)}, u32[]{:S(2)}, u32[]{:S(2)}) %all-to-all-start.2) | async-done | bytes 262176 | tf_op jit(solution)/shard_map/all_to_all | solution.py:18
  80.2 8.4 %all-to-all-start = ((bf16[4,48,1024]{2,1,0:T(8,128)(2,1)}), bf16[4,48,1024]{2,1,0:T(8,128)(2,1)S(1)}, u32[]{:S(2)}, u32[]{:S(2)}) async-start(bf16[4,48,1024]{2,1,0:T(8,128)(2,1)} %bitcast.7), calls=%async_computation | async-start | bytes 786432 | tf_op jit(solution)/shard_map/all_to_all | solution.py:18
  89.7 10.4 %all_gather.3 = bf16[4,80,1024]{2,1,0:T(8,128)(2,1)S(1)} all-gather(bf16[1,80,1024]{2,1,0:T(8,128)(2,1)S(1)} %all_gather_reshape.3), channel_id=1, replica_groups=mesh['zl'=4,'x'=4,'y'=4,'zh'=4,'c'=2] {'x'}, dimensions={0}, use_global_device_ids=true | all-gather | bytes 819200 | tf_op jit(solution)/shard_map/all_gather | solution.py:143
  100.2 3.0 %collective-permute-start.8 = (bf16[256,1024]{1,0:T(8,128)(2,1)S(1)}, bf16[256,1024]{1,0:T(8,128)(2,1)S(1)}, u32[]{:S(2)}, u32[]{:S(2)}) collective-permute-start(bf16[256,1024]{1,0:T(8,128)(2,1)S(1)} %bitcast.157), channel_id=1, source_target_pairs={{0,24},{8,0},{16,8},{24,16},{1,25},{9,1},{17,9},{25,17},{2,26},{10... | collective-permute-start | bytes 1572872 | tf_op jit(solution)/shard_map/ppermute | solution.py:37
  105.5 5.3 %collective-permute-start.7 = (bf16[256,1024]{1,0:T(8,128)(2,1)S(1)}, bf16[256,1024]{1,0:T(8,128)(2,1)}, u32[]{:S(2)}, u32[]{:S(2)}) collective-permute-start(bf16[256,1024]{1,0:T(8,128)(2,1)S(1)} %bitcast.159), channel_id=1, source_target_pairs={{0,16},{8,24},{16,0},{24,8},{1,17},{9,25},{17,1},{25,9},{2,18},{10... | collective-permute-start | bytes 1572872 | tf_op jit(solution)/shard_map/ppermute | solution.py:37
  115.8 7.9 %collective-permute-done.7 = bf16[256,1024]{1,0:T(8,128)(2,1)} collective-permute-done((bf16[256,1024]{1,0:T(8,128)(2,1)S(1)}, bf16[256,1024]{1,0:T(8,128)(2,1)}, u32[]{:S(2)}, u32[]{:S(2)}) %collective-permute-start.7) | collective-permute-done | bytes 524320 | tf_op jit(solution)/shard_map/ppermute | solution.py:37
  129.0 7.8 %reduce-scatter.7.cloned.1.call-done = bf16[32,128]{1,0:T(8,128)(2,1)} async-done(((bf16[256,128]{1,0:T(8,128)(2,1)}), bf16[32,128]{1,0:T(8,128)(2,1)}) %reduce-scatter.7.cloned.1.call-update) | async-done | bytes 8208 | tf_op jit(solution)/shard_map/reduce_scatter | solution.py:158
  138.3 7.6 %all-to-all-start.3 = ((bf16[8,88,128]{2,1,0:T(8,128)(2,1)}), bf16[8,88,128]{2,1,0:T(8,128)(2,1)S(1)}, u32[]{:S(2)}, u32[]{:S(2)}) async-start(bf16[8,88,128]{2,1,0:T(8,128)(2,1)} %broadcast_in_dim.124), calls=%async_computation.3 | async-start | bytes 360448 | tf_op jit(solution)/shard_map/all_to_all | solution.py:18
  145.9 13.6 %all-to-all-done.3 = bf16[8,88,128]{2,1,0:T(8,128)(2,1)S(1)} async-done(((bf16[8,88,128]{2,1,0:T(8,128)(2,1)}), bf16[8,88,128]{2,1,0:T(8,128)(2,1)S(1)}, u32[]{:S(2)}, u32[]{:S(2)}) %all-to-all-start.3) | async-done | bytes 180256 | tf_op jit(solution)/shard_map/all_to_all | solution.py:18
  163.3 5.7 %all-to-all-start.4 = ((bf16[4,80,1024]{2,1,0:T(8,128)(2,1)}), bf16[4,80,1024]{2,1,0:T(8,128)(2,1)S(1)}, u32[]{:S(2)}, u32[]{:S(2)}) async-start(bf16[4,80,1024]{2,1,0:T(8,128)(2,1)} %pad_maximum_fusion.4), calls=%async_computation.4 | async-start | bytes 1310720 | tf_op jit(solution)/shard_map/all_to_all | solution.py:18
  170.4 14.3 %all-to-all-done.4 = bf16[4,80,1024]{2,1,0:T(8,128)(2,1)S(1)} async-done(((bf16[4,80,1024]{2,1,0:T(8,128)(2,1)}), bf16[4,80,1024]{2,1,0:T(8,128)(2,1)S(1)}, u32[]{:S(2)}, u32[]{:S(2)}) %all-to-all-start.4) | async-done | bytes 655392 | tf_op jit(solution)/shard_map/all_to_all | solution.py:18
  186.3 7.8 %all-to-all-start.5 = ((bf16[4,200,1024]{2,1,0:T(8,128)(2,1)}), bf16[4,200,1024]{2,1,0:T(8,128)(2,1)S(1)}, u32[]{:S(2)}, u32[]{:S(2)}) async-start(bf16[4,200,1024]{2,1,0:T(8,128)(2,1)} %pad_maximum_fusion.1), calls=%async_computation.5 | async-start | bytes 3276800 | tf_op jit(solution)/shard_map/all_to_all | solution.py:18
  198.4 14.3 %all-to-all-done.5 = bf16[4,200,1024]{2,1,0:T(8,128)(2,1)S(1)} async-done(((bf16[4,200,1024]{2,1,0:T(8,128)(2,1)}), bf16[4,200,1024]{2,1,0:T(8,128)(2,1)S(1)}, u32[]{:S(2)}, u32[]{:S(2)}) %all-to-all-start.5) | async-done | bytes 1638432 | tf_op jit(solution)/shard_map/all_to_all | solution.py:18
  215.6 4.1 %all-to-all-start.6 = ((bf16[4,88,1024]{2,1,0:T(8,128)(2,1)}), bf16[4,88,1024]{2,1,0:T(8,128)(2,1)S(1)}, u32[]{:S(2)}, u32[]{:S(2)}) async-start(bf16[4,88,1024]{2,1,0:T(8,128)(2,1)} %pad_maximum_fusion.2), calls=%async_computation.6 | async-start | bytes 1441792 | tf_op jit(solution)/shard_map/all_to_all | solution.py:18
  219.7 24.0 %reduce-scatter.5.cloned.1.call-done = bf16[304,128]{1,0:T(8,128)(2,1)} async-done(((bf16[2432,128]{1,0:T(8,128)(2,1)}), bf16[304,128]{1,0:T(8,128)(2,1)}) %reduce-scatter.5.cloned.1.call-update) | async-done | bytes 77840 | tf_op jit(solution)/shard_map/reduce_scatter | solution.py:198
  246.1 7.4 %all-to-all-start.7 = ((f32[16,42,128]{2,1,0:T(8,128)}), f32[16,42,128]{2,1,0:T(8,128)S(1)}, u32[]{:S(2)}, u32[]{:S(2)}) async-start(f32[16,42,128]{2,1,0:T(8,128)} %pad_maximum_fusion.5), calls=%async_computation.8 | async-start | bytes 786432 | tf_op jit(solution)/shard_map/all_to_all | solution.py:18
  259.0 3.8 %collective-permute-start.11 = (bf16[80,1024]{1,0:T(8,128)(2,1)S(1)}, bf16[80,1024]{1,0:T(8,128)(2,1)S(1)}, u32[]{:S(2)}, u32[]{:S(2)}) collective-permute-start(bf16[80,1024]{1,0:T(8,128)(2,1)S(1)} %get-tuple-element.12), channel_id=1, source_target_pairs={{0,24},{8,0},{16,8},{24,16},{1,25},{9,1},{17,9},{25,17},{2,26},{10... | collective-permute-start | bytes 491528 | tf_op jit(solution)/shard_map/ppermute | solution.py:37
  265.1 4.2 %collective-permute-done.11 = bf16[80,1024]{1,0:T(8,128)(2,1)S(1)} collective-permute-done((bf16[80,1024]{1,0:T(8,128)(2,1)S(1)}, bf16[80,1024]{1,0:T(8,128)(2,1)S(1)}, u32[]{:S(2)}, u32[]{:S(2)}) %collective-permute-start.11) | collective-permute-done | bytes 163872 | tf_op jit(solution)/shard_map/ppermute | solution.py:37
  (223 shorter events, 62.2 us)
Async XLA Ops:
  11.3 31.9 %all-to-all-start.1 = ((bf16[16,6,128]{2,1,0:T(8,128)(2,1)}), bf16[16,6,128]{2,1,0:T(8,128)(2,1)S(1)}, u32[]{:S(2)}, u32[]{:S(2)}) async-start(bf16[16,6,128]{2,1,0:T(8,128)(2,1)} %reshape.328), calls=%async_computation.1 | async-start | bytes 65536 | tf_op jit(solution)/shard_map/all_to_all | solution.py:18
  22.3 21.2 %collective-permute-start.4 = (bf16[640,128]{1,0:T(8,128)(2,1)}, bf16[640,128]{1,0:T(8,128)(2,1)S(1)}, u32[]{:S(2)}, u32[]{:S(2)}) collective-permute-start(bf16[640,128]{1,0:T(8,128)(2,1)} %get-tuple-element.26), channel_id=1, source_target_pairs={{0,16},{8,24},{16,0},{24,8},{1,17},{9,25},{17,1},{25,9},{2,18},{10... | collective-permute-start | bytes 491528 | tf_op jit(solution)/shard_map/ppermute | solution.py:129
  26.2 20.7 %collective-permute-start.5 = (bf16[640,128]{1,0:T(8,128)(2,1)}, bf16[640,128]{1,0:T(8,128)(2,1)S(1)}, u32[]{:S(2)}, u32[]{:S(2)}) collective-permute-start(bf16[640,128]{1,0:T(8,128)(2,1)} %get-tuple-element.27), channel_id=1, source_target_pairs={{0,24},{8,0},{16,8},{24,16},{1,25},{9,1},{17,9},{25,17},{2,26},{10... | collective-permute-start | bytes 491528 | tf_op jit(solution)/shard_map/ppermute | solution.py:129
  29.2 17.7 %collective-permute-start.3 = (bf16[640,128]{1,0:T(8,128)(2,1)}, bf16[640,128]{1,0:T(8,128)(2,1)S(1)}, u32[]{:S(2)}, u32[]{:S(2)}) collective-permute-start(bf16[640,128]{1,0:T(8,128)(2,1)} %get-tuple-element.25), channel_id=1, source_target_pairs={{0,8},{8,16},{16,24},{24,0},{1,9},{9,17},{17,25},{25,1},{2,10},{10... | collective-permute-start | bytes 491528 | tf_op jit(solution)/shard_map/ppermute | solution.py:129
  33.1 31.1 %collective-permute-start.2 = (bf16[192,1024]{1,0:T(8,128)(2,1)}, bf16[192,1024]{1,0:T(8,128)(2,1)S(1)}, u32[]{:S(2)}, u32[]{:S(2)}) collective-permute-start(bf16[192,1024]{1,0:T(8,128)(2,1)} %convolution_convert_fusion.1), channel_id=1, source_target_pairs={{0,96},{32,0},{64,32},{96,64},{1,97},{33,1},{65,33},{97,65},{2,98}... | collective-permute-start | bytes 1179656 | tf_op jit(solution)/shard_map/ppermute | solution.py:84
  36.4 27.8 %collective-permute-start.1 = (bf16[192,1024]{1,0:T(8,128)(2,1)}, bf16[192,1024]{1,0:T(8,128)(2,1)}, u32[]{:S(2)}, u32[]{:S(2)}) collective-permute-start(bf16[192,1024]{1,0:T(8,128)(2,1)} %convolution_convert_fusion.2), channel_id=1, source_target_pairs={{0,64},{32,96},{64,0},{96,32},{1,65},{33,97},{65,1},{97,33},{2,66}... | collective-permute-start | bytes 1179656 | tf_op jit(solution)/shard_map/ppermute | solution.py:84
  43.5 20.7 %collective-permute-start = (bf16[192,1024]{1,0:T(8,128)(2,1)}, bf16[192,1024]{1,0:T(8,128)(2,1)}, u32[]{:S(2)}, u32[]{:S(2)}) collective-permute-start(bf16[192,1024]{1,0:T(8,128)(2,1)} %convolution_convert_fusion.3), channel_id=1, source_target_pairs={{0,32},{32,64},{64,96},{96,0},{1,33},{33,65},{65,97},{97,1},{2,34}... | collective-permute-start | bytes 1179656 | tf_op jit(solution)/shard_map/ppermute | solution.py:84
  48.0 32.2 %all-to-all-start.2 = ((bf16[8,128,128]{2,1,0:T(8,128)(2,1)}), bf16[8,128,128]{2,1,0:T(8,128)(2,1)S(1)}, u32[]{:S(2)}, u32[]{:S(2)}) async-start(bf16[8,128,128]{2,1,0:T(8,128)(2,1)} %pad_maximum_fusion.6), calls=%async_computation.2 | async-start | bytes 524288 | tf_op jit(solution)/shard_map/all_to_all | solution.py:18
  80.2 31.8 %all-to-all-start = ((bf16[4,48,1024]{2,1,0:T(8,128)(2,1)}), bf16[4,48,1024]{2,1,0:T(8,128)(2,1)S(1)}, u32[]{:S(2)}, u32[]{:S(2)}) async-start(bf16[4,48,1024]{2,1,0:T(8,128)(2,1)} %bitcast.7), calls=%async_computation | async-start | bytes 786432 | tf_op jit(solution)/shard_map/all_to_all | solution.py:18
  88.5 48.3 %reduce-scatter.7.cloned.1.call-start = ((), (), s32[]{:S(2)}) async-start(), calls=%async_computation.11 | async-start | bytes 73728 | tf_op jit(solution)/shard_map/reduce_scatter | solution.py:158
  100.2 25.4 %collective-permute-start.8 = (bf16[256,1024]{1,0:T(8,128)(2,1)S(1)}, bf16[256,1024]{1,0:T(8,128)(2,1)S(1)}, u32[]{:S(2)}, u32[]{:S(2)}) collective-permute-start(bf16[256,1024]{1,0:T(8,128)(2,1)S(1)} %bitcast.157), channel_id=1, source_target_pairs={{0,24},{8,0},{16,8},{24,16},{1,25},{9,1},{17,9},{25,17},{2,26},{10... | collective-permute-start | bytes 1572872 | tf_op jit(solution)/shard_map/ppermute | solution.py:37
  103.2 11.7 %collective-permute-start.6 = (bf16[256,1024]{1,0:T(8,128)(2,1)S(1)}, bf16[256,1024]{1,0:T(8,128)(2,1)S(1)}, u32[]{:S(2)}, u32[]{:S(2)}) collective-permute-start(bf16[256,1024]{1,0:T(8,128)(2,1)S(1)} %bitcast.158), channel_id=1, source_target_pairs={{0,8},{8,16},{16,24},{24,0},{1,9},{9,17},{17,25},{25,1},{2,10},{10... | collective-permute-start | bytes 1572872 | tf_op jit(solution)/shard_map/ppermute | solution.py:37
  105.5 18.2 %collective-permute-start.7 = (bf16[256,1024]{1,0:T(8,128)(2,1)S(1)}, bf16[256,1024]{1,0:T(8,128)(2,1)}, u32[]{:S(2)}, u32[]{:S(2)}) collective-permute-start(bf16[256,1024]{1,0:T(8,128)(2,1)S(1)} %bitcast.159), channel_id=1, source_target_pairs={{0,16},{8,24},{16,0},{24,8},{1,17},{9,25},{17,1},{25,9},{2,18},{10... | collective-permute-start | bytes 1572872 | tf_op jit(solution)/shard_map/ppermute | solution.py:37
  138.3 21.3 %all-to-all-start.3 = ((bf16[8,88,128]{2,1,0:T(8,128)(2,1)}), bf16[8,88,128]{2,1,0:T(8,128)(2,1)S(1)}, u32[]{:S(2)}, u32[]{:S(2)}) async-start(bf16[8,88,128]{2,1,0:T(8,128)(2,1)} %broadcast_in_dim.124), calls=%async_computation.3 | async-start | bytes 360448 | tf_op jit(solution)/shard_map/all_to_all | solution.py:18
  163.3 21.4 %all-to-all-start.4 = ((bf16[4,80,1024]{2,1,0:T(8,128)(2,1)}), bf16[4,80,1024]{2,1,0:T(8,128)(2,1)S(1)}, u32[]{:S(2)}, u32[]{:S(2)}) async-start(bf16[4,80,1024]{2,1,0:T(8,128)(2,1)} %pad_maximum_fusion.4), calls=%async_computation.4 | async-start | bytes 1310720 | tf_op jit(solution)/shard_map/all_to_all | solution.py:18
  186.3 26.4 %all-to-all-start.5 = ((bf16[4,200,1024]{2,1,0:T(8,128)(2,1)}), bf16[4,200,1024]{2,1,0:T(8,128)(2,1)S(1)}, u32[]{:S(2)}, u32[]{:S(2)}) async-start(bf16[4,200,1024]{2,1,0:T(8,128)(2,1)} %pad_maximum_fusion.1), calls=%async_computation.5 | async-start | bytes 3276800 | tf_op jit(solution)/shard_map/all_to_all | solution.py:18
  194.1 49.6 %reduce-scatter.5.cloned.1.call-start = ((), (), s32[]{:S(2)}) async-start(), calls=%async_computation.10 | async-start | bytes 700416 | tf_op jit(solution)/shard_map/reduce_scatter | solution.py:198
  214.7 30.2 %copy-start.27 = (s32[16,6]{0,1:T(8,128)S(1)}, s32[16,6]{0,1:T(8,128)}, u32[]{:S(2)}) copy-start(s32[16,6]{0,1:T(8,128)} %copy-done.26) | copy-start | bytes 1156
  214.7 30.2 %copy-start.35 = (pred[16,6]{0,1:T(8,128)(4,1)S(1)}, pred[16,6]{0,1:T(8,128)(4,1)}, u32[]{:S(2)}) copy-start(pred[16,6]{0,1:T(8,128)(4,1)} %copy-done.34) | copy-start | bytes 292
  215.6 29.5 %all-to-all-start.6 = ((bf16[4,88,1024]{2,1,0:T(8,128)(2,1)}), bf16[4,88,1024]{2,1,0:T(8,128)(2,1)S(1)}, u32[]{:S(2)}, u32[]{:S(2)}) async-start(bf16[4,88,1024]{2,1,0:T(8,128)(2,1)} %pad_maximum_fusion.2), calls=%async_computation.6 | async-start | bytes 1441792 | tf_op jit(solution)/shard_map/all_to_all | solution.py:18
  246.1 23.2 %all-to-all-start.7 = ((f32[16,42,128]{2,1,0:T(8,128)}), f32[16,42,128]{2,1,0:T(8,128)S(1)}, u32[]{:S(2)}, u32[]{:S(2)}) async-start(f32[16,42,128]{2,1,0:T(8,128)} %pad_maximum_fusion.5), calls=%async_computation.8 | async-start | bytes 786432 | tf_op jit(solution)/shard_map/all_to_all | solution.py:18
  253.7 9.1 %collective-permute-start.9 = (bf16[80,1024]{1,0:T(8,128)(2,1)S(1)}, bf16[80,1024]{1,0:T(8,128)(2,1)S(1)}, u32[]{:S(2)}, u32[]{:S(2)}) collective-permute-start(bf16[80,1024]{1,0:T(8,128)(2,1)S(1)} %get-tuple-element.12), channel_id=1, source_target_pairs={{0,8},{8,16},{16,24},{24,0},{1,9},{9,17},{17,25},{25,1},{2,10},{10... | collective-permute-start | bytes 491528 | tf_op jit(solution)/shard_map/ppermute | solution.py:37
  256.2 8.8 %collective-permute-start.10 = (bf16[80,1024]{1,0:T(8,128)(2,1)S(1)}, bf16[80,1024]{1,0:T(8,128)(2,1)S(1)}, u32[]{:S(2)}, u32[]{:S(2)}) collective-permute-start(bf16[80,1024]{1,0:T(8,128)(2,1)S(1)} %get-tuple-element.12), channel_id=1, source_target_pairs={{0,16},{8,24},{16,0},{24,8},{1,17},{9,25},{17,1},{25,9},{2,18},{10... | collective-permute-start | bytes 491528 | tf_op jit(solution)/shard_map/ppermute | solution.py:37
  259.0 10.3 %collective-permute-start.11 = (bf16[80,1024]{1,0:T(8,128)(2,1)S(1)}, bf16[80,1024]{1,0:T(8,128)(2,1)S(1)}, u32[]{:S(2)}, u32[]{:S(2)}) collective-permute-start(bf16[80,1024]{1,0:T(8,128)(2,1)S(1)} %get-tuple-element.12), channel_id=1, source_target_pairs={{0,24},{8,0},{16,8},{24,16},{1,25},{9,1},{17,9},{25,17},{2,26},{10... | collective-permute-start | bytes 491528 | tf_op jit(solution)/shard_map/ppermute | solution.py:37
  (34 other events, 424.6 us)
Sparse Core Ops, SparseCore 0:
  92.7 44.0 reduce-scatter.6
  198.6 45.0 reduce-scatter.4

commit v3 on v2

--- a/solution.py
+++ b/solution.py
@@ -23,6 +23,10 @@
     return jnp.sum(jnp.where(matches, grid_in, 0), axis=which_axis)
 
 
+def after(x, other):
+    return x + (other[(0,) * other.ndim] * 0).astype(x.dtype)
+
+
 def copies(x, n):
     return jnp.broadcast_to(x[None], (n, *x.shape))
 
@@ -35,6 +39,14 @@
 def from_peers(x, axis):
     n = lax.axis_size(axis)
     return [x] + [lax.ppermute(x, axis, [(i, (i + k) % n) for i in range(n)]) for k in range(1, n)]
+
+
+def to_peers(blocks, axis):
+    n, me = lax.axis_size(axis), lax.axis_index(axis)
+    return [blocks(me)] + [
+        lax.ppermute(blocks(lax.rem(me + k, n)), axis, [(i, (i + k) % n) for i in range(n)])
+        for k in range(1, n)
+    ]
 
 
 def placed(blocks, dim, axis):
@@ -73,20 +85,6 @@
     rows = toks + n_frames
     gain = lax.dynamic_slice_in_dim(gain_all, tp_index * width, width, 0)
 
-    by_x = frames.reshape(nzl, nx, n_frames, frames.shape[1])
-
-    def block_for(k):
-        part = lax.dynamic_index_in_dim(by_x, lax.rem(x_index + k, nx), 1, False)
-        part = part.reshape(nzl * n_frames, frames.shape[1])
-        return dot(part, projector, 1, 0).astype(bf16)
-
-    x_parts = [
-        lax.ppermute(block_for(k), "x", [(i, (i + k) % nx) for i in range(nx)]) for k in range(1, nx)
-    ]
-    x_sum = block_for(0).astype(f32)
-    for part in x_parts:
-        x_sum = x_sum + part.astype(f32)
-
     own_sizes = pick_entry(clip_len[0], grp_index, 0)
     before = lax.broadcasted_iota(jnp.int32, (ng, ng), 1) < lax.broadcasted_iota(jnp.int32, (ng, ng), 0)
     own_starts = jnp.sum(jnp.where(before, own_sizes[None, :], 0), axis=1)
@@ -137,15 +135,6 @@
     sent = jnp.concatenate(
         [wa, copies(jnp.concatenate([up_piece, grad_frames], axis=0), nt)], axis=1
     )
-    came = exchange(sent, TP)
-    at = piece + up_rows
-    weights = jnp.moveaxis(came[:, :at], 0, 1).reshape(at, nt * cols)
-    weights = lax.all_gather(weights, "x")
-    up_full = weights[:, piece:].reshape(rank, nt * cols)
-    weights = from_peers(weights[:, :piece].reshape(nx * piece, nt * cols), "y")
-    grad_full = jnp.moveaxis(came[:, at:], 0, 1).reshape(n_frames, nt * cols)
-    lora_frames = (adapter_scale * dot(grad_full, up_full, 1, 1)).astype(bf16)
-
     text_wide = text.astype(f32)
     text_scaled = text_wide * gain[None, :]
     pair = jnp.concatenate(
@@ -155,16 +144,48 @@
         ],
         axis=1,
     )
+    sent, pair, frames_in = lax.optimization_barrier((sent, pair, frames))
     pair = lax.psum_scatter(pair, TP, scatter_dimension=0, tiled=True)
     sq_text = dot(jnp.ones((8, width), bf16), (text_wide * text_wide).astype(bf16), 1, 1)[0]
+
+    came = exchange(sent, TP)
+
+    by_x = frames_in.reshape(nzl, nx, n_frames, frames.shape[1])
+
+    def block_for(k):
+        part = lax.dynamic_index_in_dim(by_x, lax.rem(x_index + k, nx), 1, False)
+        part = part.reshape(nzl * n_frames, frames.shape[1])
+        return dot(part, projector, 1, 0).astype(bf16)
+
+    x_parts = [
+        lax.ppermute(block_for(k), "x", [(i, (i + k) % nx) for i in range(nx)]) for k in range(1, nx)
+    ]
+    x_sum = block_for(0).astype(f32)
+    for part in x_parts:
+        x_sum = x_sum + part.astype(f32)
+
+    at = piece + up_rows
+    grad_full = jnp.moveaxis(came[:, at:], 0, 1).reshape(n_frames, nt * cols)
+    grad_all = jnp.concatenate(from_peers(grad_full, "y"), axis=0)
+    weights = jnp.moveaxis(came[:, :at], 0, 1).reshape(at, nt * cols)
+    weights = lax.all_gather(weights, "x")
+    up_full = weights[:, piece:].reshape(rank, nt * cols)
+    weights = weights[:, :piece].reshape(nx * piece, nt * cols)
+    lora_frames = (adapter_scale * dot(grad_full, up_full, 1, 1)).astype(bf16)
+    spread = dot(grad_all, weights, 1, 1).astype(bf16).reshape(ny, n_frames, nx * piece)
+    parts = [spread[0]] + [
+        lax.ppermute(spread[k], "y", [(i, (i - k) % ny) for i in range(ny)]) for k in range(1, ny)
+    ]
+    parts = [parts[0]] + parts[:0:-1]
+    grad_norm = placed([p.astype(f32) for p in parts], 1, "y")
+    grad_norm = grad_norm + dot(lora_frames, down_t, 1, 0)
+    weights = lax.all_gather(weights, "y", axis=0, tiled=True)
 
     blocks = exchange(x_sum.astype(bf16).reshape(nzl, n_frames, width), "zl")
     embedded = jnp.sum(blocks.astype(f32), axis=0).astype(bf16)
     wide = embedded.astype(f32)
     scaled = wide * gain[None, :]
 
-    grad_norm = placed([dot(grad_full, w, 1, 1) for w in weights], 1, "y")
-    grad_norm = grad_norm + dot(lora_frames, down_t, 1, 0)
     sq_hi, sq_lo = two_halves(jnp.sum(wide * wide, axis=1, keepdims=True))
     d_hi, d_lo = two_halves(jnp.sum(scaled * grad_norm, axis=1, keepdims=True))
     low_frames = dot(scaled.astype(bf16), down_t, 1, 1).astype(bf16)
@@ -180,23 +201,16 @@
     sq_frames = stats[:n_frames, rank : rank + 1] + stats[:n_frames, rank + 1 : rank + 2]
     dots = stats[:n_frames, rank + 2 : rank + 3] + stats[:n_frames, rank + 3 : rank + 4]
     sq_text = (stats[n_frames : n_frames + n_l] + stats[n_frames + n_l : n_frames + 2 * n_l]).reshape(toks, 1)
-    inv_text = lax.rsqrt(sq_text / full_width + norm_eps)
-    inv_f = lax.rsqrt(sq_frames / full_width + norm_eps)
-    inv_rms = jnp.concatenate([inv_text, inv_f], axis=0)
+    inv_rms = lax.rsqrt(jnp.concatenate([sq_text, sq_frames], axis=0) / full_width + norm_eps)
     lora = jnp.concatenate([pair[:, :rank], lora_frames], axis=0)
     low = jnp.concatenate([pair[:, rank:].astype(f32), stats[:n_frames, :rank]], axis=0)
     low_half = (low * inv_rms).astype(bf16)
 
     all_scaled = jnp.concatenate([text_scaled, scaled], axis=0)
-    quarter = width // ny
-    base = jnp.zeros((rows, nt * cols), f32)
-    for j, w in enumerate(weights):
-        at = lax.rem(y_index - j + ny, ny) * quarter
-        base = base + dot(lax.dynamic_slice_in_dim(all_scaled, at, quarter, 1).astype(bf16), w, 1, 0)
-    base = base.astype(bf16)
-    base = jnp.moveaxis(base.reshape(rows, nt, cols), 1, 0)
-    base = lax.psum_scatter(base.reshape(nt * rows, cols), TP, scatter_dimension=0, tiled=True)
-    values = base.astype(f32) * inv_rms + adapter_scale * dot(low_half, up, 1, 0)
+    base = dot(all_scaled.astype(bf16), weights, 1, 0).astype(bf16)
+    base = jnp.moveaxis(base.reshape(rows, nt, cols), 1, 0).reshape(nt * rows, cols)
+    summed = lax.psum_scatter(base, TP, scatter_dimension=0, tiled=True)
+    values = summed.astype(f32) * inv_rms + adapter_scale * dot(low_half, up, 1, 0)
     values = values.astype(bf16)
 
     normed = (all_scaled * inv_rms).astype(bf16)
@@ -206,12 +220,15 @@
     up_part = jnp.pad(up_part, ((0, 0), (0, width - cols))).reshape(nzl, nx, k, width)
     adapters = jnp.concatenate([down_part, up_part], axis=2).reshape(nzl, nx * 2 * k, width)
 
+    inv_f = after(inv_rms[toks:], base)
     frame_grad = (
         inv_f * gain[None, :] * grad_norm - wide * (inv_f * inv_f * inv_f * dots / full_width)
     ).astype(bf16)
-    came = exchange(jnp.concatenate([copies(frame_grad, nzl), adapters], axis=1), "zl")
-    adapters = jnp.sum(came[:, n_frames:].astype(f32), axis=0).astype(bf16).reshape(nx, 2 * k, width)
-    frame_grad = came[:, :n_frames].reshape(nzl * n_frames, width)
+    near = to_peers(
+        lambda z: jnp.concatenate([frame_grad, lax.dynamic_index_in_dim(adapters, z, 0, False)], axis=0), "zl"
+    )
+    adapters = sum(b[n_frames:].astype(f32) for b in near).astype(bf16).reshape(nx, 2 * k, width)
+    frame_grad = placed([b[:n_frames] for b in near], 0, "zl")
     came = exchange(jnp.concatenate([copies(frame_grad, nx), adapters], axis=1), "x")
     adapters = jnp.sum(came[:, nzl * n_frames :].astype(f32), axis=0).astype(bf16)
     all_grad = came[:, : nzl * n_frames].reshape(nx, nzl, n_frames, width)

time: 280 us -> 274 us (0.979)
  starting transfers between devices: 103 us -> 120 us
  waiting for transfers between devices: 103 us -> 90.4 us
  matrix products: 23.9 us -> 14.5 us
    all_to_all x8 -> x7, waiting for transfers between devices: 55.8 us -> 34.5 us  [exchange(): return lax.all_to_all(blocks, axis, split_axis=0, concat_axis=0, tiled=True)]
    ppermute x0 -> x6, starting transfers between devices: none -> 18.4 us  [the longest x3 9.25 us: to_peers(): lax.ppermute(blocks(lax.rem(me + k, n)), axis, [(i, (i + k) % n) for i in...]
    ppermute x3, waiting for transfers between devices: 0.01 us -> 12 us  [shards(): lax.ppermute(block_for(k), 'x', [(i, (i + k) % nx) for i in range(nx)])]
    ppermute x0 -> x6, waiting for transfers between devices: none -> 11.4 us  [the longest x3 10.2 us: to_peers(): lax.ppermute(blocks(lax.rem(me + k, n)), axis, [(i, (i + k) % n) for i in...]
    dot_general x26 -> x20, matrix products: 23.9 us -> 14.5 us  [dot(): lax.dot_general(a, b, (((ca,), (cb,)), ((), ())), preferred_element_type=...]
    ppermute x6, waiting for transfers between devices: 15.3 us -> 6.41 us  [from_peers(): lax.ppermute(x, axis, [(i, (i + k) % n) for i in range(n)])]
    reduce_scatter x1, waiting for transfers between devices: 7.77 us -> 0.02 us  [shards(): pair = lax.psum_scatter(pair, TP, scatter_dimension=0, tiled=True)]
    ppermute x3, waiting for transfers between devices: 0.01 us -> 3.67 us  [shards(): lax.ppermute(for_y(k), 'y', [(i, (i + k) % ny) for i in range(ny)])]
  transfers between devices with their start and end apart: 22 -> 28, of which waited for: 10 -> 12; matrix products, arithmetic and copies ran while one was open for 11% -> 7% of each run, Pallas kernels for 0% -> 0%
where the time goes in v3:
time: 274 us; the launch traced here: 272 us
  starting transfers between devices  120 us (44%)
  waiting for transfers between devices  90.4 us (33%)
  between operations  17.3 us (6%)
  matrix products  14.5 us (5%)
  local copies, waits for them, and re-layouts  11.9 us (4%)
  blocking collectives  10.7 us (4%)
  other arithmetic  7.62 us (3%)
    all_to_all x7, starting transfers between devices, exchange(): return lax.all_to_all(blocks, axis, split_axis=0, concat_axis=0, tiled=True)  63.2 us
    all_to_all x7, waiting for transfers between devices, exchange(): return lax.all_to_all(blocks, axis, split_axis=0, concat_axis=0, tiled=True)  34.5 us
    reduce_scatter x1, waiting for transfers between devices, shards(): summed = lax.psum_scatter(base, TP, scatter_dimension=0, tiled=True)  21.7 us
    ppermute x6, starting transfers between devices, from_peers(): lax.ppermute(x, axis, [(i, (i + k) % n) for i in range(n)])  19.1 us
    dot_general x20, matrix products, dot(): lax.dot_general(a, b, (((ca,), (cb,)), ((), ())), preferred_element_type=...  14.5 us
    ppermute x3, waiting for transfers between devices, shards(): lax.ppermute(block_for(k), 'x', [(i, (i + k) % nx) for i in range(nx)])  12 us
    all_gather x1, blocking collectives, shards(): weights = lax.all_gather(weights, 'x')  10.7 us
    ppermute x3, waiting for transfers between devices, to_peers(): lax.ppermute(blocks(lax.rem(me + k, n)), axis, [(i, (i + k) % n) for i in...  10.2 us
  transfers between devices with their start and end apart: 28, of which 12 were waited for; matrix products, arithmetic and copies ran while one was open for 7% of the time, Pallas kernels for 0%

profile of v3, /device:TPU:11, one launch (start us, length us, event | category | flops | bytes accessed | tf_op | source)
XLA Modules:
  0.0 272.0 jit_solution(6605262356979458750)
XLA Ops:
  12.1 8.3 %all-to-all-start = ((bf16[16,6,128]{2,1,0:T(8,128)(2,1)}), bf16[16,6,128]{2,1,0:T(8,128)(2,1)S(1)}, u32[]{:S(2)}, u32[]{:S(2)}) async-start(bf16[16,6,128]{2,1,0:T(8,128)(2,1)} %reshape.371), calls=%async_computation | async-start | bytes 65536 | tf_op jit(solution)/shard_map/all_to_all | solution.py:18
  28.2 4.0 %collective-permute-start.2 = (bf16[640,128]{1,0:T(8,128)(2,1)S(1)}, bf16[640,128]{1,0:T(8,128)(2,1)S(1)}, u32[]{:S(2)}, u32[]{:S(2)}) collective-permute-start(bf16[640,128]{1,0:T(8,128)(2,1)S(1)} %get-tuple-element.39), channel_id=1, source_target_pairs={{0,24},{8,0},{16,8},{24,16},{1,25},{9,1},{17,9},{25,17},{2,26},{10... | collective-permute-start | bytes 491528 | tf_op jit(solution)/shard_map/ppermute | solution.py:127
  33.9 3.7 %collective-permute-done.2 = bf16[640,128]{1,0:T(8,128)(2,1)S(1)} collective-permute-done((bf16[640,128]{1,0:T(8,128)(2,1)S(1)}, bf16[640,128]{1,0:T(8,128)(2,1)S(1)}, u32[]{:S(2)}, u32[]{:S(2)}) %collective-permute-start.2) | collective-permute-done | bytes 163872 | tf_op jit(solution)/shard_map/ppermute | solution.py:127
  39.1 13.9 %all-to-all-start.2 = ((bf16[8,128,128]{2,1,0:T(8,128)(2,1)}), bf16[8,128,128]{2,1,0:T(8,128)(2,1)S(1)}, u32[]{:S(2)}, u32[]{:S(2)}) async-start(bf16[8,128,128]{2,1,0:T(8,128)(2,1)} %pad_maximum_fusion.4), calls=%async_computation.2 | async-start | bytes 524288 | tf_op jit(solution)/shard_map/all_to_all | solution.py:18
  55.6 3.7 %collective-permute-start.4 = (bf16[192,1024]{1,0:T(8,128)(2,1)}, bf16[192,1024]{1,0:T(8,128)(2,1)S(1)}, u32[]{:S(2)}, u32[]{:S(2)}) collective-permute-start(bf16[192,1024]{1,0:T(8,128)(2,1)} %convolution_convert_fusion.3), channel_id=1, source_target_pairs={{0,64},{32,96},{64,0},{96,32},{1,65},{33,97},{65,1},{97,33},{2,66}... | collective-permute-start | bytes 1179656 | tf_op jit(solution)/shard_map/ppermute | solution.py:161
  62.3 3.3 %collective-permute-start.5 = (bf16[192,1024]{1,0:T(8,128)(2,1)}, bf16[192,1024]{1,0:T(8,128)(2,1)S(1)}, u32[]{:S(2)}, u32[]{:S(2)}) collective-permute-start(bf16[192,1024]{1,0:T(8,128)(2,1)} %convolution_convert_fusion.2), channel_id=1, source_target_pairs={{0,96},{32,0},{64,32},{96,64},{1,97},{33,1},{65,33},{97,65},{2,98}... | collective-permute-start | bytes 1179656 | tf_op jit(solution)/shard_map/ppermute | solution.py:161
  69.9 8.4 %collective-permute-done.3 = bf16[192,1024]{1,0:T(8,128)(2,1)S(1)} collective-permute-done((bf16[192,1024]{1,0:T(8,128)(2,1)}, bf16[192,1024]{1,0:T(8,128)(2,1)S(1)}, u32[]{:S(2)}, u32[]{:S(2)}) %collective-permute-start.3) | collective-permute-done | bytes 393248 | tf_op jit(solution)/shard_map/ppermute | solution.py:161
  79.8 4.3 %all-to-all-start.1 = ((bf16[4,48,1024]{2,1,0:T(8,128)(2,1)}), bf16[4,48,1024]{2,1,0:T(8,128)(2,1)S(1)}, u32[]{:S(2)}, u32[]{:S(2)}) async-start(bf16[4,48,1024]{2,1,0:T(8,128)(2,1)} %bitcast.23), calls=%async_computation.1 | async-start | bytes 786432 | tf_op jit(solution)/shard_map/all_to_all | solution.py:18
  86.2 3.4 %collective-permute-start.7 = (bf16[48,1024]{1,0:T(8,128)(2,1)S(1)}, bf16[48,1024]{1,0:T(8,128)(2,1)S(1)}, u32[]{:S(2)}, u32[]{:S(2)}) collective-permute-start(bf16[48,1024]{1,0:T(8,128)(2,1)S(1)} %copy_bitcast_fusion), channel_id=1, source_target_pairs={{0,16},{8,24},{16,0},{24,8},{1,17},{9,25},{17,1},{25,9},{2,18},{10... | collective-permute-start | bytes 294920 | tf_op jit(solution)/shard_map/ppermute | solution.py:41
  89.6 3.9 %collective-permute-start.6 = (bf16[48,1024]{1,0:T(8,128)(2,1)S(1)}, bf16[48,1024]{1,0:T(8,128)(2,1)S(1)}, u32[]{:S(2)}, u32[]{:S(2)}) collective-permute-start(bf16[48,1024]{1,0:T(8,128)(2,1)S(1)} %copy_bitcast_fusion), channel_id=1, source_target_pairs={{0,8},{8,16},{16,24},{24,0},{1,9},{9,17},{17,25},{25,1},{2,10},{10... | collective-permute-start | bytes 294920 | tf_op jit(solution)/shard_map/ppermute | solution.py:41
  93.7 10.7 %all_gather.6 = bf16[4,80,1024]{2,1,0:T(8,128)(2,1)S(1)} all-gather(bf16[1,80,1024]{2,1,0:T(8,128)(2,1)S(1)} %all_gather_reshape.3), channel_id=1, replica_groups=mesh['zl'=4,'x'=4,'y'=4,'zh'=4,'c'=2] {'x'}, dimensions={0}, use_global_device_ids=true | all-gather | bytes 819200 | tf_op jit(solution)/shard_map/all_gather | solution.py:171
  112.1 4.0 %collective-permute-start.9 = (bf16[48,256]{1,0:T(8,128)(2,1)S(1)}, bf16[48,256]{1,0:T(8,128)(2,1)S(1)}, u32[]{:S(2)}, u32[]{:S(2)}) collective-permute-start(bf16[48,256]{1,0:T(8,128)(2,1)S(1)} %get-tuple-element.46), channel_id=1, source_target_pairs={{0,8},{8,16},{16,24},{24,0},{1,9},{9,17},{17,25},{25,1},{2,10},{10... | collective-permute-start | bytes 73736 | tf_op jit(solution)/shard_map/ppermute | solution.py:177
  119.9 17.5 %all-to-all-start.3 = ((bf16[8,88,128]{2,1,0:T(8,128)(2,1)}), bf16[8,88,128]{2,1,0:T(8,128)(2,1)S(1)}, u32[]{:S(2)}, u32[]{:S(2)}) async-start(bf16[8,88,128]{2,1,0:T(8,128)(2,1)} %broadcast_in_dim.121), calls=%async_computation.3 | async-start | bytes 360448 | tf_op jit(solution)/shard_map/all_to_all | solution.py:18
  137.5 16.4 %all-to-all-done.3 = bf16[8,88,128]{2,1,0:T(8,128)(2,1)S(1)} async-done(((bf16[8,88,128]{2,1,0:T(8,128)(2,1)}), bf16[8,88,128]{2,1,0:T(8,128)(2,1)S(1)}, u32[]{:S(2)}, u32[]{:S(2)}) %all-to-all-start.3) | async-done | bytes 180256 | tf_op jit(solution)/shard_map/all_to_all | solution.py:18
  159.6 3.8 %collective-permute-start.12 = (bf16[80,1024]{1,0:T(8,128)(2,1)S(1)}, bf16[80,1024]{1,0:T(8,128)(2,1)S(1)}, u32[]{:S(2)}, u32[]{:S(2)}) collective-permute-start(bf16[80,1024]{1,0:T(8,128)(2,1)S(1)} %get-tuple-element.41), channel_id=1, source_target_pairs={{0,128},{128,256},{256,384},{384,0},{1,129},{129,257},{257,385},{3... | collective-permute-start | bytes 491528 | tf_op jit(solution)/shard_map/ppermute | solution.py:47
  163.4 3.3 %collective-permute-start.14 = (bf16[80,1024]{1,0:T(8,128)(2,1)S(1)}, bf16[80,1024]{1,0:T(8,128)(2,1)S(1)}, u32[]{:S(2)}, u32[]{:S(2)}) collective-permute-start(bf16[80,1024]{1,0:T(8,128)(2,1)S(1)} %get-tuple-element.42), channel_id=1, source_target_pairs={{0,384},{128,0},{256,128},{384,256},{1,385},{129,1},{257,129},{385... | collective-permute-start | bytes 491528 | tf_op jit(solution)/shard_map/ppermute | solution.py:47
  169.8 9.3 %collective-permute-done.13 = bf16[80,1024]{1,0:T(8,128)(2,1)S(1)} collective-permute-done((bf16[80,1024]{1,0:T(8,128)(2,1)S(1)}, bf16[80,1024]{1,0:T(8,128)(2,1)S(1)}, u32[]{:S(2)}, u32[]{:S(2)}) %collective-permute-start.13) | collective-permute-done | bytes 163872 | tf_op jit(solution)/shard_map/ppermute | solution.py:47
  180.7 6.1 %all-to-all-start.4 = ((bf16[4,200,1024]{2,1,0:T(8,128)(2,1)}), bf16[4,200,1024]{2,1,0:T(8,128)(2,1)S(1)}, u32[]{:S(2)}, u32[]{:S(2)}) async-start(bf16[4,200,1024]{2,1,0:T(8,128)(2,1)} %pad_maximum_fusion), calls=%async_computation.4 | async-start | bytes 3276800 | tf_op jit(solution)/shard_map/all_to_all | solution.py:18
  187.5 18.1 %all-to-all-done.4 = bf16[4,200,1024]{2,1,0:T(8,128)(2,1)S(1)} async-done(((bf16[4,200,1024]{2,1,0:T(8,128)(2,1)}), bf16[4,200,1024]{2,1,0:T(8,128)(2,1)S(1)}, u32[]{:S(2)}, u32[]{:S(2)}) %all-to-all-start.4) | async-done | bytes 1638432 | tf_op jit(solution)/shard_map/all_to_all | solution.py:18
  208.4 6.5 %all-to-all-start.5 = ((bf16[4,88,1024]{2,1,0:T(8,128)(2,1)}), bf16[4,88,1024]{2,1,0:T(8,128)(2,1)S(1)}, u32[]{:S(2)}, u32[]{:S(2)}) async-start(bf16[4,88,1024]{2,1,0:T(8,128)(2,1)} %pad_maximum_fusion.2), calls=%async_computation.5 | async-start | bytes 1441792 | tf_op jit(solution)/shard_map/all_to_all | solution.py:18
  214.9 21.7 %reduce-scatter.5.cloned.1.call-done = bf16[304,128]{1,0:T(8,128)(2,1)} async-done(((bf16[2432,128]{1,0:T(8,128)(2,1)}), bf16[304,128]{1,0:T(8,128)(2,1)}) %reduce-scatter.5.cloned.1.call-update) | async-done | bytes 77840 | tf_op jit(solution)/shard_map/reduce_scatter | solution.py:212
  238.9 6.7 %all-to-all-start.6 = ((f32[16,42,128]{2,1,0:T(8,128)}), f32[16,42,128]{2,1,0:T(8,128)S(1)}, u32[]{:S(2)}, u32[]{:S(2)}) async-start(f32[16,42,128]{2,1,0:T(8,128)} %pad_maximum_fusion.3), calls=%async_computation.7 | async-start | bytes 786432 | tf_op jit(solution)/shard_map/all_to_all | solution.py:18
  251.8 3.7 %collective-permute-start.17 = (bf16[80,1024]{1,0:T(8,128)(2,1)S(1)}, bf16[80,1024]{1,0:T(8,128)(2,1)S(1)}, u32[]{:S(2)}, u32[]{:S(2)}) collective-permute-start(bf16[80,1024]{1,0:T(8,128)(2,1)S(1)} %get-tuple-element.16), channel_id=1, source_target_pairs={{0,24},{8,0},{16,8},{24,16},{1,25},{9,1},{17,9},{25,17},{2,26},{10... | collective-permute-start | bytes 491528 | tf_op jit(solution)/shard_map/ppermute | solution.py:41
  258.4 3.7 %collective-permute-done.17 = bf16[80,1024]{1,0:T(8,128)(2,1)S(1)} collective-permute-done((bf16[80,1024]{1,0:T(8,128)(2,1)S(1)}, bf16[80,1024]{1,0:T(8,128)(2,1)S(1)}, u32[]{:S(2)}, u32[]{:S(2)}) %collective-permute-start.17) | collective-permute-done | bytes 163872 | tf_op jit(solution)/shard_map/ppermute | solution.py:41
  (196 shorter events, 66.5 us)
Async XLA Ops:
  12.1 21.5 %all-to-all-start = ((bf16[16,6,128]{2,1,0:T(8,128)(2,1)}), bf16[16,6,128]{2,1,0:T(8,128)(2,1)S(1)}, u32[]{:S(2)}, u32[]{:S(2)}) async-start(bf16[16,6,128]{2,1,0:T(8,128)(2,1)} %reshape.371), calls=%async_computation | async-start | bytes 65536 | tf_op jit(solution)/shard_map/all_to_all | solution.py:18
  22.3 11.5 %collective-permute-start = (bf16[640,128]{1,0:T(8,128)(2,1)S(1)}, bf16[640,128]{1,0:T(8,128)(2,1)S(1)}, u32[]{:S(2)}, u32[]{:S(2)}) collective-permute-start(bf16[640,128]{1,0:T(8,128)(2,1)S(1)} %get-tuple-element.37), channel_id=1, source_target_pairs={{0,8},{8,16},{16,24},{24,0},{1,9},{9,17},{17,25},{25,1},{2,10},{10... | collective-permute-start | bytes 491528 | tf_op jit(solution)/shard_map/ppermute | solution.py:127
  28.2 9.4 %collective-permute-start.2 = (bf16[640,128]{1,0:T(8,128)(2,1)S(1)}, bf16[640,128]{1,0:T(8,128)(2,1)S(1)}, u32[]{:S(2)}, u32[]{:S(2)}) collective-permute-start(bf16[640,128]{1,0:T(8,128)(2,1)S(1)} %get-tuple-element.39), channel_id=1, source_target_pairs={{0,24},{8,0},{16,8},{24,16},{1,25},{9,1},{17,9},{25,17},{2,26},{10... | collective-permute-start | bytes 491528 | tf_op jit(solution)/shard_map/ppermute | solution.py:127
  39.1 40.8 %all-to-all-start.2 = ((bf16[8,128,128]{2,1,0:T(8,128)(2,1)}), bf16[8,128,128]{2,1,0:T(8,128)(2,1)S(1)}, u32[]{:S(2)}, u32[]{:S(2)}) async-start(bf16[8,128,128]{2,1,0:T(8,128)(2,1)} %pad_maximum_fusion.4), calls=%async_computation.2 | async-start | bytes 524288 | tf_op jit(solution)/shard_map/all_to_all | solution.py:18
  53.0 65.5 %reduce-scatter.7.cloned.1.call-start = ((), (), s32[]{:S(2)}) async-start(), calls=%async_computation.11 | async-start | bytes 73728 | tf_op jit(solution)/shard_map/reduce_scatter | solution.py:148
  55.6 14.3 %collective-permute-start.4 = (bf16[192,1024]{1,0:T(8,128)(2,1)}, bf16[192,1024]{1,0:T(8,128)(2,1)S(1)}, u32[]{:S(2)}, u32[]{:S(2)}) collective-permute-start(bf16[192,1024]{1,0:T(8,128)(2,1)} %convolution_convert_fusion.3), channel_id=1, source_target_pairs={{0,64},{32,96},{64,0},{96,32},{1,65},{33,97},{65,1},{97,33},{2,66}... | collective-permute-start | bytes 1179656 | tf_op jit(solution)/shard_map/ppermute | solution.py:161
  59.3 19.1 %collective-permute-start.3 = (bf16[192,1024]{1,0:T(8,128)(2,1)}, bf16[192,1024]{1,0:T(8,128)(2,1)S(1)}, u32[]{:S(2)}, u32[]{:S(2)}) collective-permute-start(bf16[192,1024]{1,0:T(8,128)(2,1)} %convolution_convert_fusion.4), channel_id=1, source_target_pairs={{0,32},{32,64},{64,96},{96,0},{1,33},{33,65},{65,97},{97,1},{2,34}... | collective-permute-start | bytes 1179656 | tf_op jit(solution)/shard_map/ppermute | solution.py:161
  62.3 16.3 %collective-permute-start.5 = (bf16[192,1024]{1,0:T(8,128)(2,1)}, bf16[192,1024]{1,0:T(8,128)(2,1)S(1)}, u32[]{:S(2)}, u32[]{:S(2)}) collective-permute-start(bf16[192,1024]{1,0:T(8,128)(2,1)} %convolution_convert_fusion.2), channel_id=1, source_target_pairs={{0,96},{32,0},{64,32},{96,64},{1,97},{33,1},{65,33},{97,65},{2,98}... | collective-permute-start | bytes 1179656 | tf_op jit(solution)/shard_map/ppermute | solution.py:161
  79.8 37.5 %all-to-all-start.1 = ((bf16[4,48,1024]{2,1,0:T(8,128)(2,1)}), bf16[4,48,1024]{2,1,0:T(8,128)(2,1)S(1)}, u32[]{:S(2)}, u32[]{:S(2)}) async-start(bf16[4,48,1024]{2,1,0:T(8,128)(2,1)} %bitcast.23), calls=%async_computation.1 | async-start | bytes 786432 | tf_op jit(solution)/shard_map/all_to_all | solution.py:18
  84.1 71.4 %all-gather.2.cloned.1.call-start = ((), (), s32[]{:S(2)}) async-start(), calls=%async_computation.9 | async-start | bytes 2621440 | tf_op jit(solution)/shard_map/all_gather | solution.py:182
  84.1 21.3 %collective-permute-start.8 = (bf16[48,1024]{1,0:T(8,128)(2,1)S(1)}, bf16[48,1024]{1,0:T(8,128)(2,1)S(1)}, u32[]{:S(2)}, u32[]{:S(2)}) collective-permute-start(bf16[48,1024]{1,0:T(8,128)(2,1)S(1)} %copy_bitcast_fusion), channel_id=1, source_target_pairs={{0,24},{8,0},{16,8},{24,16},{1,25},{9,1},{17,9},{25,17},{2,26},{10... | collective-permute-start | bytes 294920 | tf_op jit(solution)/shard_map/ppermute | solution.py:41
  86.2 19.2 %collective-permute-start.7 = (bf16[48,1024]{1,0:T(8,128)(2,1)S(1)}, bf16[48,1024]{1,0:T(8,128)(2,1)S(1)}, u32[]{:S(2)}, u32[]{:S(2)}) collective-permute-start(bf16[48,1024]{1,0:T(8,128)(2,1)S(1)} %copy_bitcast_fusion), channel_id=1, source_target_pairs={{0,16},{8,24},{16,0},{24,8},{1,17},{9,25},{17,1},{25,9},{2,18},{10... | collective-permute-start | bytes 294920 | tf_op jit(solution)/shard_map/ppermute | solution.py:41
  89.6 15.8 %collective-permute-start.6 = (bf16[48,1024]{1,0:T(8,128)(2,1)S(1)}, bf16[48,1024]{1,0:T(8,128)(2,1)S(1)}, u32[]{:S(2)}, u32[]{:S(2)}) collective-permute-start(bf16[48,1024]{1,0:T(8,128)(2,1)S(1)} %copy_bitcast_fusion), channel_id=1, source_target_pairs={{0,8},{8,16},{16,24},{24,0},{1,9},{9,17},{17,25},{25,1},{2,10},{10... | collective-permute-start | bytes 294920 | tf_op jit(solution)/shard_map/ppermute | solution.py:41
  106.8 10.5 %collective-permute-start.11 = (bf16[48,256]{1,0:T(8,128)(2,1)S(1)}, bf16[48,256]{1,0:T(8,128)(2,1)S(1)}, u32[]{:S(2)}, u32[]{:S(2)}) collective-permute-start(bf16[48,256]{1,0:T(8,128)(2,1)S(1)} %get-tuple-element.44), channel_id=1, source_target_pairs={{0,24},{8,0},{16,8},{24,16},{1,25},{9,1},{17,9},{25,17},{2,26},{10... | collective-permute-start | bytes 73736 | tf_op jit(solution)/shard_map/ppermute | solution.py:177
  119.9 34.0 %all-to-all-start.3 = ((bf16[8,88,128]{2,1,0:T(8,128)(2,1)}), bf16[8,88,128]{2,1,0:T(8,128)(2,1)S(1)}, u32[]{:S(2)}, u32[]{:S(2)}) async-start(bf16[8,88,128]{2,1,0:T(8,128)(2,1)} %broadcast_in_dim.121), calls=%async_computation.3 | async-start | bytes 360448 | tf_op jit(solution)/shard_map/all_to_all | solution.py:18
  159.6 9.3 %collective-permute-start.12 = (bf16[80,1024]{1,0:T(8,128)(2,1)S(1)}, bf16[80,1024]{1,0:T(8,128)(2,1)S(1)}, u32[]{:S(2)}, u32[]{:S(2)}) collective-permute-start(bf16[80,1024]{1,0:T(8,128)(2,1)S(1)} %get-tuple-element.41), channel_id=1, source_target_pairs={{0,128},{128,256},{256,384},{384,0},{1,129},{129,257},{257,385},{3... | collective-permute-start | bytes 491528 | tf_op jit(solution)/shard_map/ppermute | solution.py:47
  166.7 12.4 %collective-permute-start.13 = (bf16[80,1024]{1,0:T(8,128)(2,1)S(1)}, bf16[80,1024]{1,0:T(8,128)(2,1)S(1)}, u32[]{:S(2)}, u32[]{:S(2)}) collective-permute-start(bf16[80,1024]{1,0:T(8,128)(2,1)S(1)} %get-tuple-element.43), channel_id=1, source_target_pairs={{0,256},{128,384},{256,0},{384,128},{1,257},{129,385},{257,1},{385... | collective-permute-start | bytes 491528 | tf_op jit(solution)/shard_map/ppermute | solution.py:47
  180.7 24.9 %all-to-all-start.4 = ((bf16[4,200,1024]{2,1,0:T(8,128)(2,1)}), bf16[4,200,1024]{2,1,0:T(8,128)(2,1)S(1)}, u32[]{:S(2)}, u32[]{:S(2)}) async-start(bf16[4,200,1024]{2,1,0:T(8,128)(2,1)} %pad_maximum_fusion), calls=%async_computation.4 | async-start | bytes 3276800 | tf_op jit(solution)/shard_map/all_to_all | solution.py:18
  186.8 49.8 %reduce-scatter.5.cloned.1.call-start = ((), (), s32[]{:S(2)}) async-start(), calls=%async_computation.10 | async-start | bytes 700416 | tf_op jit(solution)/shard_map/reduce_scatter | solution.py:212
  208.4 29.5 %all-to-all-start.5 = ((bf16[4,88,1024]{2,1,0:T(8,128)(2,1)}), bf16[4,88,1024]{2,1,0:T(8,128)(2,1)S(1)}, u32[]{:S(2)}, u32[]{:S(2)}) async-start(bf16[4,88,1024]{2,1,0:T(8,128)(2,1)} %pad_maximum_fusion.2), calls=%async_computation.5 | async-start | bytes 1441792 | tf_op jit(solution)/shard_map/all_to_all | solution.py:18
  238.9 23.2 %all-to-all-start.6 = ((f32[16,42,128]{2,1,0:T(8,128)}), f32[16,42,128]{2,1,0:T(8,128)S(1)}, u32[]{:S(2)}, u32[]{:S(2)}) async-start(f32[16,42,128]{2,1,0:T(8,128)} %pad_maximum_fusion.3), calls=%async_computation.7 | async-start | bytes 786432 | tf_op jit(solution)/shard_map/all_to_all | solution.py:18
  245.8 9.8 %collective-permute-start.15 = (bf16[80,1024]{1,0:T(8,128)(2,1)S(1)}, bf16[80,1024]{1,0:T(8,128)(2,1)S(1)}, u32[]{:S(2)}, u32[]{:S(2)}) collective-permute-start(bf16[80,1024]{1,0:T(8,128)(2,1)S(1)} %get-tuple-element.16), channel_id=1, source_target_pairs={{0,8},{8,16},{16,24},{24,0},{1,9},{9,17},{17,25},{25,1},{2,10},{10... | collective-permute-start | bytes 491528 | tf_op jit(solution)/shard_map/ppermute | solution.py:41
  249.0 9.4 %collective-permute-start.16 = (bf16[80,1024]{1,0:T(8,128)(2,1)S(1)}, bf16[80,1024]{1,0:T(8,128)(2,1)S(1)}, u32[]{:S(2)}, u32[]{:S(2)}) collective-permute-start(bf16[80,1024]{1,0:T(8,128)(2,1)S(1)} %get-tuple-element.16), channel_id=1, source_target_pairs={{0,16},{8,24},{16,0},{24,8},{1,17},{9,25},{17,1},{25,9},{2,18},{10... | collective-permute-start | bytes 491528 | tf_op jit(solution)/shard_map/ppermute | solution.py:41
  251.8 10.2 %collective-permute-start.17 = (bf16[80,1024]{1,0:T(8,128)(2,1)S(1)}, bf16[80,1024]{1,0:T(8,128)(2,1)S(1)}, u32[]{:S(2)}, u32[]{:S(2)}) collective-permute-start(bf16[80,1024]{1,0:T(8,128)(2,1)S(1)} %get-tuple-element.16), channel_id=1, source_target_pairs={{0,24},{8,0},{16,8},{24,16},{1,25},{9,1},{17,9},{25,17},{2,26},{10... | collective-permute-start | bytes 491528 | tf_op jit(solution)/shard_map/ppermute | solution.py:41
  (17 other events, 253.8 us)
Sparse Core Ops, SparseCore 0:
  66.8 50.3 reduce-scatter.6
  190.7 45.8 reduce-scatter.4
Sparse Core Ops, SparseCore 1:
  105.3 41.6 all-gather.1

commit v4 on v3

--- a/solution.py
+++ b/solution.py
@@ -39,6 +39,11 @@
 def from_peers(x, axis):
     n = lax.axis_size(axis)
     return [x] + [lax.ppermute(x, axis, [(i, (i + k) % n) for i in range(n)]) for k in range(1, n)]
+
+
+def in_order(blocks, axis):
+    n, me = lax.axis_size(axis), lax.axis_index(axis)
+    return jnp.stack([lax.dynamic_index_in_dim(blocks, lax.rem(me - j + n, n), 0, False) for j in range(n)])
 
 
 def to_peers(blocks, axis):
@@ -85,6 +90,10 @@
     rows = toks + n_frames
     gain = lax.dynamic_slice_in_dim(gain_all, tp_index * width, width, 0)
 
+    by_x = jnp.moveaxis(frames.reshape(nzl, nx, n_frames, frames.shape[1]), 1, 0)
+    partial = dot(by_x.reshape(frames.shape), projector, 1, 0).astype(bf16)
+    x_sum = lax.psum_scatter(partial, "x", scatter_dimension=0, tiled=True)
+
     own_sizes = pick_entry(clip_len[0], grp_index, 0)
     before = lax.broadcasted_iota(jnp.int32, (ng, ng), 1) < lax.broadcasted_iota(jnp.int32, (ng, ng), 0)
     own_starts = jnp.sum(jnp.where(before, own_sizes[None, :], 0), axis=1)
@@ -144,27 +153,12 @@
         ],
         axis=1,
     )
-    sent, pair, frames_in = lax.optimization_barrier((sent, pair, frames))
     pair = lax.psum_scatter(pair, TP, scatter_dimension=0, tiled=True)
     sq_text = dot(jnp.ones((8, width), bf16), (text_wide * text_wide).astype(bf16), 1, 1)[0]
 
     came = exchange(sent, TP)
-
-    by_x = frames_in.reshape(nzl, nx, n_frames, frames.shape[1])
-
-    def block_for(k):
-        part = lax.dynamic_index_in_dim(by_x, lax.rem(x_index + k, nx), 1, False)
-        part = part.reshape(nzl * n_frames, frames.shape[1])
-        return dot(part, projector, 1, 0).astype(bf16)
-
-    x_parts = [
-        lax.ppermute(block_for(k), "x", [(i, (i + k) % nx) for i in range(nx)]) for k in range(1, nx)
-    ]
-    x_sum = block_for(0).astype(f32)
-    for part in x_parts:
-        x_sum = x_sum + part.astype(f32)
-
     at = piece + up_rows
+
     grad_full = jnp.moveaxis(came[:, at:], 0, 1).reshape(n_frames, nt * cols)
     grad_all = jnp.concatenate(from_peers(grad_full, "y"), axis=0)
     weights = jnp.moveaxis(came[:, :at], 0, 1).reshape(at, nt * cols)
@@ -173,15 +167,12 @@
     weights = weights[:, :piece].reshape(nx * piece, nt * cols)
     lora_frames = (adapter_scale * dot(grad_full, up_full, 1, 1)).astype(bf16)
     spread = dot(grad_all, weights, 1, 1).astype(bf16).reshape(ny, n_frames, nx * piece)
-    parts = [spread[0]] + [
-        lax.ppermute(spread[k], "y", [(i, (i - k) % ny) for i in range(ny)]) for k in range(1, ny)
-    ]
-    parts = [parts[0]] + parts[:0:-1]
-    grad_norm = placed([p.astype(f32) for p in parts], 1, "y")
+    back = jnp.moveaxis(exchange(in_order(spread, "y"), "y"), 0, 1)
+    grad_norm = back.reshape(n_frames, width).astype(f32)
     grad_norm = grad_norm + dot(lora_frames, down_t, 1, 0)
     weights = lax.all_gather(weights, "y", axis=0, tiled=True)
 
-    blocks = exchange(x_sum.astype(bf16).reshape(nzl, n_frames, width), "zl")
+    blocks = exchange(x_sum.reshape(nzl, n_frames, width), "zl")
     embedded = jnp.sum(blocks.astype(f32), axis=0).astype(bf16)
     wide = embedded.astype(f32)
     scaled = wide * gain[None, :]
@@ -233,13 +224,13 @@
     adapters = jnp.sum(came[:, nzl * n_frames :].astype(f32), axis=0).astype(bf16)
     all_grad = came[:, : nzl * n_frames].reshape(nx, nzl, n_frames, width)
     all_grad = jnp.moveaxis(all_grad, 0, 1).reshape(ng * n_frames, width)
-    proj_part = dot(frames, all_grad, 0, 0).astype(bf16)
+    proj_part = after(dot(frames, all_grad, 0, 0), summed).astype(bf16)
     part = frames.shape[1] // ny
     came = exchange(
         jnp.concatenate([proj_part.reshape(ny, part, width), copies(adapters, ny)], axis=1), "y"
     )
     came = jnp.sum(came.astype(f32), axis=0)
-    projector_grad = placed([b.astype(f32) for b in from_peers(came[:part].astype(bf16), "y")], 0, "y")
+    projector_grad = lax.all_gather(came[:part].astype(bf16), "y", axis=0, tiled=True).astype(f32)
 
     n_d = k * width // cols
     own = jnp.concatenate([came[part : part + k].reshape(n_d, cols), came[part + k :, :cols]], axis=0)

time: 274 us -> 263 us (0.960)
  the two profiles are of different devices: /device:TPU:11 before, /device:TPU:2 now
where the time goes in v4:
time: 263 us; the launch traced here: 261 us
  waiting for transfers between devices  92.7 us (35%)
  starting transfers between devices  76.4 us (29%)
  blocking collectives  36.9 us (14%)
  between operations  17.8 us (7%)
  local copies, waits for them, and re-layouts  15.9 us (6%)
  matrix products  11.2 us (4%)
  other arithmetic  10.2 us (4%)
    all_to_all x7, waiting for transfers between devices, exchange(): return lax.all_to_all(blocks, axis, split_axis=0, concat_axis=0, tiled=True)  50.8 us
    all_to_all x7, starting transfers between devices, exchange(): return lax.all_to_all(blocks, axis, split_axis=0, concat_axis=0, tiled=True)  44.4 us
    reduce_scatter x1, waiting for transfers between devices, shards(): summed = lax.psum_scatter(base, TP, scatter_dimension=0, tiled=True)  24.6 us
    all_gather x1, blocking collectives, shards(): weights = lax.all_gather(weights, 'x')  13.7 us
    all_gather x1, blocking collectives, shards(): lax.all_gather(came[:part].astype(bf16), 'y', axis=0, tiled=True)  13.6 us
    ppermute x3, starting transfers between devices, shards(): lax.ppermute(for_y(k), 'y', [(i, (i + k) % ny) for i in range(ny)])  11.3 us
    dot_general x17, matrix products, dot(): lax.dot_general(a, b, (((ca,), (cb,)), ((), ())), preferred_element_type=...  11.2 us
    ppermute x3, starting transfers between devices, to_peers(): lax.ppermute(blocks(lax.rem(me + k, n)), axis, [(i, (i + k) % n) for i in...  11.1 us
  transfers between devices with their start and end apart: 20, of which 10 were waited for; matrix products, arithmetic and copies ran while one was open for 8% of the time, Pallas kernels for 0%

profile of v4, /device:TPU:2, one launch (start us, length us, event | category | flops | bytes accessed | tf_op | source)
XLA Modules:
  0.0 261.0 jit_solution(14950981675727070515)
XLA Ops:
  12.1 9.2 %all-to-all-start.1 = ((bf16[16,6,128]{2,1,0:T(8,128)(2,1)}), bf16[16,6,128]{2,1,0:T(8,128)(2,1)S(1)}, u32[]{:S(2)}, u32[]{:S(2)}) async-start(bf16[16,6,128]{2,1,0:T(8,128)(2,1)} %reshape.364), calls=%async_computation.2 | async-start | bytes 65536 | tf_op jit(solution)/shard_map/all_to_all | solution.py:18
  23.3 3.2 %collective-permute-start = (bf16[640,128]{1,0:T(8,128)(2,1)S(1)}, bf16[640,128]{1,0:T(8,128)(2,1)S(1)}, u32[]{:S(2)}, u32[]{:S(2)}) collective-permute-start(bf16[640,128]{1,0:T(8,128)(2,1)S(1)} %get-tuple-element.25), channel_id=1, source_target_pairs={{0,8},{8,16},{16,24},{24,0},{1,9},{9,17},{17,25},{25,1},{2,10},{10... | collective-permute-start | bytes 491528 | tf_op jit(solution)/shard_map/ppermute | solution.py:136
  26.5 4.8 %collective-permute-start.1 = (bf16[640,128]{1,0:T(8,128)(2,1)S(1)}, bf16[640,128]{1,0:T(8,128)(2,1)S(1)}, u32[]{:S(2)}, u32[]{:S(2)}) collective-permute-start(bf16[640,128]{1,0:T(8,128)(2,1)S(1)} %get-tuple-element.26), channel_id=1, source_target_pairs={{0,16},{8,24},{16,0},{24,8},{1,17},{9,25},{17,1},{25,9},{2,18},{10... | collective-permute-start | bytes 491528 | tf_op jit(solution)/shard_map/ppermute | solution.py:136
  31.3 3.3 %collective-permute-start.2 = (bf16[640,128]{1,0:T(8,128)(2,1)S(1)}, bf16[640,128]{1,0:T(8,128)(2,1)S(1)}, u32[]{:S(2)}, u32[]{:S(2)}) collective-permute-start(bf16[640,128]{1,0:T(8,128)(2,1)S(1)} %get-tuple-element.27), channel_id=1, source_target_pairs={{0,24},{8,0},{16,8},{24,16},{1,25},{9,1},{17,9},{25,17},{2,26},{10... | collective-permute-start | bytes 491528 | tf_op jit(solution)/shard_map/ppermute | solution.py:136
  39.6 12.4 %all-to-all-start.2 = ((bf16[8,128,128]{2,1,0:T(8,128)(2,1)}), bf16[8,128,128]{2,1,0:T(8,128)(2,1)S(1)}, u32[]{:S(2)}, u32[]{:S(2)}) async-start(bf16[8,128,128]{2,1,0:T(8,128)(2,1)} %pad_maximum_fusion.5), calls=%async_computation.3 | async-start | bytes 524288 | tf_op jit(solution)/shard_map/all_to_all | solution.py:18
  54.4 20.8 %all-to-all-done.2 = bf16[8,128,128]{2,1,0:T(8,128)(2,1)S(1)} async-done(((bf16[8,128,128]{2,1,0:T(8,128)(2,1)}), bf16[8,128,128]{2,1,0:T(8,128)(2,1)S(1)}, u32[]{:S(2)}, u32[]{:S(2)}) %all-to-all-start.2) | async-done | bytes 262176 | tf_op jit(solution)/shard_map/all_to_all | solution.py:18
  75.3 13.7 %all_gather.9 = bf16[4,80,1024]{2,1,0:T(8,128)(2,1)S(1)} all-gather(bf16[1,80,1024]{2,1,0:T(8,128)(2,1)S(1)} %all_gather_reshape.3), channel_id=1, replica_groups=mesh['zl'=4,'x'=4,'y'=4,'zh'=4,'c'=2] {'x'}, dimensions={0}, use_global_device_ids=true | all-gather | bytes 819200 | tf_op jit(solution)/shard_map/all_gather | solution.py:165
  89.9 4.5 %collective-permute-start.5 = (bf16[48,1024]{1,0:T(8,128)(2,1)S(1)}, bf16[48,1024]{1,0:T(8,128)(2,1)S(1)}, u32[]{:S(2)}, u32[]{:S(2)}) collective-permute-start(bf16[48,1024]{1,0:T(8,128)(2,1)S(1)} %copy_bitcast_fusion), channel_id=1, source_target_pairs={{0,24},{8,0},{16,8},{24,16},{1,25},{9,1},{17,9},{25,17},{2,26},{10... | collective-permute-start | bytes 294920 | tf_op jit(solution)/shard_map/ppermute | solution.py:41
  94.4 3.0 %collective-permute-start.4 = (bf16[48,1024]{1,0:T(8,128)(2,1)S(1)}, bf16[48,1024]{1,0:T(8,128)(2,1)S(1)}, u32[]{:S(2)}, u32[]{:S(2)}) collective-permute-start(bf16[48,1024]{1,0:T(8,128)(2,1)S(1)} %copy_bitcast_fusion), channel_id=1, source_target_pairs={{0,16},{8,24},{16,0},{24,8},{1,17},{9,25},{17,1},{25,9},{2,18},{10... | collective-permute-start | bytes 294920 | tf_op jit(solution)/shard_map/ppermute | solution.py:41
  102.4 4.5 %collective-permute-done.3 = bf16[48,1024]{1,0:T(8,128)(2,1)S(1)} collective-permute-done((bf16[48,1024]{1,0:T(8,128)(2,1)S(1)}, bf16[48,1024]{1,0:T(8,128)(2,1)S(1)}, u32[]{:S(2)}, u32[]{:S(2)}) %collective-permute-start.3) | collective-permute-done | bytes 98336 | tf_op jit(solution)/shard_map/ppermute | solution.py:41
  108.4 9.6 %all_to_all.40 = bf16[4,48,256]{2,1,0:T(8,128)(2,1)S(1)} all-to-all(bf16[4,48,256]{2,1,0:T(8,128)(2,1)S(1)} %pad_maximum_fusion.14), channel_id=1, replica_groups=mesh['zl'=4,'x'=4,'y'=4,'zh'=4,'c'=2] {'y'}, dimensions={0} | all-to-all | bytes 196608 | tf_op jit(solution)/shard_map/all_to_all | solution.py:18
  118.0 3.5 %all-to-all-start = ((bf16[4,48,1024]{2,1,0:T(8,128)(2,1)}), bf16[4,48,1024]{2,1,0:T(8,128)(2,1)S(1)}, u32[]{:S(2)}, u32[]{:S(2)}) async-start(bf16[4,48,1024]{2,1,0:T(8,128)(2,1)} %bitcast.171), calls=%async_computation.1 | async-start | bytes 786432 | tf_op jit(solution)/shard_map/all_to_all | solution.py:18
  122.0 8.4 %all-to-all-done = bf16[4,48,1024]{2,1,0:T(8,128)(2,1)S(1)} async-done(((bf16[4,48,1024]{2,1,0:T(8,128)(2,1)}), bf16[4,48,1024]{2,1,0:T(8,128)(2,1)S(1)}, u32[]{:S(2)}, u32[]{:S(2)}) %all-to-all-start) | async-done | bytes 393248 | tf_op jit(solution)/shard_map/all_to_all | solution.py:18
  132.9 4.0 %all-to-all-start.4 = ((bf16[8,88,128]{2,1,0:T(8,128)(2,1)}), bf16[8,88,128]{2,1,0:T(8,128)(2,1)}, u32[]{:S(2)}, u32[]{:S(2)}) async-start(bf16[8,88,128]{2,1,0:T(8,128)(2,1)} %broadcast_in_dim.114), calls=%async_computation.5 | async-start | bytes 360448 | tf_op jit(solution)/shard_map/all_to_all | solution.py:18
  141.0 11.7 %all-to-all-done.4 = bf16[8,88,128]{2,1,0:T(8,128)(2,1)} async-done(((bf16[8,88,128]{2,1,0:T(8,128)(2,1)}), bf16[8,88,128]{2,1,0:T(8,128)(2,1)}, u32[]{:S(2)}, u32[]{:S(2)}) %all-to-all-start.4) | async-done | bytes 180256 | tf_op jit(solution)/shard_map/all_to_all | solution.py:18
  158.6 5.4 %collective-permute-start.6 = (bf16[80,1024]{1,0:T(8,128)(2,1)S(1)}, bf16[80,1024]{1,0:T(8,128)(2,1)S(1)}, u32[]{:S(2)}, u32[]{:S(2)}) collective-permute-start(bf16[80,1024]{1,0:T(8,128)(2,1)S(1)} %get-tuple-element.29), channel_id=1, source_target_pairs={{0,128},{128,256},{256,384},{384,0},{1,129},{129,257},{257,385},{3... | collective-permute-start | bytes 491528 | tf_op jit(solution)/shard_map/ppermute | solution.py:52
  166.3 3.5 %collective-permute-start.7 = (bf16[80,1024]{1,0:T(8,128)(2,1)S(1)}, bf16[80,1024]{1,0:T(8,128)(2,1)S(1)}, u32[]{:S(2)}, u32[]{:S(2)}) collective-permute-start(bf16[80,1024]{1,0:T(8,128)(2,1)S(1)} %get-tuple-element.31), channel_id=1, source_target_pairs={{0,256},{128,384},{256,0},{384,128},{1,257},{129,385},{257,1},{385... | collective-permute-start | bytes 491528 | tf_op jit(solution)/shard_map/ppermute | solution.py:52
  172.2 6.8 %collective-permute-done.7 = bf16[80,1024]{1,0:T(8,128)(2,1)S(1)} collective-permute-done((bf16[80,1024]{1,0:T(8,128)(2,1)S(1)}, bf16[80,1024]{1,0:T(8,128)(2,1)S(1)}, u32[]{:S(2)}, u32[]{:S(2)}) %collective-permute-start.7) | collective-permute-done | bytes 163872 | tf_op jit(solution)/shard_map/ppermute | solution.py:52
  180.6 4.5 %all-to-all-start.5 = ((bf16[4,200,1024]{2,1,0:T(8,128)(2,1)}), bf16[4,200,1024]{2,1,0:T(8,128)(2,1)S(1)}, u32[]{:S(2)}, u32[]{:S(2)}) async-start(bf16[4,200,1024]{2,1,0:T(8,128)(2,1)} %pad_maximum_fusion), calls=%async_computation.6 | async-start | bytes 3276800 | tf_op jit(solution)/shard_map/all_to_all | solution.py:18
  185.1 24.6 %reduce-scatter.8.cloned.1.call-done = bf16[304,128]{1,0:T(8,128)(2,1)} async-done(((bf16[2432,128]{1,0:T(8,128)(2,1)}), bf16[304,128]{1,0:T(8,128)(2,1)}) %reduce-scatter.8.cloned.1.call-update) | async-done | bytes 77840 | tf_op jit(solution)/shard_map/reduce_scatter | solution.py:203
  214.4 4.2 %all-to-all-start.6 = ((bf16[4,88,1024]{2,1,0:T(8,128)(2,1)}), bf16[4,88,1024]{2,1,0:T(8,128)(2,1)S(1)}, u32[]{:S(2)}, u32[]{:S(2)}) async-start(bf16[4,88,1024]{2,1,0:T(8,128)(2,1)} %pad_maximum_fusion.2), calls=%async_computation.8 | async-start | bytes 1441792 | tf_op jit(solution)/shard_map/all_to_all | solution.py:18
  219.1 9.9 %all-to-all-done.6 = bf16[4,88,1024]{2,1,0:T(8,128)(2,1)S(1)} async-done(((bf16[4,88,1024]{2,1,0:T(8,128)(2,1)}), bf16[4,88,1024]{2,1,0:T(8,128)(2,1)S(1)}, u32[]{:S(2)}, u32[]{:S(2)}) %all-to-all-start.6) | async-done | bytes 720928 | tf_op jit(solution)/shard_map/all_to_all | solution.py:18
  230.0 6.7 %all-to-all-start.7 = ((f32[16,42,128]{2,1,0:T(8,128)}), f32[16,42,128]{2,1,0:T(8,128)S(1)}, u32[]{:S(2)}, u32[]{:S(2)}) async-start(f32[16,42,128]{2,1,0:T(8,128)} %pad_maximum_fusion.4), calls=%async_computation.9 | async-start | bytes 786432 | tf_op jit(solution)/shard_map/all_to_all | solution.py:18
  236.7 13.6 %all_gather.11 = bf16[320,1024]{1,0:T(8,128)(2,1)S(1)} all-gather(bf16[80,1024]{1,0:T(8,128)(2,1)S(1)} %slice.205), channel_id=1, replica_groups=mesh['zl'=4,'x'=4,'y'=4,'zh'=4,'c'=2] {'y'}, dimensions={0}, use_global_device_ids=true | all-gather | bytes 819200 | tf_op jit(solution)/shard_map/all_gather | solution.py:233
  (206 shorter events, 47.7 us)
Async XLA Ops:
  8.0 27.0 %copy-start = (bf16[320,1024]{1,0:T(8,128)(2,1)S(1)}, bf16[320,1024]{1,0:T(8,128)(2,1)}, u32[]{:S(2)}) copy-start(bf16[320,1024]{1,0:T(8,128)(2,1)} %param.13) | copy-start | bytes 1966084
  8.0 26.6 %copy-start.3 = (bf16[768,320]{0,1:T(8,128)(2,1)S(1)}, bf16[768,320]{0,1:T(8,128)(2,1)}, u32[]{:S(2)}) copy-start(bf16[768,320]{0,1:T(8,128)(2,1)} %param.12) | copy-start | bytes 1474564
  12.1 25.6 %all-to-all-start.1 = ((bf16[16,6,128]{2,1,0:T(8,128)(2,1)}), bf16[16,6,128]{2,1,0:T(8,128)(2,1)S(1)}, u32[]{:S(2)}, u32[]{:S(2)}) async-start(bf16[16,6,128]{2,1,0:T(8,128)(2,1)} %reshape.364), calls=%async_computation.2 | async-start | bytes 65536 | tf_op jit(solution)/shard_map/all_to_all | solution.py:18
  21.3 96.7 %reduce-scatter.6.cloned.1.call-start = ((), (), s32[]{:S(2)}) async-start(), calls=%async_computation.11 | async-start | bytes 1966080 | tf_op jit(solution)/shard_map/reduce_scatter | solution.py:95
  23.3 14.7 %collective-permute-start = (bf16[640,128]{1,0:T(8,128)(2,1)S(1)}, bf16[640,128]{1,0:T(8,128)(2,1)S(1)}, u32[]{:S(2)}, u32[]{:S(2)}) collective-permute-start(bf16[640,128]{1,0:T(8,128)(2,1)S(1)} %get-tuple-element.25), channel_id=1, source_target_pairs={{0,8},{8,16},{16,24},{24,0},{1,9},{9,17},{17,25},{25,1},{2,10},{10... | collective-permute-start | bytes 491528 | tf_op jit(solution)/shard_map/ppermute | solution.py:136
  26.5 11.5 %collective-permute-start.1 = (bf16[640,128]{1,0:T(8,128)(2,1)S(1)}, bf16[640,128]{1,0:T(8,128)(2,1)S(1)}, u32[]{:S(2)}, u32[]{:S(2)}) collective-permute-start(bf16[640,128]{1,0:T(8,128)(2,1)S(1)} %get-tuple-element.26), channel_id=1, source_target_pairs={{0,16},{8,24},{16,0},{24,8},{1,17},{9,25},{17,1},{25,9},{2,18},{10... | collective-permute-start | bytes 491528 | tf_op jit(solution)/shard_map/ppermute | solution.py:136
  31.3 7.2 %collective-permute-start.2 = (bf16[640,128]{1,0:T(8,128)(2,1)S(1)}, bf16[640,128]{1,0:T(8,128)(2,1)S(1)}, u32[]{:S(2)}, u32[]{:S(2)}) collective-permute-start(bf16[640,128]{1,0:T(8,128)(2,1)S(1)} %get-tuple-element.27), channel_id=1, source_target_pairs={{0,24},{8,0},{16,8},{24,16},{1,25},{9,1},{17,9},{25,17},{2,26},{10... | collective-permute-start | bytes 491528 | tf_op jit(solution)/shard_map/ppermute | solution.py:136
  39.6 35.6 %all-to-all-start.2 = ((bf16[8,128,128]{2,1,0:T(8,128)(2,1)}), bf16[8,128,128]{2,1,0:T(8,128)(2,1)S(1)}, u32[]{:S(2)}, u32[]{:S(2)}) async-start(bf16[8,128,128]{2,1,0:T(8,128)(2,1)} %pad_maximum_fusion.5), calls=%async_computation.3 | async-start | bytes 524288 | tf_op jit(solution)/shard_map/all_to_all | solution.py:18
  52.0 79.4 %reduce-scatter.10.cloned.1.call-start = ((), (), s32[]{:S(2)}) async-start(), calls=%async_computation.14 | async-start | bytes 73728 | tf_op jit(solution)/shard_map/reduce_scatter | solution.py:156
  54.3 82.8 %all-gather.2.cloned.1.call-start = ((), (), s32[]{:S(2)}) async-start(), calls=%async_computation.12 | async-start | bytes 2621440 | tf_op jit(solution)/shard_map/all_gather | solution.py:173
  89.9 9.6 %collective-permute-start.5 = (bf16[48,1024]{1,0:T(8,128)(2,1)S(1)}, bf16[48,1024]{1,0:T(8,128)(2,1)S(1)}, u32[]{:S(2)}, u32[]{:S(2)}) collective-permute-start(bf16[48,1024]{1,0:T(8,128)(2,1)S(1)} %copy_bitcast_fusion), channel_id=1, source_target_pairs={{0,24},{8,0},{16,8},{24,16},{1,25},{9,1},{17,9},{25,17},{2,26},{10... | collective-permute-start | bytes 294920 | tf_op jit(solution)/shard_map/ppermute | solution.py:41
  94.4 8.0 %collective-permute-start.4 = (bf16[48,1024]{1,0:T(8,128)(2,1)S(1)}, bf16[48,1024]{1,0:T(8,128)(2,1)S(1)}, u32[]{:S(2)}, u32[]{:S(2)}) collective-permute-start(bf16[48,1024]{1,0:T(8,128)(2,1)S(1)} %copy_bitcast_fusion), channel_id=1, source_target_pairs={{0,16},{8,24},{16,0},{24,8},{1,17},{9,25},{17,1},{25,9},{2,18},{10... | collective-permute-start | bytes 294920 | tf_op jit(solution)/shard_map/ppermute | solution.py:41
  97.4 9.6 %collective-permute-start.3 = (bf16[48,1024]{1,0:T(8,128)(2,1)S(1)}, bf16[48,1024]{1,0:T(8,128)(2,1)S(1)}, u32[]{:S(2)}, u32[]{:S(2)}) collective-permute-start(bf16[48,1024]{1,0:T(8,128)(2,1)S(1)} %copy_bitcast_fusion), channel_id=1, source_target_pairs={{0,8},{8,16},{16,24},{24,0},{1,9},{9,17},{17,25},{25,1},{2,10},{10... | collective-permute-start | bytes 294920 | tf_op jit(solution)/shard_map/ppermute | solution.py:41
  118.0 12.3 %all-to-all-start = ((bf16[4,48,1024]{2,1,0:T(8,128)(2,1)}), bf16[4,48,1024]{2,1,0:T(8,128)(2,1)S(1)}, u32[]{:S(2)}, u32[]{:S(2)}) async-start(bf16[4,48,1024]{2,1,0:T(8,128)(2,1)} %bitcast.171), calls=%async_computation.1 | async-start | bytes 786432 | tf_op jit(solution)/shard_map/all_to_all | solution.py:18
  132.9 19.8 %all-to-all-start.4 = ((bf16[8,88,128]{2,1,0:T(8,128)(2,1)}), bf16[8,88,128]{2,1,0:T(8,128)(2,1)}, u32[]{:S(2)}, u32[]{:S(2)}) async-start(bf16[8,88,128]{2,1,0:T(8,128)(2,1)} %broadcast_in_dim.114), calls=%async_computation.5 | async-start | bytes 360448 | tf_op jit(solution)/shard_map/all_to_all | solution.py:18
  136.9 72.8 %reduce-scatter.8.cloned.1.call-start = ((), (), s32[]{:S(2)}) async-start(), calls=%async_computation.13 | async-start | bytes 700416 | tf_op jit(solution)/shard_map/reduce_scatter | solution.py:203
  139.6 17.7 %copy-start.13 = (bf16[48,128]{1,0:T(8,128)(2,1)S(1)}, bf16[48,128]{1,0:T(8,128)(2,1)}, u32[]{:S(2)}) copy-start(bf16[48,128]{1,0:T(8,128)(2,1)} %copy-done.12) | copy-start | bytes 36868
  139.8 18.3 %copy-start.1 = (bf16[8,304,128]{2,1,0:T(8,128)(2,1)}, bf16[8,304,128]{2,1,0:T(8,128)(2,1)S(1)}, u32[]{:S(2)}) copy-start(bf16[8,304,128]{2,1,0:T(8,128)(2,1)S(1)} %copy.210) | copy-start | bytes 1867780
  158.6 11.2 %collective-permute-start.6 = (bf16[80,1024]{1,0:T(8,128)(2,1)S(1)}, bf16[80,1024]{1,0:T(8,128)(2,1)S(1)}, u32[]{:S(2)}, u32[]{:S(2)}) collective-permute-start(bf16[80,1024]{1,0:T(8,128)(2,1)S(1)} %get-tuple-element.29), channel_id=1, source_target_pairs={{0,128},{128,256},{256,384},{384,0},{1,129},{129,257},{257,385},{3... | collective-permute-start | bytes 491528 | tf_op jit(solution)/shard_map/ppermute | solution.py:52
  164.1 8.1 %collective-permute-start.8 = (bf16[80,1024]{1,0:T(8,128)(2,1)S(1)}, bf16[80,1024]{1,0:T(8,128)(2,1)S(1)}, u32[]{:S(2)}, u32[]{:S(2)}) collective-permute-start(bf16[80,1024]{1,0:T(8,128)(2,1)S(1)} %get-tuple-element.30), channel_id=1, source_target_pairs={{0,384},{128,0},{256,128},{384,256},{1,385},{129,1},{257,129},{385... | collective-permute-start | bytes 491528 | tf_op jit(solution)/shard_map/ppermute | solution.py:52
  166.3 12.7 %collective-permute-start.7 = (bf16[80,1024]{1,0:T(8,128)(2,1)S(1)}, bf16[80,1024]{1,0:T(8,128)(2,1)S(1)}, u32[]{:S(2)}, u32[]{:S(2)}) collective-permute-start(bf16[80,1024]{1,0:T(8,128)(2,1)S(1)} %get-tuple-element.31), channel_id=1, source_target_pairs={{0,256},{128,384},{256,0},{384,128},{1,257},{129,385},{257,1},{385... | collective-permute-start | bytes 491528 | tf_op jit(solution)/shard_map/ppermute | solution.py:52
  180.6 30.9 %all-to-all-start.5 = ((bf16[4,200,1024]{2,1,0:T(8,128)(2,1)}), bf16[4,200,1024]{2,1,0:T(8,128)(2,1)S(1)}, u32[]{:S(2)}, u32[]{:S(2)}) async-start(bf16[4,200,1024]{2,1,0:T(8,128)(2,1)} %pad_maximum_fusion), calls=%async_computation.6 | async-start | bytes 3276800 | tf_op jit(solution)/shard_map/all_to_all | solution.py:18
  214.4 14.6 %all-to-all-start.6 = ((bf16[4,88,1024]{2,1,0:T(8,128)(2,1)}), bf16[4,88,1024]{2,1,0:T(8,128)(2,1)S(1)}, u32[]{:S(2)}, u32[]{:S(2)}) async-start(bf16[4,88,1024]{2,1,0:T(8,128)(2,1)} %pad_maximum_fusion.2), calls=%async_computation.8 | async-start | bytes 1441792 | tf_op jit(solution)/shard_map/all_to_all | solution.py:18
  230.0 21.5 %all-to-all-start.7 = ((f32[16,42,128]{2,1,0:T(8,128)}), f32[16,42,128]{2,1,0:T(8,128)S(1)}, u32[]{:S(2)}, u32[]{:S(2)}) async-start(f32[16,42,128]{2,1,0:T(8,128)} %pad_maximum_fusion.4), calls=%async_computation.9 | async-start | bytes 786432 | tf_op jit(solution)/shard_map/all_to_all | solution.py:18
  (23 other events, 114.6 us)
Sparse Core Ops, SparseCore 0:
  37.2 31.5 reduce-scatter.5
  72.2 52.8 reduce-scatter.9
  164.2 45.4 reduce-scatter.7
Sparse Core Ops, SparseCore 1:
  89.9 32.6 all-gather.1

commit v5 on v4

--- a/solution.py
+++ b/solution.py
@@ -34,16 +34,6 @@
 def two_halves(v):
     hi = lax.reduce_precision(v, 8, 7)
     return hi.astype(bf16), (v - hi).astype(bf16)
-
-
-def from_peers(x, axis):
-    n = lax.axis_size(axis)
-    return [x] + [lax.ppermute(x, axis, [(i, (i + k) % n) for i in range(n)]) for k in range(1, n)]
-
-
-def in_order(blocks, axis):
-    n, me = lax.axis_size(axis), lax.axis_index(axis)
-    return jnp.stack([lax.dynamic_index_in_dim(blocks, lax.rem(me - j + n, n), 0, False) for j in range(n)])
 
 
 def to_peers(blocks, axis):
@@ -141,9 +131,6 @@
     down_t = jnp.moveaxis(down_t.reshape(nt, rank, cols), 0, 1).reshape(rank, width)
     up_rows = rank // nx
     up_piece = lax.dynamic_slice_in_dim(up, x_index * up_rows, up_rows, 0)
-    sent = jnp.concatenate(
-        [wa, copies(jnp.concatenate([up_piece, grad_frames], axis=0), nt)], axis=1
-    )
     text_wide = text.astype(f32)
     text_scaled = text_wide * gain[None, :]
     pair = jnp.concatenate(
@@ -153,29 +140,37 @@
         ],
         axis=1,
     )
-    pair = lax.psum_scatter(pair, TP, scatter_dimension=0, tiled=True)
     sq_text = dot(jnp.ones((8, width), bf16), (text_wide * text_wide).astype(bf16), 1, 1)[0]
 
+    sent = jnp.concatenate(
+        [
+            wa,
+            copies(jnp.concatenate([up_piece, grad_frames], axis=0), nt),
+            pair.reshape(nt, toks // nt, cols),
+        ],
+        axis=1,
+    )
     came = exchange(sent, TP)
     at = piece + up_rows
-
-    grad_full = jnp.moveaxis(came[:, at:], 0, 1).reshape(n_frames, nt * cols)
-    grad_all = jnp.concatenate(from_peers(grad_full, "y"), axis=0)
+    pair = jnp.sum(came[:, at + n_frames :].astype(f32), axis=0).astype(bf16)
+
+    blocks = exchange(x_sum.reshape(nzl, n_frames, width), "zl")
+    embedded = jnp.sum(blocks.astype(f32), axis=0).astype(bf16)
+    wide = embedded.astype(f32)
+    scaled = wide * gain[None, :]
+
+    grad_full = jnp.moveaxis(came[:, at : at + n_frames], 0, 1).reshape(n_frames, nt * cols)
+    grad_all = lax.all_gather(grad_full, "y", axis=0, tiled=True)
     weights = jnp.moveaxis(came[:, :at], 0, 1).reshape(at, nt * cols)
     weights = lax.all_gather(weights, "x")
     up_full = weights[:, piece:].reshape(rank, nt * cols)
     weights = weights[:, :piece].reshape(nx * piece, nt * cols)
     lora_frames = (adapter_scale * dot(grad_full, up_full, 1, 1)).astype(bf16)
     spread = dot(grad_all, weights, 1, 1).astype(bf16).reshape(ny, n_frames, nx * piece)
-    back = jnp.moveaxis(exchange(in_order(spread, "y"), "y"), 0, 1)
+    back = jnp.moveaxis(exchange(after(spread, embedded), "y"), 0, 1)
     grad_norm = back.reshape(n_frames, width).astype(f32)
     grad_norm = grad_norm + dot(lora_frames, down_t, 1, 0)
     weights = lax.all_gather(weights, "y", axis=0, tiled=True)
-
-    blocks = exchange(x_sum.reshape(nzl, n_frames, width), "zl")
-    embedded = jnp.sum(blocks.astype(f32), axis=0).astype(bf16)
-    wide = embedded.astype(f32)
-    scaled = wide * gain[None, :]
 
     sq_hi, sq_lo = two_halves(jnp.sum(wide * wide, axis=1, keepdims=True))
     d_hi, d_lo = two_halves(jnp.sum(scaled * grad_norm, axis=1, keepdims=True))

time: 263 us -> 252 us (0.958)
  blocking collectives: 36.9 us -> 76.1 us
  waiting for transfers between devices: 92.7 us -> 65 us
  starting transfers between devices: 76.4 us -> 58.7 us
  other arithmetic: 10.2 us -> 7.03 us
    all_to_all x1, blocking collectives: 9.64 us -> 35.6 us  [exchange(): return lax.all_to_all(blocks, axis, split_axis=0, concat_axis=0, tiled=True)]
    all_to_all x7, waiting for transfers between devices: 50.8 us -> 35.2 us  [exchange(): return lax.all_to_all(blocks, axis, split_axis=0, concat_axis=0, tiled=True)]
    all_gather x0 -> x1, blocking collectives: none -> 13.7 us  [shards(): grad_all = lax.all_gather(grad_full, 'y', axis=0, tiled=True)]
    ppermute x3 -> x0, starting transfers between devices: 9.52 us -> none  [from_peers(): lax.ppermute(x, axis, [(i, (i + k) % n) for i in range(n)])]
    all_to_all x7, starting transfers between devices: 44.4 us -> 36 us  [exchange(): return lax.all_to_all(blocks, axis, split_axis=0, concat_axis=0, tiled=True)]
    ppermute x3 -> x0, waiting for transfers between devices: 7.52 us -> none  [from_peers(): lax.ppermute(x, axis, [(i, (i + k) % n) for i in range(n)])]
  transfers between devices with their start and end apart: 20 -> 16, of which waited for: 10 -> 7; matrix products, arithmetic and copies ran while one was open for 8% -> 8% of each run, Pallas kernels for 0% -> 0%
where the time goes in v5:
time: 252 us; the launch traced here: 251 us
  blocking collectives  76.1 us (30%)
  waiting for transfers between devices  65 us (26%)
  starting transfers between devices  58.7 us (23%)
  between operations  18.7 us (7%)
  local copies, waits for them, and re-layouts  14.5 us (6%)
  matrix products  10.7 us (4%)
  other arithmetic  7.03 us (3%)
    all_to_all x7, starting transfers between devices, exchange(): return lax.all_to_all(blocks, axis, split_axis=0, concat_axis=0, tiled=True)  36 us
    all_to_all x1, blocking collectives, exchange(): return lax.all_to_all(blocks, axis, split_axis=0, concat_axis=0, tiled=True)  35.6 us
    all_to_all x7, waiting for transfers between devices, exchange(): return lax.all_to_all(blocks, axis, split_axis=0, concat_axis=0, tiled=True)  35.2 us
    reduce_scatter x1, waiting for transfers between devices, shards(): summed = lax.psum_scatter(base, TP, scatter_dimension=0, tiled=True)  22.7 us
    all_gather x1, blocking collectives, shards(): lax.all_gather(came[:part].astype(bf16), 'y', axis=0, tiled=True)  13.7 us
    all_gather x1, blocking collectives, shards(): grad_all = lax.all_gather(grad_full, 'y', axis=0, tiled=True)  13.7 us
    all_gather x1, blocking collectives, shards(): weights = lax.all_gather(weights, 'x')  13 us
    ppermute x3, starting transfers between devices, shards(): lax.ppermute(for_y(k), 'y', [(i, (i + k) % ny) for i in range(ny)])  11.6 us
  transfers between devices with their start and end apart: 16, of which 7 were waited for; matrix products, arithmetic and copies ran while one was open for 8% of the time, Pallas kernels for 0%

profile of v5, /device:TPU:2, one launch (start us, length us, event | category | flops | bytes accessed | tf_op | source)
XLA Modules:
  0.0 250.8 jit_solution(9664677344223815653)
XLA Ops:
  10.1 3.5 %collective-permute-start = (bf16[640,128]{1,0:T(8,128)(2,1)S(1)}, bf16[640,128]{1,0:T(8,128)(2,1)S(1)}, u32[]{:S(2)}, u32[]{:S(2)}) collective-permute-start(bf16[640,128]{1,0:T(8,128)(2,1)S(1)} %get-tuple-element.25), channel_id=1, source_target_pairs={{0,8},{8,16},{16,24},{24,0},{1,9},{9,17},{17,25},{25,1},{2,10},{10... | collective-permute-start | bytes 491528 | tf_op jit(solution)/shard_map/ppermute | solution.py:126
  13.6 4.8 %collective-permute-start.1 = (bf16[640,128]{1,0:T(8,128)(2,1)S(1)}, bf16[640,128]{1,0:T(8,128)(2,1)S(1)}, u32[]{:S(2)}, u32[]{:S(2)}) collective-permute-start(bf16[640,128]{1,0:T(8,128)(2,1)S(1)} %get-tuple-element.26), channel_id=1, source_target_pairs={{0,16},{8,24},{16,0},{24,8},{1,17},{9,25},{17,1},{25,9},{2,18},{10... | collective-permute-start | bytes 491528 | tf_op jit(solution)/shard_map/ppermute | solution.py:126
  18.4 3.3 %collective-permute-start.2 = (bf16[640,128]{1,0:T(8,128)(2,1)S(1)}, bf16[640,128]{1,0:T(8,128)(2,1)S(1)}, u32[]{:S(2)}, u32[]{:S(2)}) collective-permute-start(bf16[640,128]{1,0:T(8,128)(2,1)S(1)} %get-tuple-element.27), channel_id=1, source_target_pairs={{0,24},{8,0},{16,8},{24,16},{1,25},{9,1},{17,9},{25,17},{2,26},{10... | collective-permute-start | bytes 491528 | tf_op jit(solution)/shard_map/ppermute | solution.py:126
  23.5 8.9 %all-to-all-start.1 = ((bf16[16,6,128]{2,1,0:T(8,128)(2,1)}), bf16[16,6,128]{2,1,0:T(8,128)(2,1)S(1)}, u32[]{:S(2)}, u32[]{:S(2)}) async-start(bf16[16,6,128]{2,1,0:T(8,128)(2,1)} %reshape.369), calls=%async_computation.2 | async-start | bytes 65536 | tf_op jit(solution)/shard_map/all_to_all | solution.py:18
  36.5 2.6 %all-to-all-done.1 = bf16[16,6,128]{2,1,0:T(8,128)(2,1)S(1)} async-done(((bf16[16,6,128]{2,1,0:T(8,128)(2,1)}), bf16[16,6,128]{2,1,0:T(8,128)(2,1)S(1)}, u32[]{:S(2)}, u32[]{:S(2)}) %all-to-all-start.1) | async-done | bytes 24608 | tf_op jit(solution)/shard_map/all_to_all | solution.py:18
  41.7 35.6 %all_to_all.40 = bf16[8,160,128]{2,1,0:T(8,128)(2,1)S(1)} all-to-all(bf16[8,160,128]{2,1,0:T(8,128)(2,1)S(1)} %pad_maximum_fusion.5), channel_id=1, replica_groups=mesh['zl'=4,'x'=4,'y'=4,'zh'=4,'c'=2] {'zh','c'}, dimensions={0} | all-to-all | bytes 655360 | tf_op jit(solution)/shard_map/all_to_all | solution.py:18
  77.5 13.0 %all_gather.13 = bf16[4,80,1024]{2,1,0:T(8,128)(2,1)S(1)} all-gather(bf16[1,80,1024]{2,1,0:T(8,128)(2,1)S(1)} %all_gather_reshape.3), channel_id=1, replica_groups=mesh['zl'=4,'x'=4,'y'=4,'zh'=4,'c'=2] {'x'}, dimensions={0}, use_global_device_ids=true | all-gather | bytes 819200 | tf_op jit(solution)/shard_map/all_gather | solution.py:165
  91.4 4.5 %all-to-all-start = ((bf16[4,48,1024]{2,1,0:T(8,128)(2,1)}), bf16[4,48,1024]{2,1,0:T(8,128)(2,1)S(1)}, u32[]{:S(2)}, u32[]{:S(2)}) async-start(bf16[4,48,1024]{2,1,0:T(8,128)(2,1)} %bitcast.174), calls=%async_computation.1 | async-start | bytes 786432 | tf_op jit(solution)/shard_map/all_to_all | solution.py:18
  96.2 13.7 %all_gather.12 = bf16[192,1024]{1,0:T(8,128)(2,1)S(1)} all-gather(bf16[48,1024]{1,0:T(8,128)(2,1)S(1)} %copy_bitcast_fusion.1), channel_id=1, replica_groups=mesh['zl'=4,'x'=4,'y'=4,'zh'=4,'c'=2] {'y'}, dimensions={0}, use_global_device_ids=true | all-gather | bytes 491520 | tf_op jit(solution)/shard_map/all_gather | solution.py:163
  112.4 3.3 %all-to-all-start.3 = ((bf16[4,48,256]{2,1,0:T(8,128)(2,1)}), bf16[4,48,256]{2,1,0:T(8,128)(2,1)S(1)}, u32[]{:S(2)}, u32[]{:S(2)}) async-start(bf16[4,48,256]{2,1,0:T(8,128)(2,1)} %bitcast.28), calls=%async_computation.4 | async-start | bytes 196608 | tf_op jit(solution)/shard_map/all_to_all | solution.py:18
  115.9 6.6 %all-to-all-done.3 = bf16[4,48,256]{2,1,0:T(8,128)(2,1)S(1)} async-done(((bf16[4,48,256]{2,1,0:T(8,128)(2,1)}), bf16[4,48,256]{2,1,0:T(8,128)(2,1)S(1)}, u32[]{:S(2)}, u32[]{:S(2)}) %all-to-all-start.3) | async-done | bytes 98336 | tf_op jit(solution)/shard_map/all_to_all | solution.py:18
  124.1 3.4 %all-to-all-start.4 = ((bf16[8,88,128]{2,1,0:T(8,128)(2,1)}), bf16[8,88,128]{2,1,0:T(8,128)(2,1)S(1)}, u32[]{:S(2)}, u32[]{:S(2)}) async-start(bf16[8,88,128]{2,1,0:T(8,128)(2,1)} %broadcast_in_dim.114), calls=%async_computation.5 | async-start | bytes 360448 | tf_op jit(solution)/shard_map/all_to_all | solution.py:18
  127.8 2.4 fusion.1
  131.5 15.6 %all-to-all-done.4 = bf16[8,88,128]{2,1,0:T(8,128)(2,1)S(1)} async-done(((bf16[8,88,128]{2,1,0:T(8,128)(2,1)}), bf16[8,88,128]{2,1,0:T(8,128)(2,1)S(1)}, u32[]{:S(2)}, u32[]{:S(2)}) %all-to-all-start.4) | async-done | bytes 180256 | tf_op jit(solution)/shard_map/all_to_all | solution.py:18
  151.0 2.9 %collective-permute-start.3 = (bf16[80,1024]{1,0:T(8,128)(2,1)S(1)}, bf16[80,1024]{1,0:T(8,128)(2,1)S(1)}, u32[]{:S(2)}, u32[]{:S(2)}) collective-permute-start(bf16[80,1024]{1,0:T(8,128)(2,1)S(1)} %get-tuple-element.29), channel_id=1, source_target_pairs={{0,128},{128,256},{256,384},{384,0},{1,129},{129,257},{257,385},{3... | collective-permute-start | bytes 491528 | tf_op jit(solution)/shard_map/ppermute | solution.py:42
  154.0 3.3 %collective-permute-start.4 = (bf16[80,1024]{1,0:T(8,128)(2,1)S(1)}, bf16[80,1024]{1,0:T(8,128)(2,1)S(1)}, u32[]{:S(2)}, u32[]{:S(2)}) collective-permute-start(bf16[80,1024]{1,0:T(8,128)(2,1)S(1)} %get-tuple-element.31), channel_id=1, source_target_pairs={{0,256},{128,384},{256,0},{384,128},{1,257},{129,385},{257,1},{385... | collective-permute-start | bytes 491528 | tf_op jit(solution)/shard_map/ppermute | solution.py:42
  157.3 4.8 %collective-permute-start.5 = (bf16[80,1024]{1,0:T(8,128)(2,1)S(1)}, bf16[80,1024]{1,0:T(8,128)(2,1)S(1)}, u32[]{:S(2)}, u32[]{:S(2)}) collective-permute-start(bf16[80,1024]{1,0:T(8,128)(2,1)S(1)} %get-tuple-element.30), channel_id=1, source_target_pairs={{0,384},{128,0},{256,128},{384,256},{1,385},{129,1},{257,129},{385... | collective-permute-start | bytes 491528 | tf_op jit(solution)/shard_map/ppermute | solution.py:42
  162.1 5.9 %collective-permute-done.4 = bf16[80,1024]{1,0:T(8,128)(2,1)S(1)} collective-permute-done((bf16[80,1024]{1,0:T(8,128)(2,1)S(1)}, bf16[80,1024]{1,0:T(8,128)(2,1)S(1)}, u32[]{:S(2)}, u32[]{:S(2)}) %collective-permute-start.4) | collective-permute-done | bytes 163872 | tf_op jit(solution)/shard_map/ppermute | solution.py:42
  170.9 4.9 %all-to-all-start.5 = ((bf16[4,200,1024]{2,1,0:T(8,128)(2,1)}), bf16[4,200,1024]{2,1,0:T(8,128)(2,1)S(1)}, u32[]{:S(2)}, u32[]{:S(2)}) async-start(bf16[4,200,1024]{2,1,0:T(8,128)(2,1)} %pad_maximum_fusion), calls=%async_computation.6 | async-start | bytes 3276800 | tf_op jit(solution)/shard_map/all_to_all | solution.py:18
  175.7 22.7 %reduce-scatter.5.cloned.1.call-done = bf16[304,128]{1,0:T(8,128)(2,1)} async-done(((bf16[2432,128]{1,0:T(8,128)(2,1)}), bf16[304,128]{1,0:T(8,128)(2,1)}) %reduce-scatter.5.cloned.1.call-update) | async-done | bytes 77840 | tf_op jit(solution)/shard_map/reduce_scatter | solution.py:198
  203.1 4.5 %all-to-all-start.6 = ((bf16[4,88,1024]{2,1,0:T(8,128)(2,1)}), bf16[4,88,1024]{2,1,0:T(8,128)(2,1)S(1)}, u32[]{:S(2)}, u32[]{:S(2)}) async-start(bf16[4,88,1024]{2,1,0:T(8,128)(2,1)} %pad_maximum_fusion.2), calls=%async_computation.8 | async-start | bytes 1441792 | tf_op jit(solution)/shard_map/all_to_all | solution.py:18
  208.1 10.3 %all-to-all-done.6 = bf16[4,88,1024]{2,1,0:T(8,128)(2,1)S(1)} async-done(((bf16[4,88,1024]{2,1,0:T(8,128)(2,1)}), bf16[4,88,1024]{2,1,0:T(8,128)(2,1)S(1)}, u32[]{:S(2)}, u32[]{:S(2)}) %all-to-all-start.6) | async-done | bytes 720928 | tf_op jit(solution)/shard_map/all_to_all | solution.py:18
  219.5 6.5 %all-to-all-start.7 = ((f32[16,42,128]{2,1,0:T(8,128)}), f32[16,42,128]{2,1,0:T(8,128)S(1)}, u32[]{:S(2)}, u32[]{:S(2)}) async-start(f32[16,42,128]{2,1,0:T(8,128)} %pad_maximum_fusion.4), calls=%async_computation.9 | async-start | bytes 786432 | tf_op jit(solution)/shard_map/all_to_all | solution.py:18
  226.0 13.7 %all_gather.15 = bf16[320,1024]{1,0:T(8,128)(2,1)S(1)} all-gather(bf16[80,1024]{1,0:T(8,128)(2,1)S(1)} %slice.216), channel_id=1, replica_groups=mesh['zl'=4,'x'=4,'y'=4,'zh'=4,'c'=2] {'y'}, dimensions={0}, use_global_device_ids=true | all-gather | bytes 819200 | tf_op jit(solution)/shard_map/all_gather | solution.py:228
  (207 shorter events, 31.2 us)
Async XLA Ops:
  8.0 24.8 %copy-start = (bf16[320,1024]{1,0:T(8,128)(2,1)S(1)}, bf16[320,1024]{1,0:T(8,128)(2,1)}, u32[]{:S(2)}) copy-start(bf16[320,1024]{1,0:T(8,128)(2,1)} %param.13) | copy-start | bytes 1966084
  8.0 13.9 %copy-start.20 = (s32[1,16,16]{2,1,0:T(8,128)S(1)}, s32[1,16,16]{2,1,0:T(8,128)}, u32[]{:S(2)}) copy-start(s32[1,16,16]{2,1,0:T(8,128)} %param.19) | copy-start | bytes 3076
  8.1 14.5 %copy-start.10 = (bf16[256,128]{1,0:T(8,128)(2,1)S(1)}, bf16[256,128]{1,0:T(8,128)(2,1)}, u32[]{:S(2)}) copy-start(bf16[256,128]{1,0:T(8,128)(2,1)} %param.23) | copy-start | bytes 196612
  8.1 24.3 %copy-start.4 = (bf16[768,320]{0,1:T(8,128)(2,1)S(1)}, bf16[768,320]{0,1:T(8,128)(2,1)}, u32[]{:S(2)}) copy-start(bf16[768,320]{0,1:T(8,128)(2,1)} %param.12) | copy-start | bytes 1474564
  10.1 29.3 %collective-permute-start = (bf16[640,128]{1,0:T(8,128)(2,1)S(1)}, bf16[640,128]{1,0:T(8,128)(2,1)S(1)}, u32[]{:S(2)}, u32[]{:S(2)}) collective-permute-start(bf16[640,128]{1,0:T(8,128)(2,1)S(1)} %get-tuple-element.25), channel_id=1, source_target_pairs={{0,8},{8,16},{16,24},{24,0},{1,9},{9,17},{17,25},{25,1},{2,10},{10... | collective-permute-start | bytes 491528 | tf_op jit(solution)/shard_map/ppermute | solution.py:126
  13.6 25.8 %collective-permute-start.1 = (bf16[640,128]{1,0:T(8,128)(2,1)S(1)}, bf16[640,128]{1,0:T(8,128)(2,1)S(1)}, u32[]{:S(2)}, u32[]{:S(2)}) collective-permute-start(bf16[640,128]{1,0:T(8,128)(2,1)S(1)} %get-tuple-element.26), channel_id=1, source_target_pairs={{0,16},{8,24},{16,0},{24,8},{1,17},{9,25},{17,1},{25,9},{2,18},{10... | collective-permute-start | bytes 491528 | tf_op jit(solution)/shard_map/ppermute | solution.py:126
  18.4 21.0 %collective-permute-start.2 = (bf16[640,128]{1,0:T(8,128)(2,1)S(1)}, bf16[640,128]{1,0:T(8,128)(2,1)S(1)}, u32[]{:S(2)}, u32[]{:S(2)}) collective-permute-start(bf16[640,128]{1,0:T(8,128)(2,1)S(1)} %get-tuple-element.27), channel_id=1, source_target_pairs={{0,24},{8,0},{16,8},{24,16},{1,25},{9,1},{17,9},{25,17},{2,26},{10... | collective-permute-start | bytes 491528 | tf_op jit(solution)/shard_map/ppermute | solution.py:126
  23.5 15.7 %all-to-all-start.1 = ((bf16[16,6,128]{2,1,0:T(8,128)(2,1)}), bf16[16,6,128]{2,1,0:T(8,128)(2,1)S(1)}, u32[]{:S(2)}, u32[]{:S(2)}) async-start(bf16[16,6,128]{2,1,0:T(8,128)(2,1)} %reshape.369), calls=%async_computation.2 | async-start | bytes 65536 | tf_op jit(solution)/shard_map/all_to_all | solution.py:18
  32.4 59.1 %reduce-scatter.3.cloned.1.call-start = ((), (), s32[]{:S(2)}) async-start(), calls=%async_computation.10 | async-start | bytes 1966080 | tf_op jit(solution)/shard_map/reduce_scatter | solution.py:85
  34.9 92.8 %all-gather.2.cloned.1.call-start = ((), (), s32[]{:S(2)}) async-start(), calls=%async_computation.11 | async-start | bytes 2621440 | tf_op jit(solution)/shard_map/all_gather | solution.py:173
  91.4 20.0 %copy-start.1 = (bf16[4,64,1024]{2,1,0:T(8,128)(2,1)S(1)}, bf16[4,64,1024]{2,1,0:T(8,128)(2,1)}, u32[]{:S(2)}) copy-start(bf16[4,64,1024]{2,1,0:T(8,128)(2,1)} %slice.163) | copy-start | bytes 1572868
  91.4 18.7 %all-to-all-start = ((bf16[4,48,1024]{2,1,0:T(8,128)(2,1)}), bf16[4,48,1024]{2,1,0:T(8,128)(2,1)S(1)}, u32[]{:S(2)}, u32[]{:S(2)}) async-start(bf16[4,48,1024]{2,1,0:T(8,128)(2,1)} %bitcast.174), calls=%async_computation.1 | async-start | bytes 786432 | tf_op jit(solution)/shard_map/all_to_all | solution.py:18
  112.4 10.1 %all-to-all-start.3 = ((bf16[4,48,256]{2,1,0:T(8,128)(2,1)}), bf16[4,48,256]{2,1,0:T(8,128)(2,1)S(1)}, u32[]{:S(2)}, u32[]{:S(2)}) async-start(bf16[4,48,256]{2,1,0:T(8,128)(2,1)} %bitcast.28), calls=%async_computation.4 | async-start | bytes 196608 | tf_op jit(solution)/shard_map/all_to_all | solution.py:18
  124.1 23.0 %all-to-all-start.4 = ((bf16[8,88,128]{2,1,0:T(8,128)(2,1)}), bf16[8,88,128]{2,1,0:T(8,128)(2,1)S(1)}, u32[]{:S(2)}, u32[]{:S(2)}) async-start(bf16[8,88,128]{2,1,0:T(8,128)(2,1)} %broadcast_in_dim.114), calls=%async_computation.5 | async-start | bytes 360448 | tf_op jit(solution)/shard_map/all_to_all | solution.py:18
  127.5 70.9 %reduce-scatter.5.cloned.1.call-start = ((), (), s32[]{:S(2)}) async-start(), calls=%async_computation.12 | async-start | bytes 700416 | tf_op jit(solution)/shard_map/reduce_scatter | solution.py:198
  130.2 18.4 %copy-start.12 = (bf16[48,64]{1,0:T(8,128)(2,1)S(1)}, bf16[48,64]{1,0:T(8,128)(2,1)}, u32[]{:S(2)}) copy-start(bf16[48,64]{1,0:T(8,128)(2,1)} %copy-done.11) | copy-start | bytes 18436
  130.3 20.0 %copy-start.2 = (bf16[38,8,8,128]{3,2,0,1:T(8,128)(2,1)}, bf16[38,8,8,128]{3,2,0,1:T(8,128)(2,1)S(1)}, u32[]{:S(2)}) copy-start(bf16[38,8,8,128]{3,2,0,1:T(8,128)(2,1)S(1)} %copy.220) | copy-start | bytes 1867780
  130.3 18.9 %copy-start.7 = (bf16[256,128]{1,0:T(8,128)(2,1)S(1)}, bf16[256,128]{1,0:T(8,128)(2,1)}, u32[]{:S(2)}) copy-start(bf16[256,128]{1,0:T(8,128)(2,1)} %copy-done.6) | copy-start | bytes 196612
  151.0 11.1 %collective-permute-start.3 = (bf16[80,1024]{1,0:T(8,128)(2,1)S(1)}, bf16[80,1024]{1,0:T(8,128)(2,1)S(1)}, u32[]{:S(2)}, u32[]{:S(2)}) collective-permute-start(bf16[80,1024]{1,0:T(8,128)(2,1)S(1)} %get-tuple-element.29), channel_id=1, source_target_pairs={{0,128},{128,256},{256,384},{384,0},{1,129},{129,257},{257,385},{3... | collective-permute-start | bytes 491528 | tf_op jit(solution)/shard_map/ppermute | solution.py:42
  154.0 14.0 %collective-permute-start.4 = (bf16[80,1024]{1,0:T(8,128)(2,1)S(1)}, bf16[80,1024]{1,0:T(8,128)(2,1)S(1)}, u32[]{:S(2)}, u32[]{:S(2)}) collective-permute-start(bf16[80,1024]{1,0:T(8,128)(2,1)S(1)} %get-tuple-element.31), channel_id=1, source_target_pairs={{0,256},{128,384},{256,0},{384,128},{1,257},{129,385},{257,1},{385... | collective-permute-start | bytes 491528 | tf_op jit(solution)/shard_map/ppermute | solution.py:42
  157.3 12.0 %collective-permute-start.5 = (bf16[80,1024]{1,0:T(8,128)(2,1)S(1)}, bf16[80,1024]{1,0:T(8,128)(2,1)S(1)}, u32[]{:S(2)}, u32[]{:S(2)}) collective-permute-start(bf16[80,1024]{1,0:T(8,128)(2,1)S(1)} %get-tuple-element.30), channel_id=1, source_target_pairs={{0,384},{128,0},{256,128},{384,256},{1,385},{129,1},{257,129},{385... | collective-permute-start | bytes 491528 | tf_op jit(solution)/shard_map/ppermute | solution.py:42
  170.9 29.4 %all-to-all-start.5 = ((bf16[4,200,1024]{2,1,0:T(8,128)(2,1)}), bf16[4,200,1024]{2,1,0:T(8,128)(2,1)S(1)}, u32[]{:S(2)}, u32[]{:S(2)}) async-start(bf16[4,200,1024]{2,1,0:T(8,128)(2,1)} %pad_maximum_fusion), calls=%async_computation.6 | async-start | bytes 3276800 | tf_op jit(solution)/shard_map/all_to_all | solution.py:18
  203.1 15.3 %all-to-all-start.6 = ((bf16[4,88,1024]{2,1,0:T(8,128)(2,1)}), bf16[4,88,1024]{2,1,0:T(8,128)(2,1)S(1)}, u32[]{:S(2)}, u32[]{:S(2)}) async-start(bf16[4,88,1024]{2,1,0:T(8,128)(2,1)} %pad_maximum_fusion.2), calls=%async_computation.8 | async-start | bytes 1441792 | tf_op jit(solution)/shard_map/all_to_all | solution.py:18
  219.5 21.5 %all-to-all-start.7 = ((f32[16,42,128]{2,1,0:T(8,128)}), f32[16,42,128]{2,1,0:T(8,128)S(1)}, u32[]{:S(2)}, u32[]{:S(2)}) async-start(f32[16,42,128]{2,1,0:T(8,128)} %pad_maximum_fusion.4), calls=%async_computation.9 | async-start | bytes 786432 | tf_op jit(solution)/shard_map/all_to_all | solution.py:18
  (24 other events, 110.8 us)
Sparse Core Ops, SparseCore 0:
  36.0 31.5 reduce-scatter.2
  154.1 44.2 reduce-scatter.4
Sparse Core Ops, SparseCore 1:
  91.5 31.7 all-gather.1

commit v6 on v5

--- a/solution.py
+++ b/solution.py
@@ -83,6 +83,7 @@
     by_x = jnp.moveaxis(frames.reshape(nzl, nx, n_frames, frames.shape[1]), 1, 0)
     partial = dot(by_x.reshape(frames.shape), projector, 1, 0).astype(bf16)
     x_sum = lax.psum_scatter(partial, "x", scatter_dimension=0, tiled=True)
+    all_frames = lax.all_gather(by_x.reshape(frames.shape), "y", axis=0, tiled=True)
 
     own_sizes = pick_entry(clip_len[0], grp_index, 0)
     before = lax.broadcasted_iota(jnp.int32, (ng, ng), 1) < lax.broadcasted_iota(jnp.int32, (ng, ng), 0)
@@ -160,7 +161,7 @@
     scaled = wide * gain[None, :]
 
     grad_full = jnp.moveaxis(came[:, at : at + n_frames], 0, 1).reshape(n_frames, nt * cols)
-    grad_all = lax.all_gather(grad_full, "y", axis=0, tiled=True)
+    grad_all = lax.all_gather(after(grad_full, all_frames), "y", axis=0, tiled=True)
     weights = jnp.moveaxis(came[:, :at], 0, 1).reshape(at, nt * cols)
     weights = lax.all_gather(weights, "x")
     up_full = weights[:, piece:].reshape(rank, nt * cols)
@@ -196,15 +197,13 @@
     base = dot(all_scaled.astype(bf16), weights, 1, 0).astype(bf16)
     base = jnp.moveaxis(base.reshape(rows, nt, cols), 1, 0).reshape(nt * rows, cols)
     summed = lax.psum_scatter(base, TP, scatter_dimension=0, tiled=True)
-    values = summed.astype(f32) * inv_rms + adapter_scale * dot(low_half, up, 1, 0)
-    values = values.astype(bf16)
 
     normed = (all_scaled * inv_rms).astype(bf16)
-    k = rank // ng
-    down_part = dot(lora, normed, 0, 0).astype(bf16).reshape(nzl, nx, k, width)
+    quarter = width // ny
+    down_part = dot(lora, normed, 0, 0).astype(bf16).reshape(nzl, ny * nx, width)
     up_part = (adapter_scale * dot(low_half, grad_rows, 0, 0)).astype(bf16)
-    up_part = jnp.pad(up_part, ((0, 0), (0, width - cols))).reshape(nzl, nx, k, width)
-    adapters = jnp.concatenate([down_part, up_part], axis=2).reshape(nzl, nx * 2 * k, width)
+    up_part = jnp.pad(up_part, ((0, 0), (0, width - cols))).reshape(nzl, ny * nx, width)
+    adapters = jnp.concatenate([down_part, up_part], axis=1)
 
     inv_f = after(inv_rms[toks:], base)
     frame_grad = (
@@ -213,27 +212,34 @@
     near = to_peers(
         lambda z: jnp.concatenate([frame_grad, lax.dynamic_index_in_dim(adapters, z, 0, False)], axis=0), "zl"
     )
-    adapters = sum(b[n_frames:].astype(f32) for b in near).astype(bf16).reshape(nx, 2 * k, width)
+    adapters = sum(b[n_frames:].astype(f32) for b in near).astype(bf16)
     frame_grad = placed([b[:n_frames] for b in near], 0, "zl")
-    came = exchange(jnp.concatenate([copies(frame_grad, nx), adapters], axis=1), "x")
-    adapters = jnp.sum(came[:, nzl * n_frames :].astype(f32), axis=0).astype(bf16)
-    all_grad = came[:, : nzl * n_frames].reshape(nx, nzl, n_frames, width)
-    all_grad = jnp.moveaxis(all_grad, 0, 1).reshape(ng * n_frames, width)
-    proj_part = after(dot(frames, all_grad, 0, 0), summed).astype(bf16)
-    part = frames.shape[1] // ny
-    came = exchange(
-        jnp.concatenate([proj_part.reshape(ny, part, width), copies(adapters, ny)], axis=1), "y"
-    )
-    came = jnp.sum(came.astype(f32), axis=0)
-    projector_grad = lax.all_gather(came[:part].astype(bf16), "y", axis=0, tiled=True).astype(f32)
-
-    n_d = k * width // cols
-    own = jnp.concatenate([came[part : part + k].reshape(n_d, cols), came[part + k :, :cols]], axis=0)
-    out_slots = dot(sender, values[toks:], 1, 0).reshape(ng, cap, cols)
-    last = exchange(jnp.concatenate([copies(own, ng), out_slots], axis=1), GRP)
-    down_grad = last[:, :n_d].reshape(rank, width).T
-    up_grad = last[:, n_d : n_d + k].reshape(rank, cols)
-    in_slots = last[:, n_d + k :].astype(bf16).reshape(slots, cols)
+
+    n_x = nzl * n_frames
+    frame_grad = jnp.moveaxis(frame_grad.reshape(n_x, ny, quarter), 1, 0)
+    frame_grad = jnp.broadcast_to(frame_grad[:, None], (ny, nx, n_x, quarter))
+    frame_grad = frame_grad.reshape(ny * nx, n_x, quarter)
+    down_part = adapters[: ny * nx].reshape(ny * nx, ny, quarter)
+    up_part = adapters[ny * nx :, :quarter].reshape(ny * nx, 1, quarter)
+    spare = jnp.zeros((ny * nx, 7 - ny, quarter), bf16)
+    came = exchange(jnp.concatenate([frame_grad, down_part, up_part, spare], axis=1), ("y", "x"))
+    own = jnp.sum(came[:, n_x : n_x + ny + 1].astype(f32), axis=0).astype(bf16)
+    own = jnp.concatenate([own[:ny].reshape(width // cols, cols), own[ny:, :cols]], axis=0)
+
+    values = summed.astype(f32) * inv_rms + adapter_scale * dot(low_half, up, 1, 0)
+    values = values.astype(bf16)
+    out_slots = dot(sender, values[toks:], 1, 0).astype(bf16).reshape(nzl, 1, nx, cap, cols)
+    out_slots = jnp.broadcast_to(out_slots, (nzl, ny, nx, cap, cols)).reshape(ny * ng, cap, cols)
+    last = exchange(jnp.concatenate([copies(own, ny * ng), out_slots], axis=1), ("zl", "y", "x"))
+    n_d = width // cols
+    down_grad = last[:, :n_d].reshape(rank, width).astype(f32).T
+    up_grad = last[:, n_d].astype(f32)
+    all_grad = came[:, :n_x].reshape(ny * nx * n_x, quarter)
+    projector_grad = after(dot(all_frames, all_grad, 0, 0), summed).astype(bf16)
+    projector_grad = lax.all_gather(projector_grad, "y", axis=1, tiled=True).astype(f32)
+
+    in_slots = last[:, -cap:].reshape(nzl, ny, nx * cap, cols)
+    in_slots = lax.dynamic_index_in_dim(in_slots, y_index, 1, False).reshape(slots, cols)
     audio_values = dot(receiver, in_slots, 1, 0).astype(bf16)
     value_output = jnp.where(is_audio[:, None], audio_values, values[:toks])
     return value_output, projector_grad, down_grad, up_grad

time: 252 us -> 253 us (level)
  starting transfers between devices: 58.7 us -> 55 us
    all_to_all x7 -> x6, waiting for transfers between devices: 35.2 us -> 26.5 us  [exchange(): return lax.all_to_all(blocks, axis, split_axis=0, concat_axis=0, tiled=True)]
    reduce_scatter x1, waiting for transfers between devices: 22.7 us -> 28.1 us  [shards(): summed = lax.psum_scatter(base, TP, scatter_dimension=0, tiled=True)]
    all_to_all x7 -> x6, starting transfers between devices: 36 us -> 33.8 us  [exchange(): return lax.all_to_all(blocks, axis, split_axis=0, concat_axis=0, tiled=True)]
    unnamed x69 -> x64, local copies, waits for them, and re-layouts: 4.17 us -> 5.48 us
  transfers between devices with their start and end apart: 16 -> 16, of which waited for: 7 -> 5; matrix products, arithmetic and copies ran while one was open for 8% -> 10% of each run, Pallas kernels for 0% -> 0%
where the time goes in v6:
time: 253 us; the launch traced here: 252 us
  blocking collectives  76.9 us (30%)
  waiting for transfers between devices  63.3 us (25%)
  starting transfers between devices  55 us (22%)
  between operations  19.2 us (8%)
  local copies, waits for them, and re-layouts  16.6 us (7%)
  matrix products  11.1 us (4%)
  other arithmetic  9.38 us (4%)
    all_to_all x1, blocking collectives, exchange(): return lax.all_to_all(blocks, axis, split_axis=0, concat_axis=0, tiled=True)  35.5 us
    all_to_all x6, starting transfers between devices, exchange(): return lax.all_to_all(blocks, axis, split_axis=0, concat_axis=0, tiled=True)  33.8 us
    reduce_scatter x1, waiting for transfers between devices, shards(): summed = lax.psum_scatter(base, TP, scatter_dimension=0, tiled=True)  28.1 us
    all_to_all x6, waiting for transfers between devices, exchange(): return lax.all_to_all(blocks, axis, split_axis=0, concat_axis=0, tiled=True)  26.5 us
    all_gather x1, blocking collectives, shards(): lax.all_gather(projector_grad, 'y', axis=1, tiled=True).astype(f32)  14.2 us
    all_gather x1, blocking collectives, shards(): lax.all_gather(after(grad_full, all_frames), 'y', axis=0, tiled=True)  13.8 us
    all_gather x1, blocking collectives, shards(): weights = lax.all_gather(weights, 'x')  13.4 us
    dot_general x17, matrix products, dot(): lax.dot_general(a, b, (((ca,), (cb,)), ((), ())), preferred_element_type=...  11.1 us
  transfers between devices with their start and end apart: 16, of which 5 were waited for; matrix products, arithmetic and copies ran while one was open for 10% of the time, Pallas kernels for 0%

profile of v6, /device:TPU:2, one launch (start us, length us, event | category | flops | bytes accessed | tf_op | source)
XLA Modules:
  0.0 251.5 jit_solution(15844560568495834469)
XLA Ops:
  9.6 2.2 convolution_convert_fusion
  12.8 5.1 %collective-permute-start.1 = (bf16[640,128]{1,0:T(8,128)(2,1)S(1)}, bf16[640,128]{1,0:T(8,128)(2,1)S(1)}, u32[]{:S(2)}, u32[]{:S(2)}) collective-permute-start(bf16[640,128]{1,0:T(8,128)(2,1)S(1)} %get-tuple-element.26), channel_id=1, source_target_pairs={{0,16},{8,24},{16,0},{24,8},{1,17},{9,25},{17,1},{25,9},{2,18},{10... | collective-permute-start | bytes 491528 | tf_op jit(solution)/shard_map/ppermute | solution.py:127
  17.9 3.0 %collective-permute-start.2 = (bf16[640,128]{1,0:T(8,128)(2,1)S(1)}, bf16[640,128]{1,0:T(8,128)(2,1)S(1)}, u32[]{:S(2)}, u32[]{:S(2)}) collective-permute-start(bf16[640,128]{1,0:T(8,128)(2,1)S(1)} %get-tuple-element.27), channel_id=1, source_target_pairs={{0,24},{8,0},{16,8},{24,16},{1,25},{9,1},{17,9},{25,17},{2,26},{10... | collective-permute-start | bytes 491528 | tf_op jit(solution)/shard_map/ppermute | solution.py:127
  20.9 2.9 %collective-permute-start = (bf16[640,128]{1,0:T(8,128)(2,1)S(1)}, bf16[640,128]{1,0:T(8,128)(2,1)S(1)}, u32[]{:S(2)}, u32[]{:S(2)}) collective-permute-start(bf16[640,128]{1,0:T(8,128)(2,1)S(1)} %get-tuple-element.25), channel_id=1, source_target_pairs={{0,8},{8,16},{16,24},{24,0},{1,9},{9,17},{17,25},{25,1},{2,10},{10... | collective-permute-start | bytes 491528 | tf_op jit(solution)/shard_map/ppermute | solution.py:127
  27.1 8.9 %all-to-all-start.1 = ((bf16[16,6,128]{2,1,0:T(8,128)(2,1)}), bf16[16,6,128]{2,1,0:T(8,128)(2,1)S(1)}, u32[]{:S(2)}, u32[]{:S(2)}) async-start(bf16[16,6,128]{2,1,0:T(8,128)(2,1)} %reshape.407), calls=%async_computation.2 | async-start | bytes 65536 | tf_op jit(solution)/shard_map/all_to_all | solution.py:18
  38.8 4.1 %all-to-all-done.1 = bf16[16,6,128]{2,1,0:T(8,128)(2,1)S(1)} async-done(((bf16[16,6,128]{2,1,0:T(8,128)(2,1)}), bf16[16,6,128]{2,1,0:T(8,128)(2,1)S(1)}, u32[]{:S(2)}, u32[]{:S(2)}) %all-to-all-start.1) | async-done | bytes 24608 | tf_op jit(solution)/shard_map/all_to_all | solution.py:18
  45.4 35.5 %all_to_all.35 = bf16[8,160,128]{2,1,0:T(8,128)(2,1)S(1)} all-to-all(bf16[8,160,128]{2,1,0:T(8,128)(2,1)S(1)} %pad_maximum_fusion.2), channel_id=1, replica_groups=mesh['zl'=4,'x'=4,'y'=4,'zh'=4,'c'=2] {'zh','c'}, dimensions={0} | all-to-all | bytes 655360 | tf_op jit(solution)/shard_map/all_to_all | solution.py:18
  81.0 13.4 %all_gather.17 = bf16[4,80,1024]{2,1,0:T(8,128)(2,1)S(1)} all-gather(bf16[1,80,1024]{2,1,0:T(8,128)(2,1)S(1)} %all_gather_reshape.3), channel_id=1, replica_groups=mesh['zl'=4,'x'=4,'y'=4,'zh'=4,'c'=2] {'x'}, dimensions={0}, use_global_device_ids=true | all-gather | bytes 819200 | tf_op jit(solution)/shard_map/all_gather | solution.py:166
  95.3 3.6 %all-to-all-start = ((bf16[4,48,1024]{2,1,0:T(8,128)(2,1)}), bf16[4,48,1024]{2,1,0:T(8,128)(2,1)S(1)}, u32[]{:S(2)}, u32[]{:S(2)}) async-start(bf16[4,48,1024]{2,1,0:T(8,128)(2,1)} %bitcast.186), calls=%async_computation.1 | async-start | bytes 786432 | tf_op jit(solution)/shard_map/all_to_all | solution.py:18
  101.3 13.8 %all_gather.16 = bf16[192,1024]{1,0:T(8,128)(2,1)S(1)} all-gather(bf16[48,1024]{1,0:T(8,128)(2,1)S(1)} %bitcast_add_fusion), channel_id=1, replica_groups=mesh['zl'=4,'x'=4,'y'=4,'zh'=4,'c'=2] {'y'}, dimensions={0}, use_global_device_ids=true | all-gather | bytes 491520 | tf_op jit(solution)/shard_map/all_gather | solution.py:164
  117.3 3.4 %all-to-all-start.3 = ((bf16[4,48,256]{2,1,0:T(8,128)(2,1)}), bf16[4,48,256]{2,1,0:T(8,128)(2,1)S(1)}, u32[]{:S(2)}, u32[]{:S(2)}) async-start(bf16[4,48,256]{2,1,0:T(8,128)(2,1)} %bitcast.29), calls=%async_computation.4 | async-start | bytes 196608 | tf_op jit(solution)/shard_map/all_to_all | solution.py:18
  120.8 6.7 %all-to-all-done.3 = bf16[4,48,256]{2,1,0:T(8,128)(2,1)S(1)} async-done(((bf16[4,48,256]{2,1,0:T(8,128)(2,1)}), bf16[4,48,256]{2,1,0:T(8,128)(2,1)S(1)}, u32[]{:S(2)}, u32[]{:S(2)}) %all-to-all-start.3) | async-done | bytes 98336 | tf_op jit(solution)/shard_map/all_to_all | solution.py:18
  129.1 4.0 %all-to-all-start.4 = ((bf16[8,88,128]{2,1,0:T(8,128)(2,1)}), bf16[8,88,128]{2,1,0:T(8,128)(2,1)}, u32[]{:S(2)}, u32[]{:S(2)}) async-start(bf16[8,88,128]{2,1,0:T(8,128)(2,1)} %broadcast_in_dim.118), calls=%async_computation.5 | async-start | bytes 360448 | tf_op jit(solution)/shard_map/all_to_all | solution.py:18
  133.4 2.4 fusion
  137.2 15.7 %all-to-all-done.4 = bf16[8,88,128]{2,1,0:T(8,128)(2,1)} async-done(((bf16[8,88,128]{2,1,0:T(8,128)(2,1)}), bf16[8,88,128]{2,1,0:T(8,128)(2,1)}, u32[]{:S(2)}, u32[]{:S(2)}) %all-to-all-start.4) | async-done | bytes 180256 | tf_op jit(solution)/shard_map/all_to_all | solution.py:18
  156.5 3.1 %collective-permute-start.5 = (bf16[80,1024]{1,0:T(8,128)(2,1)S(1)}, bf16[80,1024]{1,0:T(8,128)(2,1)S(1)}, u32[]{:S(2)}, u32[]{:S(2)}) collective-permute-start(bf16[80,1024]{1,0:T(8,128)(2,1)S(1)} %get-tuple-element.30), channel_id=1, source_target_pairs={{0,384},{128,0},{256,128},{384,256},{1,385},{129,1},{257,129},{385... | collective-permute-start | bytes 491528 | tf_op jit(solution)/shard_map/ppermute | solution.py:42
  159.6 3.5 %collective-permute-start.4 = (bf16[80,1024]{1,0:T(8,128)(2,1)S(1)}, bf16[80,1024]{1,0:T(8,128)(2,1)S(1)}, u32[]{:S(2)}, u32[]{:S(2)}) collective-permute-start(bf16[80,1024]{1,0:T(8,128)(2,1)S(1)} %get-tuple-element.31), channel_id=1, source_target_pairs={{0,256},{128,384},{256,0},{384,128},{1,257},{129,385},{257,1},{385... | collective-permute-start | bytes 491528 | tf_op jit(solution)/shard_map/ppermute | solution.py:42
  163.1 3.5 %collective-permute-start.3 = (bf16[80,1024]{1,0:T(8,128)(2,1)S(1)}, bf16[80,1024]{1,0:T(8,128)(2,1)S(1)}, u32[]{:S(2)}, u32[]{:S(2)}) collective-permute-start(bf16[80,1024]{1,0:T(8,128)(2,1)S(1)} %get-tuple-element.29), channel_id=1, source_target_pairs={{0,128},{128,256},{256,384},{384,0},{1,129},{129,257},{257,385},{3... | collective-permute-start | bytes 491528 | tf_op jit(solution)/shard_map/ppermute | solution.py:42
  166.8 8.1 %collective-permute-done.4 = bf16[80,1024]{1,0:T(8,128)(2,1)S(1)} collective-permute-done((bf16[80,1024]{1,0:T(8,128)(2,1)S(1)}, bf16[80,1024]{1,0:T(8,128)(2,1)S(1)}, u32[]{:S(2)}, u32[]{:S(2)}) %collective-permute-start.4) | collective-permute-done | bytes 163872 | tf_op jit(solution)/shard_map/ppermute | solution.py:42
  175.6 1.9 maximum_maximum_fusion
  177.5 6.1 %all-to-all-start.5 = ((bf16[16,200,256]{2,1,0:T(8,128)(2,1)}), bf16[16,200,256]{2,1,0:T(8,128)(2,1)S(1)}, u32[]{:S(2)}, u32[]{:S(2)}) async-start(bf16[16,200,256]{2,1,0:T(8,128)(2,1)} %maximum_maximum_fusion), calls=%async_computation.6 | async-start | bytes 3276800 | tf_op jit(solution)/shard_map/all_to_all | solution.py:18
  183.7 28.1 %reduce-scatter.5.cloned.1.call-done = bf16[304,128]{1,0:T(8,128)(2,1)} async-done(((bf16[2432,128]{1,0:T(8,128)(2,1)}), bf16[304,128]{1,0:T(8,128)(2,1)}) %reduce-scatter.5.cloned.1.call-update) | async-done | bytes 77840 | tf_op jit(solution)/shard_map/reduce_scatter | solution.py:199
  214.1 7.7 %all-to-all-start.6 = ((bf16[64,15,128]{2,1,0:T(8,128)(2,1)}), bf16[64,15,128]{2,1,0:T(8,128)(2,1)S(1)}, u32[]{:S(2)}, u32[]{:S(2)}) async-start(bf16[64,15,128]{2,1,0:T(8,128)(2,1)} %pad_maximum_fusion.3), calls=%async_computation.8 | async-start | bytes 524288 | tf_op jit(solution)/shard_map/all_to_all | solution.py:18
  226.4 14.2 %all_gather.19 = bf16[320,1024]{1,0:T(8,128)(2,1)S(1)} all-gather(bf16[320,256]{1,0:T(8,128)(2,1)S(1)} %fusion.2), channel_id=1, replica_groups=mesh['zl'=4,'x'=4,'y'=4,'zh'=4,'c'=2] {'y'}, dimensions={1}, use_global_device_ids=true | all-gather | bytes 819200 | tf_op jit(solution)/shard_map/all_gather | solution.py:239
  (213 shorter events, 31.5 us)
Async XLA Ops:
  8.0 87.3 %reduce-scatter.3.cloned.1.call-start = ((), (), s32[]{:S(2)}) async-start(), calls=%async_computation.9 | async-start | bytes 1966080 | tf_op jit(solution)/shard_map/reduce_scatter | solution.py:85
  11.8 26.8 %copy-start.12 = (bf16[64,128]{1,0:T(8,128)(2,1)S(1)}, bf16[64,128]{1,0:T(8,128)(2,1)}, u32[]{:S(2)}) copy-start(bf16[64,128]{1,0:T(8,128)(2,1)} %param.18) | copy-start | bytes 49156
  12.8 30.3 %collective-permute-start.1 = (bf16[640,128]{1,0:T(8,128)(2,1)S(1)}, bf16[640,128]{1,0:T(8,128)(2,1)S(1)}, u32[]{:S(2)}, u32[]{:S(2)}) collective-permute-start(bf16[640,128]{1,0:T(8,128)(2,1)S(1)} %get-tuple-element.26), channel_id=1, source_target_pairs={{0,16},{8,24},{16,0},{24,8},{1,17},{9,25},{17,1},{25,9},{2,18},{10... | collective-permute-start | bytes 491528 | tf_op jit(solution)/shard_map/ppermute | solution.py:127
  17.9 25.2 %collective-permute-start.2 = (bf16[640,128]{1,0:T(8,128)(2,1)S(1)}, bf16[640,128]{1,0:T(8,128)(2,1)S(1)}, u32[]{:S(2)}, u32[]{:S(2)}) collective-permute-start(bf16[640,128]{1,0:T(8,128)(2,1)S(1)} %get-tuple-element.27), channel_id=1, source_target_pairs={{0,24},{8,0},{16,8},{24,16},{1,25},{9,1},{17,9},{25,17},{2,26},{10... | collective-permute-start | bytes 491528 | tf_op jit(solution)/shard_map/ppermute | solution.py:127
  20.9 22.3 %collective-permute-start = (bf16[640,128]{1,0:T(8,128)(2,1)S(1)}, bf16[640,128]{1,0:T(8,128)(2,1)S(1)}, u32[]{:S(2)}, u32[]{:S(2)}) collective-permute-start(bf16[640,128]{1,0:T(8,128)(2,1)S(1)} %get-tuple-element.25), channel_id=1, source_target_pairs={{0,8},{8,16},{16,24},{24,0},{1,9},{9,17},{17,25},{25,1},{2,10},{10... | collective-permute-start | bytes 491528 | tf_op jit(solution)/shard_map/ppermute | solution.py:127
  27.1 15.8 %all-to-all-start.1 = ((bf16[16,6,128]{2,1,0:T(8,128)(2,1)}), bf16[16,6,128]{2,1,0:T(8,128)(2,1)S(1)}, u32[]{:S(2)}, u32[]{:S(2)}) async-start(bf16[16,6,128]{2,1,0:T(8,128)(2,1)} %reshape.407), calls=%async_computation.2 | async-start | bytes 65536 | tf_op jit(solution)/shard_map/all_to_all | solution.py:18
  36.0 63.5 %all-gather.3.cloned.1.call-start = ((), (), s32[]{:S(2)}) async-start(), calls=%async_computation.10 | async-start | bytes 2949120 | tf_op jit(solution)/shard_map/all_gather | solution.py:86
  36.5 96.9 %all-gather.5.cloned.1.call-start = ((), (), s32[]{:S(2)}) async-start(), calls=%async_computation.11 | async-start | bytes 2621440 | tf_op jit(solution)/shard_map/all_gather | solution.py:174
  95.3 19.7 %all-to-all-start = ((bf16[4,48,1024]{2,1,0:T(8,128)(2,1)}), bf16[4,48,1024]{2,1,0:T(8,128)(2,1)S(1)}, u32[]{:S(2)}, u32[]{:S(2)}) async-start(bf16[4,48,1024]{2,1,0:T(8,128)(2,1)} %bitcast.186), calls=%async_computation.1 | async-start | bytes 786432 | tf_op jit(solution)/shard_map/all_to_all | solution.py:18
  117.3 10.2 %all-to-all-start.3 = ((bf16[4,48,256]{2,1,0:T(8,128)(2,1)}), bf16[4,48,256]{2,1,0:T(8,128)(2,1)S(1)}, u32[]{:S(2)}, u32[]{:S(2)}) async-start(bf16[4,48,256]{2,1,0:T(8,128)(2,1)} %bitcast.29), calls=%async_computation.4 | async-start | bytes 196608 | tf_op jit(solution)/shard_map/all_to_all | solution.py:18
  129.1 23.8 %all-to-all-start.4 = ((bf16[8,88,128]{2,1,0:T(8,128)(2,1)}), bf16[8,88,128]{2,1,0:T(8,128)(2,1)}, u32[]{:S(2)}, u32[]{:S(2)}) async-start(bf16[8,88,128]{2,1,0:T(8,128)(2,1)} %broadcast_in_dim.118), calls=%async_computation.5 | async-start | bytes 360448 | tf_op jit(solution)/shard_map/all_to_all | solution.py:18
  133.2 78.6 %reduce-scatter.5.cloned.1.call-start = ((), (), s32[]{:S(2)}) async-start(), calls=%async_computation.12 | async-start | bytes 700416 | tf_op jit(solution)/shard_map/reduce_scatter | solution.py:199
  156.5 10.3 %collective-permute-start.5 = (bf16[80,1024]{1,0:T(8,128)(2,1)S(1)}, bf16[80,1024]{1,0:T(8,128)(2,1)S(1)}, u32[]{:S(2)}, u32[]{:S(2)}) collective-permute-start(bf16[80,1024]{1,0:T(8,128)(2,1)S(1)} %get-tuple-element.30), channel_id=1, source_target_pairs={{0,384},{128,0},{256,128},{384,256},{1,385},{129,1},{257,129},{385... | collective-permute-start | bytes 491528 | tf_op jit(solution)/shard_map/ppermute | solution.py:42
  159.6 15.3 %collective-permute-start.4 = (bf16[80,1024]{1,0:T(8,128)(2,1)S(1)}, bf16[80,1024]{1,0:T(8,128)(2,1)S(1)}, u32[]{:S(2)}, u32[]{:S(2)}) collective-permute-start(bf16[80,1024]{1,0:T(8,128)(2,1)S(1)} %get-tuple-element.31), channel_id=1, source_target_pairs={{0,256},{128,384},{256,0},{384,128},{1,257},{129,385},{257,1},{385... | collective-permute-start | bytes 491528 | tf_op jit(solution)/shard_map/ppermute | solution.py:42
  163.1 11.8 %collective-permute-start.3 = (bf16[80,1024]{1,0:T(8,128)(2,1)S(1)}, bf16[80,1024]{1,0:T(8,128)(2,1)S(1)}, u32[]{:S(2)}, u32[]{:S(2)}) collective-permute-start(bf16[80,1024]{1,0:T(8,128)(2,1)S(1)} %get-tuple-element.29), channel_id=1, source_target_pairs={{0,128},{128,256},{256,384},{384,0},{1,129},{129,257},{257,385},{3... | collective-permute-start | bytes 491528 | tf_op jit(solution)/shard_map/ppermute | solution.py:42
  177.5 34.2 %copy-start.9 = (f32[256,64]{1,0:T(8,128)S(1)}, f32[256,64]{1,0:T(8,128)}, u32[]{:S(2)}) copy-start(f32[256,64]{1,0:T(8,128)} %copy-done.8) | copy-start | bytes 196612
  177.5 34.2 %copy-start.13 = (bf16[64,128]{1,0:T(8,128)(2,1)S(1)}, bf16[64,128]{1,0:T(8,128)(2,1)}, u32[]{:S(2)}) copy-start(bf16[64,128]{1,0:T(8,128)(2,1)} %param.18) | copy-start | bytes 49156
  177.5 34.2 %copy-start.15 = (f32[48,64]{1,0:T(8,128)S(1)}, f32[48,64]{1,0:T(8,128)}, u32[]{:S(2)}) copy-start(f32[48,64]{1,0:T(8,128)} %copy-done.14) | copy-start | bytes 36868
  177.5 34.2 %copy-start.19 = (f32[304]{0:T(512)S(1)}, f32[304]{0:T(512)}, u32[]{:S(2)}) copy-start(f32[304]{0:T(512)} %copy-done.18) | copy-start | bytes 3652
  177.5 35.4 %copy-start.26 = (s32[96]{0:T(128)S(1)}, s32[96]{0:T(128)}, u32[]{:S(2)}) copy-start(s32[96]{0:T(128)} %get-tuple-element.47) | copy-start | bytes 1156
  177.5 35.4 %copy-start.27 = (pred[96]{0:T(512)(128)(4,1)S(1)}, pred[96]{0:T(512)(128)(4,1)}, u32[]{:S(2)}) copy-start(pred[96]{0:T(512)(128)(4,1)} %get-tuple-element.45) | copy-start | bytes 292
  177.5 35.6 %all-to-all-start.5 = ((bf16[16,200,256]{2,1,0:T(8,128)(2,1)}), bf16[16,200,256]{2,1,0:T(8,128)(2,1)S(1)}, u32[]{:S(2)}, u32[]{:S(2)}) async-start(bf16[16,200,256]{2,1,0:T(8,128)(2,1)} %maximum_maximum_fusion), calls=%async_computation.6 | async-start | bytes 3276800 | tf_op jit(solution)/shard_map/all_to_all | solution.py:18
  183.7 38.1 %copy-start.7 = (pred[256,16,6]{0,2,1:T(8,128)(4,1)S(1)}, pred[256,16,6]{0,2,1:T(8,128)(4,1)}, u32[]{:S(2)}) copy-start(pred[256,16,6]{0,2,1:T(8,128)(4,1)} %get-tuple-element.37) | copy-start | bytes 73732
  214.1 27.7 %all-to-all-start.6 = ((bf16[64,15,128]{2,1,0:T(8,128)(2,1)}), bf16[64,15,128]{2,1,0:T(8,128)(2,1)S(1)}, u32[]{:S(2)}, u32[]{:S(2)}) async-start(bf16[64,15,128]{2,1,0:T(8,128)(2,1)} %pad_maximum_fusion.3), calls=%async_computation.8 | async-start | bytes 524288 | tf_op jit(solution)/shard_map/all_to_all | solution.py:18
  (21 other events, 168.2 us)
Sparse Core Ops, SparseCore 0:
  11.9 36.9 reduce-scatter.2
  166.9 44.7 reduce-scatter.4
Sparse Core Ops, SparseCore 1:
  39.1 41.3 all-gather.2
  95.3 33.0 all-gather.4

commit v7 on v6

--- a/solution.py
+++ b/solution.py
@@ -161,7 +161,7 @@
     scaled = wide * gain[None, :]
 
     grad_full = jnp.moveaxis(came[:, at : at + n_frames], 0, 1).reshape(n_frames, nt * cols)
-    grad_all = lax.all_gather(after(grad_full, all_frames), "y", axis=0, tiled=True)
+    grad_all = lax.all_gather(grad_full, "y", axis=0, tiled=True)
     weights = jnp.moveaxis(came[:, :at], 0, 1).reshape(at, nt * cols)
     weights = lax.all_gather(weights, "x")
     up_full = weights[:, piece:].reshape(rank, nt * cols)

time: 253 us -> 248 us (0.980)
    reduce_scatter x1, waiting for transfers between devices: 28.1 us -> 2.16 us  [shards(): summed = lax.psum_scatter(base, TP, scatter_dimension=0, tiled=True)]
    all_to_all x6, waiting for transfers between devices: 26.5 us -> 44.5 us  [exchange(): return lax.all_to_all(blocks, axis, split_axis=0, concat_axis=0, tiled=True)]
    ppermute x3, waiting for transfers between devices: 8.15 us -> 14.4 us  [to_peers(): lax.ppermute(blocks(lax.rem(me + k, n)), axis, [(i, (i + k) % n) for i in...]
    unnamed x64 -> x32, local copies, waits for them, and re-layouts: 5.48 us -> 3.02 us
  transfers between devices with their start and end apart: 16 -> 16, of which waited for: 5 -> 6; matrix products, arithmetic and copies ran while one was open for 10% -> 12% of each run, Pallas kernels for 0% -> 0%
where the time goes in v7:
time: 248 us; the launch traced here: 247 us
  blocking collectives  75.3 us (30%)
  waiting for transfers between devices  61.2 us (25%)
  starting transfers between devices  56.6 us (23%)
  between operations  18.4 us (7%)
  local copies, waits for them, and re-layouts  14.8 us (6%)
  matrix products  13.3 us (5%)
  other arithmetic  7.26 us (3%)
    all_to_all x6, waiting for transfers between devices, exchange(): return lax.all_to_all(blocks, axis, split_axis=0, concat_axis=0, tiled=True)  44.5 us
    all_to_all x1, blocking collectives, exchange(): return lax.all_to_all(blocks, axis, split_axis=0, concat_axis=0, tiled=True)  35.8 us
    all_to_all x6, starting transfers between devices, exchange(): return lax.all_to_all(blocks, axis, split_axis=0, concat_axis=0, tiled=True)  35.4 us
    ppermute x3, waiting for transfers between devices, to_peers(): lax.ppermute(blocks(lax.rem(me + k, n)), axis, [(i, (i + k) % n) for i in...  14.4 us
    all_gather x1, blocking collectives, shards(): lax.all_gather(projector_grad, 'y', axis=1, tiled=True).astype(f32)  14.1 us
    all_gather x1, blocking collectives, shards(): grad_all = lax.all_gather(grad_full, 'y', axis=0, tiled=True)  13.7 us
    dot_general x17, matrix products, dot(): lax.dot_general(a, b, (((ca,), (cb,)), ((), ())), preferred_element_type=...  13.3 us
    all_gather x1, blocking collectives, shards(): weights = lax.all_gather(weights, 'x')  11.8 us
  transfers between devices with their start and end apart: 16, of which 6 were waited for; matrix products, arithmetic and copies ran while one was open for 12% of the time, Pallas kernels for 0%

profile of v7, /device:TPU:2, one launch (start us, length us, event | category | flops | bytes accessed | tf_op | source)
XLA Modules:
  0.0 246.9 jit_solution(11273466182231475390)
XLA Ops:
  10.1 5.1 %collective-permute-start.1 = (bf16[640,128]{1,0:T(8,128)(2,1)S(1)}, bf16[640,128]{1,0:T(8,128)(2,1)S(1)}, u32[]{:S(2)}, u32[]{:S(2)}) collective-permute-start(bf16[640,128]{1,0:T(8,128)(2,1)S(1)} %get-tuple-element.26), channel_id=1, source_target_pairs={{0,16},{8,24},{16,0},{24,8},{1,17},{9,25},{17,1},{25,9},{2,18},{10... | collective-permute-start | bytes 491528 | tf_op jit(solution)/shard_map/ppermute | solution.py:127
  15.2 3.0 %collective-permute-start.2 = (bf16[640,128]{1,0:T(8,128)(2,1)S(1)}, bf16[640,128]{1,0:T(8,128)(2,1)S(1)}, u32[]{:S(2)}, u32[]{:S(2)}) collective-permute-start(bf16[640,128]{1,0:T(8,128)(2,1)S(1)} %get-tuple-element.27), channel_id=1, source_target_pairs={{0,24},{8,0},{16,8},{24,16},{1,25},{9,1},{17,9},{25,17},{2,26},{10... | collective-permute-start | bytes 491528 | tf_op jit(solution)/shard_map/ppermute | solution.py:127
  18.2 2.9 %collective-permute-start = (bf16[640,128]{1,0:T(8,128)(2,1)S(1)}, bf16[640,128]{1,0:T(8,128)(2,1)S(1)}, u32[]{:S(2)}, u32[]{:S(2)}) collective-permute-start(bf16[640,128]{1,0:T(8,128)(2,1)S(1)} %get-tuple-element.25), channel_id=1, source_target_pairs={{0,8},{8,16},{16,24},{24,0},{1,9},{9,17},{17,25},{25,1},{2,10},{10... | collective-permute-start | bytes 491528 | tf_op jit(solution)/shard_map/ppermute | solution.py:127
  23.8 8.9 %all-to-all-start.1 = ((bf16[16,6,128]{2,1,0:T(8,128)(2,1)}), bf16[16,6,128]{2,1,0:T(8,128)(2,1)S(1)}, u32[]{:S(2)}, u32[]{:S(2)}) async-start(bf16[16,6,128]{2,1,0:T(8,128)(2,1)} %reshape.405), calls=%async_computation.2 | async-start | bytes 65536 | tf_op jit(solution)/shard_map/all_to_all | solution.py:18
  37.0 2.5 %all-to-all-done.1 = bf16[16,6,128]{2,1,0:T(8,128)(2,1)S(1)} async-done(((bf16[16,6,128]{2,1,0:T(8,128)(2,1)}), bf16[16,6,128]{2,1,0:T(8,128)(2,1)S(1)}, u32[]{:S(2)}, u32[]{:S(2)}) %all-to-all-start.1) | async-done | bytes 24608 | tf_op jit(solution)/shard_map/all_to_all | solution.py:18
  41.4 35.8 %all_to_all.35 = bf16[8,160,128]{2,1,0:T(8,128)(2,1)S(1)} all-to-all(bf16[8,160,128]{2,1,0:T(8,128)(2,1)S(1)} %pad_maximum_fusion.2), channel_id=1, replica_groups=mesh['zl'=4,'x'=4,'y'=4,'zh'=4,'c'=2] {'zh','c'}, dimensions={0} | all-to-all | bytes 655360 | tf_op jit(solution)/shard_map/all_to_all | solution.py:18
  77.3 11.8 %all_gather.16 = bf16[4,80,1024]{2,1,0:T(8,128)(2,1)S(1)} all-gather(bf16[1,80,1024]{2,1,0:T(8,128)(2,1)S(1)} %all_gather_reshape.3), channel_id=1, replica_groups=mesh['zl'=4,'x'=4,'y'=4,'zh'=4,'c'=2] {'x'}, dimensions={0}, use_global_device_ids=true | all-gather | bytes 819200 | tf_op jit(solution)/shard_map/all_gather | solution.py:166
  90.1 5.7 %all-to-all-start = ((bf16[4,48,1024]{2,1,0:T(8,128)(2,1)}), bf16[4,48,1024]{2,1,0:T(8,128)(2,1)S(1)}, u32[]{:S(2)}, u32[]{:S(2)}) async-start(bf16[4,48,1024]{2,1,0:T(8,128)(2,1)} %bitcast.184), calls=%async_computation.1 | async-start | bytes 786432 | tf_op jit(solution)/shard_map/all_to_all | solution.py:18
  96.1 13.7 %all_gather.15 = bf16[192,1024]{1,0:T(8,128)(2,1)S(1)} all-gather(bf16[48,1024]{1,0:T(8,128)(2,1)S(1)} %copy_bitcast_fusion.1), channel_id=1, replica_groups=mesh['zl'=4,'x'=4,'y'=4,'zh'=4,'c'=2] {'y'}, dimensions={0}, use_global_device_ids=true | all-gather | bytes 491520 | tf_op jit(solution)/shard_map/all_gather | solution.py:164
  112.1 3.4 %all-to-all-start.3 = ((bf16[4,48,256]{2,1,0:T(8,128)(2,1)}), bf16[4,48,256]{2,1,0:T(8,128)(2,1)S(1)}, u32[]{:S(2)}, u32[]{:S(2)}) async-start(bf16[4,48,256]{2,1,0:T(8,128)(2,1)} %bitcast.28), calls=%async_computation.4 | async-start | bytes 196608 | tf_op jit(solution)/shard_map/all_to_all | solution.py:18
  115.8 6.7 %all-to-all-done.3 = bf16[4,48,256]{2,1,0:T(8,128)(2,1)S(1)} async-done(((bf16[4,48,256]{2,1,0:T(8,128)(2,1)}), bf16[4,48,256]{2,1,0:T(8,128)(2,1)S(1)}, u32[]{:S(2)}, u32[]{:S(2)}) %all-to-all-start.3) | async-done | bytes 98336 | tf_op jit(solution)/shard_map/all_to_all | solution.py:18
  124.0 3.4 %all-to-all-start.4 = ((bf16[8,88,128]{2,1,0:T(8,128)(2,1)}), bf16[8,88,128]{2,1,0:T(8,128)(2,1)S(1)}, u32[]{:S(2)}, u32[]{:S(2)}) async-start(bf16[8,88,128]{2,1,0:T(8,128)(2,1)} %broadcast_in_dim.118), calls=%async_computation.5 | async-start | bytes 360448 | tf_op jit(solution)/shard_map/all_to_all | solution.py:18
  127.7 2.4 fusion
  133.0 14.1 %all-to-all-done.4 = bf16[8,88,128]{2,1,0:T(8,128)(2,1)S(1)} async-done(((bf16[8,88,128]{2,1,0:T(8,128)(2,1)}), bf16[8,88,128]{2,1,0:T(8,128)(2,1)S(1)}, u32[]{:S(2)}, u32[]{:S(2)}) %all-to-all-start.4) | async-done | bytes 180256 | tf_op jit(solution)/shard_map/all_to_all | solution.py:18
  148.5 2.8 %collective-permute-start.5 = (bf16[80,1024]{1,0:T(8,128)(2,1)S(1)}, bf16[80,1024]{1,0:T(8,128)(2,1)S(1)}, u32[]{:S(2)}, u32[]{:S(2)}) collective-permute-start(bf16[80,1024]{1,0:T(8,128)(2,1)S(1)} %get-tuple-element.30), channel_id=1, source_target_pairs={{0,384},{128,0},{256,128},{384,256},{1,385},{129,1},{257,129},{385... | collective-permute-start | bytes 491528 | tf_op jit(solution)/shard_map/ppermute | solution.py:42
  151.3 3.5 %collective-permute-start.4 = (bf16[80,1024]{1,0:T(8,128)(2,1)S(1)}, bf16[80,1024]{1,0:T(8,128)(2,1)S(1)}, u32[]{:S(2)}, u32[]{:S(2)}) collective-permute-start(bf16[80,1024]{1,0:T(8,128)(2,1)S(1)} %get-tuple-element.31), channel_id=1, source_target_pairs={{0,256},{128,384},{256,0},{384,128},{1,257},{129,385},{257,1},{385... | collective-permute-start | bytes 491528 | tf_op jit(solution)/shard_map/ppermute | solution.py:42
  154.9 3.8 %collective-permute-start.3 = (bf16[80,1024]{1,0:T(8,128)(2,1)S(1)}, bf16[80,1024]{1,0:T(8,128)(2,1)S(1)}, u32[]{:S(2)}, u32[]{:S(2)}) collective-permute-start(bf16[80,1024]{1,0:T(8,128)(2,1)S(1)} %get-tuple-element.29), channel_id=1, source_target_pairs={{0,128},{128,256},{256,384},{384,0},{1,129},{129,257},{257,385},{3... | collective-permute-start | bytes 491528 | tf_op jit(solution)/shard_map/ppermute | solution.py:42
  158.8 14.4 %collective-permute-done.4 = bf16[80,1024]{1,0:T(8,128)(2,1)S(1)} collective-permute-done((bf16[80,1024]{1,0:T(8,128)(2,1)S(1)}, bf16[80,1024]{1,0:T(8,128)(2,1)S(1)}, u32[]{:S(2)}, u32[]{:S(2)}) %collective-permute-start.4) | collective-permute-done | bytes 163872 | tf_op jit(solution)/shard_map/ppermute | solution.py:42
  175.7 6.1 %all-to-all-start.5 = ((bf16[16,200,256]{2,1,0:T(8,128)(2,1)}), bf16[16,200,256]{2,1,0:T(8,128)(2,1)S(1)}, u32[]{:S(2)}, u32[]{:S(2)}) async-start(bf16[16,200,256]{2,1,0:T(8,128)(2,1)} %maximum_maximum_fusion), calls=%async_computation.6 | async-start | bytes 3276800 | tf_op jit(solution)/shard_map/all_to_all | solution.py:18
  181.8 2.2 reduce-scatter.5.cloned.1.call-done
  185.4 21.3 %all-to-all-done.5 = bf16[16,200,256]{2,1,0:T(8,128)(2,1)S(1)} async-done(((bf16[16,200,256]{2,1,0:T(8,128)(2,1)}), bf16[16,200,256]{2,1,0:T(8,128)(2,1)S(1)}, u32[]{:S(2)}, u32[]{:S(2)}) %all-to-all-start.5) | async-done | bytes 1638432 | tf_op jit(solution)/shard_map/all_to_all | solution.py:18
  207.6 7.9 %all-to-all-start.6 = ((bf16[64,15,128]{2,1,0:T(8,128)(2,1)}), bf16[64,15,128]{2,1,0:T(8,128)(2,1)S(1)}, u32[]{:S(2)}, u32[]{:S(2)}) async-start(bf16[64,15,128]{2,1,0:T(8,128)(2,1)} %pad_maximum_fusion.3), calls=%async_computation.8 | async-start | bytes 524288 | tf_op jit(solution)/shard_map/all_to_all | solution.py:18
  218.7 3.1 %fusion.2 = bf16[320,256]{1,0:T(8,128)(2,1)S(1)} fusion(bf16[3072,256]{1,0:T(8,128)(2,1)} %bitcast.169, bf16[3072,320]{1,0:T(8,128)(2,1)} %all-gather.5.cloned.1.call-done, f32[]{:T(128)S(6)} %convert.13), kind=kOutput, calls=%fused_computation.12 | convolution fusion | flops 503480320 | bytes 3702788 | tf_op jit(solution)/shard_map/dot_general | solution.py:14
  221.9 14.1 %all_gather.19 = bf16[320,1024]{1,0:T(8,128)(2,1)S(1)} all-gather(bf16[320,256]{1,0:T(8,128)(2,1)S(1)} %fusion.2), channel_id=1, replica_groups=mesh['zl'=4,'x'=4,'y'=4,'zh'=4,'c'=2] {'y'}, dimensions={1}, use_global_device_ids=true | all-gather | bytes 819200 | tf_op jit(solution)/shard_map/all_gather | solution.py:239
  (180 shorter events, 30.0 us)
Async XLA Ops:
  8.0 25.2 %copy-start = (bf16[320,1024]{1,0:T(8,128)(2,1)S(1)}, bf16[320,1024]{1,0:T(8,128)(2,1)}, u32[]{:S(2)}) copy-start(bf16[320,1024]{1,0:T(8,128)(2,1)} %param.13) | copy-start | bytes 1966084
  8.0 13.1 %copy-start.8 = (s32[1,16,16]{2,1,0:T(8,128)S(1)}, s32[1,16,16]{2,1,0:T(8,128)}, u32[]{:S(2)}) copy-start(s32[1,16,16]{2,1,0:T(8,128)} %param.19) | copy-start | bytes 3076
  8.0 13.1 %copy-start.9 = (s32[1,16,16]{2,1,0:T(8,128)S(1)}, s32[1,16,16]{2,1,0:T(8,128)}, u32[]{:S(2)}) copy-start(s32[1,16,16]{2,1,0:T(8,128)} %param.20) | copy-start | bytes 3076
  8.0 14.1 %copy-start.10 = (s32[256]{0:T(256)S(1)}, s32[256]{0:T(256)}, u32[]{:S(2)}) copy-start(s32[256]{0:T(256)} %param.22) | copy-start | bytes 3076
  8.0 14.1 %copy-start.11 = (s32[256]{0:T(256)S(1)}, s32[256]{0:T(256)}, u32[]{:S(2)}) copy-start(s32[256]{0:T(256)} %param.21) | copy-start | bytes 3076
  8.1 14.8 %copy-start.5 = (bf16[256,128]{1,0:T(8,128)(2,1)S(1)}, bf16[256,128]{1,0:T(8,128)(2,1)}, u32[]{:S(2)}) copy-start(bf16[256,128]{1,0:T(8,128)(2,1)} %param.23) | copy-start | bytes 196612
  8.1 24.7 %copy-start.4 = (bf16[768,320]{0,1:T(8,128)(2,1)S(1)}, bf16[768,320]{0,1:T(8,128)(2,1)}, u32[]{:S(2)}) copy-start(bf16[768,320]{0,1:T(8,128)(2,1)} %param.12) | copy-start | bytes 1474564
  10.1 29.6 %collective-permute-start.1 = (bf16[640,128]{1,0:T(8,128)(2,1)S(1)}, bf16[640,128]{1,0:T(8,128)(2,1)S(1)}, u32[]{:S(2)}, u32[]{:S(2)}) collective-permute-start(bf16[640,128]{1,0:T(8,128)(2,1)S(1)} %get-tuple-element.26), channel_id=1, source_target_pairs={{0,16},{8,24},{16,0},{24,8},{1,17},{9,25},{17,1},{25,9},{2,18},{10... | collective-permute-start | bytes 491528 | tf_op jit(solution)/shard_map/ppermute | solution.py:127
  15.2 24.5 %collective-permute-start.2 = (bf16[640,128]{1,0:T(8,128)(2,1)S(1)}, bf16[640,128]{1,0:T(8,128)(2,1)S(1)}, u32[]{:S(2)}, u32[]{:S(2)}) collective-permute-start(bf16[640,128]{1,0:T(8,128)(2,1)S(1)} %get-tuple-element.27), channel_id=1, source_target_pairs={{0,24},{8,0},{16,8},{24,16},{1,25},{9,1},{17,9},{25,17},{2,26},{10... | collective-permute-start | bytes 491528 | tf_op jit(solution)/shard_map/ppermute | solution.py:127
  18.2 21.6 %collective-permute-start = (bf16[640,128]{1,0:T(8,128)(2,1)S(1)}, bf16[640,128]{1,0:T(8,128)(2,1)S(1)}, u32[]{:S(2)}, u32[]{:S(2)}) collective-permute-start(bf16[640,128]{1,0:T(8,128)(2,1)S(1)} %get-tuple-element.25), channel_id=1, source_target_pairs={{0,8},{8,16},{16,24},{24,0},{1,9},{9,17},{17,25},{25,1},{2,10},{10... | collective-permute-start | bytes 491528 | tf_op jit(solution)/shard_map/ppermute | solution.py:127
  23.8 15.7 %all-to-all-start.1 = ((bf16[16,6,128]{2,1,0:T(8,128)(2,1)}), bf16[16,6,128]{2,1,0:T(8,128)(2,1)S(1)}, u32[]{:S(2)}, u32[]{:S(2)}) async-start(bf16[16,6,128]{2,1,0:T(8,128)(2,1)} %reshape.405), calls=%async_computation.2 | async-start | bytes 65536 | tf_op jit(solution)/shard_map/all_to_all | solution.py:18
  32.7 57.3 %reduce-scatter.3.cloned.1.call-start = ((), (), s32[]{:S(2)}) async-start(), calls=%async_computation.9 | async-start | bytes 1966080 | tf_op jit(solution)/shard_map/reduce_scatter | solution.py:85
  35.4 92.3 %all-gather.3.cloned.1.call-start = ((), (), s32[]{:S(2)}) async-start(), calls=%async_computation.10 | async-start | bytes 2621440 | tf_op jit(solution)/shard_map/all_gather | solution.py:174
  90.0 21.1 %copy-start.1 = (bf16[4,64,1024]{2,1,0:T(8,128)(2,1)S(1)}, bf16[4,64,1024]{2,1,0:T(8,128)(2,1)}, u32[]{:S(2)}) copy-start(bf16[4,64,1024]{2,1,0:T(8,128)(2,1)} %slice.165) | copy-start | bytes 1572868
  90.1 19.8 %all-to-all-start = ((bf16[4,48,1024]{2,1,0:T(8,128)(2,1)}), bf16[4,48,1024]{2,1,0:T(8,128)(2,1)S(1)}, u32[]{:S(2)}, u32[]{:S(2)}) async-start(bf16[4,48,1024]{2,1,0:T(8,128)(2,1)} %bitcast.184), calls=%async_computation.1 | async-start | bytes 786432 | tf_op jit(solution)/shard_map/all_to_all | solution.py:18
  112.1 10.3 %all-to-all-start.3 = ((bf16[4,48,256]{2,1,0:T(8,128)(2,1)}), bf16[4,48,256]{2,1,0:T(8,128)(2,1)S(1)}, u32[]{:S(2)}, u32[]{:S(2)}) async-start(bf16[4,48,256]{2,1,0:T(8,128)(2,1)} %bitcast.28), calls=%async_computation.4 | async-start | bytes 196608 | tf_op jit(solution)/shard_map/all_to_all | solution.py:18
  124.0 23.0 %all-to-all-start.4 = ((bf16[8,88,128]{2,1,0:T(8,128)(2,1)}), bf16[8,88,128]{2,1,0:T(8,128)(2,1)S(1)}, u32[]{:S(2)}, u32[]{:S(2)}) async-start(bf16[8,88,128]{2,1,0:T(8,128)(2,1)} %broadcast_in_dim.118), calls=%async_computation.5 | async-start | bytes 360448 | tf_op jit(solution)/shard_map/all_to_all | solution.py:18
  127.4 56.6 %reduce-scatter.5.cloned.1.call-start = ((), (), s32[]{:S(2)}) async-start(), calls=%async_computation.11 | async-start | bytes 700416 | tf_op jit(solution)/shard_map/reduce_scatter | solution.py:199
  131.1 87.7 %all-gather.5.cloned.1.call-start = ((), (), s32[]{:S(2)}) async-start(), calls=%async_computation.12 | async-start | bytes 2949120 | tf_op jit(solution)/shard_map/all_gather | solution.py:86
  148.5 10.3 %collective-permute-start.5 = (bf16[80,1024]{1,0:T(8,128)(2,1)S(1)}, bf16[80,1024]{1,0:T(8,128)(2,1)S(1)}, u32[]{:S(2)}, u32[]{:S(2)}) collective-permute-start(bf16[80,1024]{1,0:T(8,128)(2,1)S(1)} %get-tuple-element.30), channel_id=1, source_target_pairs={{0,384},{128,0},{256,128},{384,256},{1,385},{129,1},{257,129},{385... | collective-permute-start | bytes 491528 | tf_op jit(solution)/shard_map/ppermute | solution.py:42
  151.3 21.9 %collective-permute-start.4 = (bf16[80,1024]{1,0:T(8,128)(2,1)S(1)}, bf16[80,1024]{1,0:T(8,128)(2,1)S(1)}, u32[]{:S(2)}, u32[]{:S(2)}) collective-permute-start(bf16[80,1024]{1,0:T(8,128)(2,1)S(1)} %get-tuple-element.31), channel_id=1, source_target_pairs={{0,256},{128,384},{256,0},{384,128},{1,257},{129,385},{257,1},{385... | collective-permute-start | bytes 491528 | tf_op jit(solution)/shard_map/ppermute | solution.py:42
  154.9 18.4 %collective-permute-start.3 = (bf16[80,1024]{1,0:T(8,128)(2,1)S(1)}, bf16[80,1024]{1,0:T(8,128)(2,1)S(1)}, u32[]{:S(2)}, u32[]{:S(2)}) collective-permute-start(bf16[80,1024]{1,0:T(8,128)(2,1)S(1)} %get-tuple-element.29), channel_id=1, source_target_pairs={{0,128},{128,256},{256,384},{384,0},{1,129},{129,257},{257,385},{3... | collective-permute-start | bytes 491528 | tf_op jit(solution)/shard_map/ppermute | solution.py:42
  175.7 30.9 %all-to-all-start.5 = ((bf16[16,200,256]{2,1,0:T(8,128)(2,1)}), bf16[16,200,256]{2,1,0:T(8,128)(2,1)S(1)}, u32[]{:S(2)}, u32[]{:S(2)}) async-start(bf16[16,200,256]{2,1,0:T(8,128)(2,1)} %maximum_maximum_fusion), calls=%async_computation.6 | async-start | bytes 3276800 | tf_op jit(solution)/shard_map/all_to_all | solution.py:18
  207.6 29.5 %all-to-all-start.6 = ((bf16[64,15,128]{2,1,0:T(8,128)(2,1)}), bf16[64,15,128]{2,1,0:T(8,128)(2,1)S(1)}, u32[]{:S(2)}, u32[]{:S(2)}) async-start(bf16[64,15,128]{2,1,0:T(8,128)(2,1)} %pad_maximum_fusion.3), calls=%async_computation.8 | async-start | bytes 524288 | tf_op jit(solution)/shard_map/all_to_all | solution.py:18
  (5 other events, 16.8 us)
Sparse Core Ops, SparseCore 0:
  36.4 33.2 reduce-scatter.2
  131.7 52.2 reduce-scatter.4
Sparse Core Ops, SparseCore 1:
  90.1 34.3 all-gather.2
  158.8 48.7 all-gather.4

commit v8 on v7

--- a/solution.py
+++ b/solution.py
@@ -34,24 +34,6 @@
 def two_halves(v):
     hi = lax.reduce_precision(v, 8, 7)
     return hi.astype(bf16), (v - hi).astype(bf16)
-
-
-def to_peers(blocks, axis):
-    n, me = lax.axis_size(axis), lax.axis_index(axis)
-    return [blocks(me)] + [
-        lax.ppermute(blocks(lax.rem(me + k, n)), axis, [(i, (i + k) % n) for i in range(n)])
-        for k in range(1, n)
-    ]
-
-
-def placed(blocks, dim, axis):
-    n, me, size = len(blocks), lax.axis_index(axis), blocks[0].shape[dim]
-    shape = list(blocks[0].shape)
-    shape[dim] *= n
-    out = jnp.zeros(shape, blocks[0].dtype)
-    for k, block in enumerate(blocks):
-        out = lax.dynamic_update_slice_in_dim(out, block, lax.rem(me - k + n, n) * size, dim)
-    return out
 
 
 def shards(
@@ -209,11 +191,9 @@
     frame_grad = (
         inv_f * gain[None, :] * grad_norm - wide * (inv_f * inv_f * inv_f * dots / full_width)
     ).astype(bf16)
-    near = to_peers(
-        lambda z: jnp.concatenate([frame_grad, lax.dynamic_index_in_dim(adapters, z, 0, False)], axis=0), "zl"
-    )
-    adapters = sum(b[n_frames:].astype(f32) for b in near).astype(bf16)
-    frame_grad = placed([b[:n_frames] for b in near], 0, "zl")
+    came = exchange(jnp.concatenate([copies(frame_grad, nzl), adapters], axis=1), "zl")
+    adapters = jnp.sum(came[:, n_frames:].astype(f32), axis=0).astype(bf16)
+    frame_grad = came[:, :n_frames]
 
     n_x = nzl * n_frames
     frame_grad = jnp.moveaxis(frame_grad.reshape(n_x, ny, quarter), 1, 0)

time: 248 us -> 245 us (0.988)
  starting transfers between devices: 56.6 us -> 49.3 us
  waiting for transfers between devices: 61.2 us -> 66.2 us
    reduce_scatter x1, waiting for transfers between devices: 2.16 us -> 22.8 us  [shards(): summed = lax.psum_scatter(base, TP, scatter_dimension=0, tiled=True)]
    ppermute x3 -> x0, waiting for transfers between devices: 14.4 us -> none  [to_peers(): lax.ppermute(blocks(lax.rem(me + k, n)), axis, [(i, (i + k) % n) for i in...]
    ppermute x3 -> x0, starting transfers between devices: 10.1 us -> none  [to_peers(): lax.ppermute(blocks(lax.rem(me + k, n)), axis, [(i, (i + k) % n) for i in...]
    all_to_all x6 -> x7, starting transfers between devices: 35.4 us -> 38.2 us  [exchange(): return lax.all_to_all(blocks, axis, split_axis=0, concat_axis=0, tiled=True)]
    all_to_all x6 -> x7, waiting for transfers between devices: 44.5 us -> 42 us  [exchange(): return lax.all_to_all(blocks, axis, split_axis=0, concat_axis=0, tiled=True)]
  transfers between devices with their start and end apart: 16 -> 14, of which waited for: 6 -> 6; matrix products, arithmetic and copies ran while one was open for 12% -> 11% of each run, Pallas kernels for 0% -> 0%
where the time goes in v8:
time: 245 us; the launch traced here: 244 us
  blocking collectives  75.6 us (31%)
  waiting for transfers between devices  66.2 us (27%)
  starting transfers between devices  49.3 us (20%)
  between operations  18.4 us (8%)
  local copies, waits for them, and re-layouts  13.3 us (5%)
  matrix products  13.2 us (5%)
  other arithmetic  8.08 us (3%)
    all_to_all x7, waiting for transfers between devices, exchange(): return lax.all_to_all(blocks, axis, split_axis=0, concat_axis=0, tiled=True)  42 us
    all_to_all x7, starting transfers between devices, exchange(): return lax.all_to_all(blocks, axis, split_axis=0, concat_axis=0, tiled=True)  38.2 us
    all_to_all x1, blocking collectives, exchange(): return lax.all_to_all(blocks, axis, split_axis=0, concat_axis=0, tiled=True)  35.7 us
    reduce_scatter x1, waiting for transfers between devices, shards(): summed = lax.psum_scatter(base, TP, scatter_dimension=0, tiled=True)  22.8 us
    all_gather x1, blocking collectives, shards(): lax.all_gather(projector_grad, 'y', axis=1, tiled=True).astype(f32)  14.4 us
    all_gather x1, blocking collectives, shards(): grad_all = lax.all_gather(grad_full, 'y', axis=0, tiled=True)  13.7 us
    dot_general x17, matrix products, dot(): lax.dot_general(a, b, (((ca,), (cb,)), ((), ())), preferred_element_type=...  13.2 us
    all_gather x1, blocking collectives, shards(): weights = lax.all_gather(weights, 'x')  11.8 us
  transfers between devices with their start and end apart: 14, of which 6 were waited for; matrix products, arithmetic and copies ran while one was open for 11% of the time, Pallas kernels for 0%

profile of v8, /device:TPU:2, one launch (start us, length us, event | category | flops | bytes accessed | tf_op | source)
XLA Modules:
  0.0 244.0 jit_solution(16889027735061551922)
XLA Ops:
  10.1 5.1 %collective-permute-start.1 = (bf16[640,128]{1,0:T(8,128)(2,1)S(1)}, bf16[640,128]{1,0:T(8,128)(2,1)S(1)}, u32[]{:S(2)}, u32[]{:S(2)}) collective-permute-start(bf16[640,128]{1,0:T(8,128)(2,1)S(1)} %get-tuple-element.21), channel_id=1, source_target_pairs={{0,16},{8,24},{16,0},{24,8},{1,17},{9,25},{17,1},{25,9},{2,18},{10... | collective-permute-start | bytes 491528 | tf_op jit(solution)/shard_map/ppermute | solution.py:109
  15.2 3.0 %collective-permute-start.2 = (bf16[640,128]{1,0:T(8,128)(2,1)S(1)}, bf16[640,128]{1,0:T(8,128)(2,1)S(1)}, u32[]{:S(2)}, u32[]{:S(2)}) collective-permute-start(bf16[640,128]{1,0:T(8,128)(2,1)S(1)} %get-tuple-element.22), channel_id=1, source_target_pairs={{0,24},{8,0},{16,8},{24,16},{1,25},{9,1},{17,9},{25,17},{2,26},{10... | collective-permute-start | bytes 491528 | tf_op jit(solution)/shard_map/ppermute | solution.py:109
  18.2 2.9 %collective-permute-start = (bf16[640,128]{1,0:T(8,128)(2,1)S(1)}, bf16[640,128]{1,0:T(8,128)(2,1)S(1)}, u32[]{:S(2)}, u32[]{:S(2)}) collective-permute-start(bf16[640,128]{1,0:T(8,128)(2,1)S(1)} %get-tuple-element.20), channel_id=1, source_target_pairs={{0,8},{8,16},{16,24},{24,0},{1,9},{9,17},{17,25},{25,1},{2,10},{10... | collective-permute-start | bytes 491528 | tf_op jit(solution)/shard_map/ppermute | solution.py:109
  23.8 8.9 %all-to-all-start.1 = ((bf16[16,6,128]{2,1,0:T(8,128)(2,1)}), bf16[16,6,128]{2,1,0:T(8,128)(2,1)S(1)}, u32[]{:S(2)}, u32[]{:S(2)}) async-start(bf16[16,6,128]{2,1,0:T(8,128)(2,1)} %reshape.404), calls=%async_computation.2 | async-start | bytes 65536 | tf_op jit(solution)/shard_map/all_to_all | solution.py:18
  33.2 2.1 convolution_convert_fusion
  36.9 2.5 %all-to-all-done.1 = bf16[16,6,128]{2,1,0:T(8,128)(2,1)S(1)} async-done(((bf16[16,6,128]{2,1,0:T(8,128)(2,1)}), bf16[16,6,128]{2,1,0:T(8,128)(2,1)S(1)}, u32[]{:S(2)}, u32[]{:S(2)}) %all-to-all-start.1) | async-done | bytes 24608 | tf_op jit(solution)/shard_map/all_to_all | solution.py:18
  41.4 35.7 %all_to_all.40 = bf16[8,160,128]{2,1,0:T(8,128)(2,1)S(1)} all-to-all(bf16[8,160,128]{2,1,0:T(8,128)(2,1)S(1)} %pad_maximum_fusion.3), channel_id=1, replica_groups=mesh['zl'=4,'x'=4,'y'=4,'zh'=4,'c'=2] {'zh','c'}, dimensions={0} | all-to-all | bytes 655360 | tf_op jit(solution)/shard_map/all_to_all | solution.py:18
  77.3 11.8 %all_gather.16 = bf16[4,80,1024]{2,1,0:T(8,128)(2,1)S(1)} all-gather(bf16[1,80,1024]{2,1,0:T(8,128)(2,1)S(1)} %all_gather_reshape.3), channel_id=1, replica_groups=mesh['zl'=4,'x'=4,'y'=4,'zh'=4,'c'=2] {'x'}, dimensions={0}, use_global_device_ids=true | all-gather | bytes 819200 | tf_op jit(solution)/shard_map/all_gather | solution.py:148
  90.0 5.7 %all-to-all-start = ((bf16[4,48,1024]{2,1,0:T(8,128)(2,1)}), bf16[4,48,1024]{2,1,0:T(8,128)(2,1)S(1)}, u32[]{:S(2)}, u32[]{:S(2)}) async-start(bf16[4,48,1024]{2,1,0:T(8,128)(2,1)} %bitcast.171), calls=%async_computation.1 | async-start | bytes 786432 | tf_op jit(solution)/shard_map/all_to_all | solution.py:18
  96.0 13.7 %all_gather.15 = bf16[192,1024]{1,0:T(8,128)(2,1)S(1)} all-gather(bf16[48,1024]{1,0:T(8,128)(2,1)S(1)} %copy_bitcast_fusion.1), channel_id=1, replica_groups=mesh['zl'=4,'x'=4,'y'=4,'zh'=4,'c'=2] {'y'}, dimensions={0}, use_global_device_ids=true | all-gather | bytes 491520 | tf_op jit(solution)/shard_map/all_gather | solution.py:146
  112.1 3.5 %all-to-all-start.3 = ((bf16[4,48,256]{2,1,0:T(8,128)(2,1)}), bf16[4,48,256]{2,1,0:T(8,128)(2,1)S(1)}, u32[]{:S(2)}, u32[]{:S(2)}) async-start(bf16[4,48,256]{2,1,0:T(8,128)(2,1)} %bitcast.28), calls=%async_computation.4 | async-start | bytes 196608 | tf_op jit(solution)/shard_map/all_to_all | solution.py:18
  115.7 6.7 %all-to-all-done.3 = bf16[4,48,256]{2,1,0:T(8,128)(2,1)S(1)} async-done(((bf16[4,48,256]{2,1,0:T(8,128)(2,1)}), bf16[4,48,256]{2,1,0:T(8,128)(2,1)S(1)}, u32[]{:S(2)}, u32[]{:S(2)}) %all-to-all-start.3) | async-done | bytes 98336 | tf_op jit(solution)/shard_map/all_to_all | solution.py:18
  124.0 3.4 %all-to-all-start.4 = ((bf16[8,88,128]{2,1,0:T(8,128)(2,1)}), bf16[8,88,128]{2,1,0:T(8,128)(2,1)S(1)}, u32[]{:S(2)}, u32[]{:S(2)}) async-start(bf16[8,88,128]{2,1,0:T(8,128)(2,1)} %broadcast_in_dim.120), calls=%async_computation.5 | async-start | bytes 360448 | tf_op jit(solution)/shard_map/all_to_all | solution.py:18
  127.6 2.4 fusion
  131.4 15.7 %all-to-all-done.4 = bf16[8,88,128]{2,1,0:T(8,128)(2,1)S(1)} async-done(((bf16[8,88,128]{2,1,0:T(8,128)(2,1)}), bf16[8,88,128]{2,1,0:T(8,128)(2,1)S(1)}, u32[]{:S(2)}, u32[]{:S(2)}) %all-to-all-start.4) | async-done | bytes 180256 | tf_op jit(solution)/shard_map/all_to_all | solution.py:18
  149.3 3.6 %all-to-all-start.5 = ((bf16[4,80,1024]{2,1,0:T(8,128)(2,1)}), bf16[4,80,1024]{2,1,0:T(8,128)(2,1)S(1)}, u32[]{:S(2)}, u32[]{:S(2)}) async-start(bf16[4,80,1024]{2,1,0:T(8,128)(2,1)} %pad_maximum_fusion.2), calls=%async_computation.6 | async-start | bytes 1310720 | tf_op jit(solution)/shard_map/all_to_all | solution.py:18
  154.4 16.3 %all-to-all-done.5 = bf16[4,80,1024]{2,1,0:T(8,128)(2,1)S(1)} async-done(((bf16[4,80,1024]{2,1,0:T(8,128)(2,1)}), bf16[4,80,1024]{2,1,0:T(8,128)(2,1)S(1)}, u32[]{:S(2)}, u32[]{:S(2)}) %all-to-all-start.5) | async-done | bytes 655392 | tf_op jit(solution)/shard_map/all_to_all | solution.py:18
  171.3 1.8 maximum_maximum_fusion
  173.2 6.0 %all-to-all-start.6 = ((bf16[16,200,256]{2,1,0:T(8,128)(2,1)}), bf16[16,200,256]{2,1,0:T(8,128)(2,1)S(1)}, u32[]{:S(2)}, u32[]{:S(2)}) async-start(bf16[16,200,256]{2,1,0:T(8,128)(2,1)} %maximum_maximum_fusion), calls=%async_computation.7 | async-start | bytes 3276800 | tf_op jit(solution)/shard_map/all_to_all | solution.py:18
  179.1 22.8 %reduce-scatter.5.cloned.1.call-done = bf16[304,128]{1,0:T(8,128)(2,1)} async-done(((bf16[2432,128]{1,0:T(8,128)(2,1)}), bf16[304,128]{1,0:T(8,128)(2,1)}) %reduce-scatter.5.cloned.1.call-update) | async-done | bytes 77840 | tf_op jit(solution)/shard_map/reduce_scatter | solution.py:181
  205.2 7.2 %all-to-all-start.7 = ((bf16[64,15,128]{2,1,0:T(8,128)(2,1)}), bf16[64,15,128]{2,1,0:T(8,128)(2,1)S(1)}, u32[]{:S(2)}, u32[]{:S(2)}) async-start(bf16[64,15,128]{2,1,0:T(8,128)(2,1)} %pad_maximum_fusion.4), calls=%async_computation.9 | async-start | bytes 524288 | tf_op jit(solution)/shard_map/all_to_all | solution.py:18
  214.2 1.3 slice.175
  215.5 3.1 %fusion.2 = bf16[320,256]{1,0:T(8,128)(2,1)S(1)} fusion(bf16[3072,256]{1,0:T(8,128)(2,1)} %bitcast.158, bf16[3072,320]{1,0:T(8,128)(2,1)} %all-gather.5.cloned.1.call-done, f32[]{:T(128)S(6)} %convert.12), kind=kOutput, calls=%fused_computation.12 | convolution fusion | flops 503480320 | bytes 3702788 | tf_op jit(solution)/shard_map/dot_general | solution.py:14
  218.7 14.4 %all_gather.19 = bf16[320,1024]{1,0:T(8,128)(2,1)S(1)} all-gather(bf16[320,256]{1,0:T(8,128)(2,1)S(1)} %fusion.2), channel_id=1, replica_groups=mesh['zl'=4,'x'=4,'y'=4,'zh'=4,'c'=2] {'y'}, dimensions={1}, use_global_device_ids=true | all-gather | bytes 819200 | tf_op jit(solution)/shard_map/all_gather | solution.py:219
  (177 shorter events, 26.1 us)
Async XLA Ops:
  8.0 25.1 %copy-start = (bf16[320,1024]{1,0:T(8,128)(2,1)S(1)}, bf16[320,1024]{1,0:T(8,128)(2,1)}, u32[]{:S(2)}) copy-start(bf16[320,1024]{1,0:T(8,128)(2,1)} %param.13) | copy-start | bytes 1966084
  8.0 13.1 %copy-start.10 = (s32[1,16,16]{2,1,0:T(8,128)S(1)}, s32[1,16,16]{2,1,0:T(8,128)}, u32[]{:S(2)}) copy-start(s32[1,16,16]{2,1,0:T(8,128)} %param.19) | copy-start | bytes 3076
  8.0 14.1 %copy-start.12 = (s32[256]{0:T(256)S(1)}, s32[256]{0:T(256)}, u32[]{:S(2)}) copy-start(s32[256]{0:T(256)} %param.22) | copy-start | bytes 3076
  8.0 14.1 %copy-start.13 = (s32[256]{0:T(256)S(1)}, s32[256]{0:T(256)}, u32[]{:S(2)}) copy-start(s32[256]{0:T(256)} %param.21) | copy-start | bytes 3076
  8.1 14.8 %copy-start.6 = (bf16[256,128]{1,0:T(8,128)(2,1)S(1)}, bf16[256,128]{1,0:T(8,128)(2,1)}, u32[]{:S(2)}) copy-start(bf16[256,128]{1,0:T(8,128)(2,1)} %param.23) | copy-start | bytes 196612
  8.1 24.7 %copy-start.5 = (bf16[768,320]{0,1:T(8,128)(2,1)S(1)}, bf16[768,320]{0,1:T(8,128)(2,1)}, u32[]{:S(2)}) copy-start(bf16[768,320]{0,1:T(8,128)(2,1)} %param.12) | copy-start | bytes 1474564
  10.1 29.6 %collective-permute-start.1 = (bf16[640,128]{1,0:T(8,128)(2,1)S(1)}, bf16[640,128]{1,0:T(8,128)(2,1)S(1)}, u32[]{:S(2)}, u32[]{:S(2)}) collective-permute-start(bf16[640,128]{1,0:T(8,128)(2,1)S(1)} %get-tuple-element.21), channel_id=1, source_target_pairs={{0,16},{8,24},{16,0},{24,8},{1,17},{9,25},{17,1},{25,9},{2,18},{10... | collective-permute-start | bytes 491528 | tf_op jit(solution)/shard_map/ppermute | solution.py:109
  15.2 24.5 %collective-permute-start.2 = (bf16[640,128]{1,0:T(8,128)(2,1)S(1)}, bf16[640,128]{1,0:T(8,128)(2,1)S(1)}, u32[]{:S(2)}, u32[]{:S(2)}) collective-permute-start(bf16[640,128]{1,0:T(8,128)(2,1)S(1)} %get-tuple-element.22), channel_id=1, source_target_pairs={{0,24},{8,0},{16,8},{24,16},{1,25},{9,1},{17,9},{25,17},{2,26},{10... | collective-permute-start | bytes 491528 | tf_op jit(solution)/shard_map/ppermute | solution.py:109
  18.2 21.6 %collective-permute-start = (bf16[640,128]{1,0:T(8,128)(2,1)S(1)}, bf16[640,128]{1,0:T(8,128)(2,1)S(1)}, u32[]{:S(2)}, u32[]{:S(2)}) collective-permute-start(bf16[640,128]{1,0:T(8,128)(2,1)S(1)} %get-tuple-element.20), channel_id=1, source_target_pairs={{0,8},{8,16},{16,24},{24,0},{1,9},{9,17},{17,25},{25,1},{2,10},{10... | collective-permute-start | bytes 491528 | tf_op jit(solution)/shard_map/ppermute | solution.py:109
  23.8 15.7 %all-to-all-start.1 = ((bf16[16,6,128]{2,1,0:T(8,128)(2,1)}), bf16[16,6,128]{2,1,0:T(8,128)(2,1)S(1)}, u32[]{:S(2)}, u32[]{:S(2)}) async-start(bf16[16,6,128]{2,1,0:T(8,128)(2,1)} %reshape.404), calls=%async_computation.2 | async-start | bytes 65536 | tf_op jit(solution)/shard_map/all_to_all | solution.py:18
  32.7 57.3 %reduce-scatter.3.cloned.1.call-start = ((), (), s32[]{:S(2)}) async-start(), calls=%async_computation.10 | async-start | bytes 1966080 | tf_op jit(solution)/shard_map/reduce_scatter | solution.py:67
  35.3 92.3 %all-gather.3.cloned.1.call-start = ((), (), s32[]{:S(2)}) async-start(), calls=%async_computation.11 | async-start | bytes 2621440 | tf_op jit(solution)/shard_map/all_gather | solution.py:156
  90.0 21.1 %copy-start.1 = (bf16[4,64,1024]{2,1,0:T(8,128)(2,1)S(1)}, bf16[4,64,1024]{2,1,0:T(8,128)(2,1)}, u32[]{:S(2)}) copy-start(bf16[4,64,1024]{2,1,0:T(8,128)(2,1)} %slice.149) | copy-start | bytes 1572868
  90.0 19.8 %all-to-all-start = ((bf16[4,48,1024]{2,1,0:T(8,128)(2,1)}), bf16[4,48,1024]{2,1,0:T(8,128)(2,1)S(1)}, u32[]{:S(2)}, u32[]{:S(2)}) async-start(bf16[4,48,1024]{2,1,0:T(8,128)(2,1)} %bitcast.171), calls=%async_computation.1 | async-start | bytes 786432 | tf_op jit(solution)/shard_map/all_to_all | solution.py:18
  112.1 10.3 %all-to-all-start.3 = ((bf16[4,48,256]{2,1,0:T(8,128)(2,1)}), bf16[4,48,256]{2,1,0:T(8,128)(2,1)S(1)}, u32[]{:S(2)}, u32[]{:S(2)}) async-start(bf16[4,48,256]{2,1,0:T(8,128)(2,1)} %bitcast.28), calls=%async_computation.4 | async-start | bytes 196608 | tf_op jit(solution)/shard_map/all_to_all | solution.py:18
  124.0 23.0 %all-to-all-start.4 = ((bf16[8,88,128]{2,1,0:T(8,128)(2,1)}), bf16[8,88,128]{2,1,0:T(8,128)(2,1)S(1)}, u32[]{:S(2)}, u32[]{:S(2)}) async-start(bf16[8,88,128]{2,1,0:T(8,128)(2,1)} %broadcast_in_dim.120), calls=%async_computation.5 | async-start | bytes 360448 | tf_op jit(solution)/shard_map/all_to_all | solution.py:18
  130.0 17.4 %copy-start.9 = (bf16[48,128]{1,0:T(8,128)(2,1)S(1)}, bf16[48,128]{1,0:T(8,128)(2,1)}, u32[]{:S(2)}) copy-start(bf16[48,128]{1,0:T(8,128)(2,1)} %copy-done.8) | copy-start | bytes 36868
  130.1 18.3 %copy-start.2 = (bf16[38,8,8,128]{3,2,0,1:T(8,128)(2,1)}, bf16[38,8,8,128]{3,2,0,1:T(8,128)(2,1)S(1)}, u32[]{:S(2)}) copy-start(bf16[38,8,8,128]{3,2,0,1:T(8,128)(2,1)S(1)} %copy.242) | copy-start | bytes 1867780
  149.3 21.3 %all-to-all-start.5 = ((bf16[4,80,1024]{2,1,0:T(8,128)(2,1)}), bf16[4,80,1024]{2,1,0:T(8,128)(2,1)S(1)}, u32[]{:S(2)}, u32[]{:S(2)}) async-start(bf16[4,80,1024]{2,1,0:T(8,128)(2,1)} %pad_maximum_fusion.2), calls=%async_computation.6 | async-start | bytes 1310720 | tf_op jit(solution)/shard_map/all_to_all | solution.py:18
  153.0 49.0 %reduce-scatter.5.cloned.1.call-start = ((), (), s32[]{:S(2)}) async-start(), calls=%async_computation.12 | async-start | bytes 700416 | tf_op jit(solution)/shard_map/reduce_scatter | solution.py:181
  153.7 61.8 %all-gather.5.cloned.1.call-start = ((), (), s32[]{:S(2)}) async-start(), calls=%async_computation.13 | async-start | bytes 2949120 | tf_op jit(solution)/shard_map/all_gather | solution.py:68
  173.2 29.9 %copy-start.14 = (pred[96]{0:T(512)(128)(4,1)S(1)}, pred[96]{0:T(512)(128)(4,1)}, u32[]{:S(2)}) copy-start(pred[96]{0:T(512)(128)(4,1)} %get-tuple-element.37) | copy-start | bytes 292
  173.2 31.1 %all-to-all-start.6 = ((bf16[16,200,256]{2,1,0:T(8,128)(2,1)}), bf16[16,200,256]{2,1,0:T(8,128)(2,1)S(1)}, u32[]{:S(2)}, u32[]{:S(2)}) async-start(bf16[16,200,256]{2,1,0:T(8,128)(2,1)} %maximum_maximum_fusion), calls=%async_computation.7 | async-start | bytes 3276800 | tf_op jit(solution)/shard_map/all_to_all | solution.py:18
  205.2 29.1 %all-to-all-start.7 = ((bf16[64,15,128]{2,1,0:T(8,128)(2,1)}), bf16[64,15,128]{2,1,0:T(8,128)(2,1)S(1)}, u32[]{:S(2)}, u32[]{:S(2)}) async-start(bf16[64,15,128]{2,1,0:T(8,128)(2,1)} %pad_maximum_fusion.4), calls=%async_computation.9 | async-start | bytes 524288 | tf_op jit(solution)/shard_map/all_to_all | solution.py:18
  (5 other events, 18.5 us)
Sparse Core Ops, SparseCore 0:
  36.4 33.1 reduce-scatter.2
  156.6 45.2 reduce-scatter.4
Sparse Core Ops, SparseCore 1:
  90.1 34.2 all-gather.2
  156.3 50.3 all-gather.4

commit v9 on v8

--- a/solution.py
+++ b/solution.py
@@ -65,7 +65,8 @@
     by_x = jnp.moveaxis(frames.reshape(nzl, nx, n_frames, frames.shape[1]), 1, 0)
     partial = dot(by_x.reshape(frames.shape), projector, 1, 0).astype(bf16)
     x_sum = lax.psum_scatter(partial, "x", scatter_dimension=0, tiled=True)
-    all_frames = lax.all_gather(by_x.reshape(frames.shape), "y", axis=0, tiled=True)
+    all_frames = jnp.pad(by_x.reshape(nx, nzl * n_frames, -1), ((0, 0), (0, 8), (0, 0)))
+    all_frames = lax.all_gather(all_frames.reshape(nx * (nzl * n_frames + 8), -1), "y", axis=0, tiled=True)
 
     own_sizes = pick_entry(clip_len[0], grp_index, 0)
     before = lax.broadcasted_iota(jnp.int32, (ng, ng), 1) < lax.broadcasted_iota(jnp.int32, (ng, ng), 0)
@@ -214,8 +215,8 @@
     n_d = width // cols
     down_grad = last[:, :n_d].reshape(rank, width).astype(f32).T
     up_grad = last[:, n_d].astype(f32)
-    all_grad = came[:, :n_x].reshape(ny * nx * n_x, quarter)
-    projector_grad = after(dot(all_frames, all_grad, 0, 0), summed).astype(bf16)
+    all_grad = came.reshape(ny * nx * (n_x + 8), quarter)
+    projector_grad = dot(all_frames, all_grad, 0, 0).astype(bf16)
     projector_grad = lax.all_gather(projector_grad, "y", axis=1, tiled=True).astype(f32)
 
     in_slots = last[:, -cap:].reshape(nzl, ny, nx * cap, cols)

time: 245 us -> 260 us (1.061)
  local copies, waits for them, and re-layouts: 13.3 us -> 22.1 us
  other arithmetic: 8.08 us -> 13.3 us
  waiting for transfers between devices: 66.2 us -> 62.8 us
  matrix products: 13.2 us -> 16 us
    unnamed x36 -> x70, local copies, waits for them, and re-layouts: 3.03 us -> 8.56 us
    all_to_all x7, waiting for transfers between devices: 42 us -> 38.4 us  [exchange(): return lax.all_to_all(blocks, axis, split_axis=0, concat_axis=0, tiled=True)]
    all_gather x0 -> x1, local copies, waits for them, and re-layouts: none -> 3.42 us  [shards(): lax.all_gather(all_frames.reshape(nx * (nzl * n_frames + 8), -1), 'y', ax...]
    dot_general x17, matrix products: 13.2 us -> 16 us  [dot(): lax.dot_general(a, b, (((ca,), (cb,)), ((), ())), preferred_element_type=...]
  transfers between devices with their start and end apart: 14 -> 14, of which waited for: 6 -> 6; matrix products, arithmetic and copies ran while one was open for 11% -> 14% of each run, Pallas kernels for 0% -> 0%
where the time goes in v9:
time: 260 us; the launch traced here: 258 us
  blocking collectives  75.2 us (29%)
  waiting for transfers between devices  62.8 us (24%)
  starting transfers between devices  51 us (20%)
  local copies, waits for them, and re-layouts  22.1 us (8%)
  between operations  17.8 us (7%)
  matrix products  16 us (6%)
  other arithmetic  13.3 us (5%)
    all_to_all x7, starting transfers between devices, exchange(): return lax.all_to_all(blocks, axis, split_axis=0, concat_axis=0, tiled=True)  40 us
    all_to_all x7, waiting for transfers between devices, exchange(): return lax.all_to_all(blocks, axis, split_axis=0, concat_axis=0, tiled=True)  38.4 us
    all_to_all x1, blocking collectives, exchange(): return lax.all_to_all(blocks, axis, split_axis=0, concat_axis=0, tiled=True)  34.6 us
    reduce_scatter x1, waiting for transfers between devices, shards(): summed = lax.psum_scatter(base, TP, scatter_dimension=0, tiled=True)  23.6 us
    dot_general x17, matrix products, dot(): lax.dot_general(a, b, (((ca,), (cb,)), ((), ())), preferred_element_type=...  16 us
    all_gather x1, blocking collectives, shards(): grad_all = lax.all_gather(grad_full, 'y', axis=0, tiled=True)  14 us
    all_gather x1, blocking collectives, shards(): lax.all_gather(projector_grad, 'y', axis=1, tiled=True).astype(f32)  13.9 us
    all_gather x1, blocking collectives, shards(): weights = lax.all_gather(weights, 'x')  12.7 us
  transfers between devices with their start and end apart: 14, of which 6 were waited for; matrix products, arithmetic and copies ran while one was open for 14% of the time, Pallas kernels for 0%

profile of v9, /device:TPU:2, one launch (start us, length us, event | category | flops | bytes accessed | tf_op | source)
XLA Modules:
  0.0 258.4 jit_solution(1355783441544190334)
XLA Ops:
  10.1 5.1 %collective-permute-start.1 = (bf16[640,128]{1,0:T(8,128)(2,1)S(1)}, bf16[640,128]{1,0:T(8,128)(2,1)S(1)}, u32[]{:S(2)}, u32[]{:S(2)}) collective-permute-start(bf16[640,128]{1,0:T(8,128)(2,1)S(1)} %get-tuple-element.21), channel_id=1, source_target_pairs={{0,16},{8,24},{16,0},{24,8},{1,17},{9,25},{17,1},{25,9},{2,18},{10... | collective-permute-start | bytes 491528 | tf_op jit(solution)/shard_map/ppermute | solution.py:110
  15.2 3.0 %collective-permute-start.2 = (bf16[640,128]{1,0:T(8,128)(2,1)S(1)}, bf16[640,128]{1,0:T(8,128)(2,1)S(1)}, u32[]{:S(2)}, u32[]{:S(2)}) collective-permute-start(bf16[640,128]{1,0:T(8,128)(2,1)S(1)} %get-tuple-element.22), channel_id=1, source_target_pairs={{0,24},{8,0},{16,8},{24,16},{1,25},{9,1},{17,9},{25,17},{2,26},{10... | collective-permute-start | bytes 491528 | tf_op jit(solution)/shard_map/ppermute | solution.py:110
  18.2 2.9 %collective-permute-start = (bf16[640,128]{1,0:T(8,128)(2,1)S(1)}, bf16[640,128]{1,0:T(8,128)(2,1)S(1)}, u32[]{:S(2)}, u32[]{:S(2)}) collective-permute-start(bf16[640,128]{1,0:T(8,128)(2,1)S(1)} %get-tuple-element.20), channel_id=1, source_target_pairs={{0,8},{8,16},{16,24},{24,0},{1,9},{9,17},{17,25},{25,1},{2,10},{10... | collective-permute-start | bytes 491528 | tf_op jit(solution)/shard_map/ppermute | solution.py:110
  24.3 8.9 %all-to-all-start.1 = ((bf16[16,6,128]{2,1,0:T(8,128)(2,1)}), bf16[16,6,128]{2,1,0:T(8,128)(2,1)S(1)}, u32[]{:S(2)}, u32[]{:S(2)}) async-start(bf16[16,6,128]{2,1,0:T(8,128)(2,1)} %reshape.405), calls=%async_computation.2 | async-start | bytes 65536 | tf_op jit(solution)/shard_map/all_to_all | solution.py:18
  33.7 2.1 convolution_convert_fusion
  38.0 2.0 all-to-all-done.1
  42.0 34.6 %all_to_all.40 = bf16[8,160,128]{2,1,0:T(8,128)(2,1)S(1)} all-to-all(bf16[8,160,128]{2,1,0:T(8,128)(2,1)S(1)} %pad_maximum_fusion.3), channel_id=1, replica_groups=mesh['zl'=4,'x'=4,'y'=4,'zh'=4,'c'=2] {'zh','c'}, dimensions={0} | all-to-all | bytes 655360 | tf_op jit(solution)/shard_map/all_to_all | solution.py:18
  77.5 12.7 %all_gather.16 = bf16[4,80,1024]{2,1,0:T(8,128)(2,1)S(1)} all-gather(bf16[1,80,1024]{2,1,0:T(8,128)(2,1)S(1)} %all_gather_reshape.3), channel_id=1, replica_groups=mesh['zl'=4,'x'=4,'y'=4,'zh'=4,'c'=2] {'x'}, dimensions={0}, use_global_device_ids=true | all-gather | bytes 819200 | tf_op jit(solution)/shard_map/all_gather | solution.py:149
  91.1 6.5 %all-to-all-start = ((bf16[4,48,1024]{2,1,0:T(8,128)(2,1)}), bf16[4,48,1024]{2,1,0:T(8,128)(2,1)S(1)}, u32[]{:S(2)}, u32[]{:S(2)}) async-start(bf16[4,48,1024]{2,1,0:T(8,128)(2,1)} %bitcast.172), calls=%async_computation.1 | async-start | bytes 786432 | tf_op jit(solution)/shard_map/all_to_all | solution.py:18
  100.2 14.0 %all_gather.15 = bf16[192,1024]{1,0:T(8,128)(2,1)S(1)} all-gather(bf16[48,1024]{1,0:T(8,128)(2,1)S(1)} %copy_bitcast_fusion.1), channel_id=1, replica_groups=mesh['zl'=4,'x'=4,'y'=4,'zh'=4,'c'=2] {'y'}, dimensions={0}, use_global_device_ids=true | all-gather | bytes 491520 | tf_op jit(solution)/shard_map/all_gather | solution.py:147
  117.6 4.0 %all-to-all-start.3 = ((bf16[4,48,256]{2,1,0:T(8,128)(2,1)}), bf16[4,48,256]{2,1,0:T(8,128)(2,1)S(1)}, u32[]{:S(2)}, u32[]{:S(2)}) async-start(bf16[4,48,256]{2,1,0:T(8,128)(2,1)} %bitcast.28), calls=%async_computation.4 | async-start | bytes 196608 | tf_op jit(solution)/shard_map/all_to_all | solution.py:18
  122.6 4.7 %all-to-all-done.3 = bf16[4,48,256]{2,1,0:T(8,128)(2,1)S(1)} async-done(((bf16[4,48,256]{2,1,0:T(8,128)(2,1)}), bf16[4,48,256]{2,1,0:T(8,128)(2,1)S(1)}, u32[]{:S(2)}, u32[]{:S(2)}) %all-to-all-start.3) | async-done | bytes 98336 | tf_op jit(solution)/shard_map/all_to_all | solution.py:18
  129.0 4.0 %all-to-all-start.4 = ((bf16[8,88,128]{2,1,0:T(8,128)(2,1)}), bf16[8,88,128]{2,1,0:T(8,128)(2,1)}, u32[]{:S(2)}, u32[]{:S(2)}) async-start(bf16[8,88,128]{2,1,0:T(8,128)(2,1)} %broadcast_in_dim.120), calls=%async_computation.5 | async-start | bytes 360448 | tf_op jit(solution)/shard_map/all_to_all | solution.py:18
  133.2 2.4 fusion
  136.9 15.8 %all-to-all-done.4 = bf16[8,88,128]{2,1,0:T(8,128)(2,1)} async-done(((bf16[8,88,128]{2,1,0:T(8,128)(2,1)}), bf16[8,88,128]{2,1,0:T(8,128)(2,1)}, u32[]{:S(2)}, u32[]{:S(2)}) %all-to-all-start.4) | async-done | bytes 180256 | tf_op jit(solution)/shard_map/all_to_all | solution.py:18
  161.2 3.6 %all-to-all-start.5 = ((bf16[4,80,1024]{2,1,0:T(8,128)(2,1)}), bf16[4,80,1024]{2,1,0:T(8,128)(2,1)S(1)}, u32[]{:S(2)}, u32[]{:S(2)}) async-start(bf16[4,80,1024]{2,1,0:T(8,128)(2,1)} %pad_maximum_fusion.2), calls=%async_computation.6 | async-start | bytes 1310720 | tf_op jit(solution)/shard_map/all_to_all | solution.py:18
  166.9 15.6 %all-to-all-done.5 = bf16[4,80,1024]{2,1,0:T(8,128)(2,1)S(1)} async-done(((bf16[4,80,1024]{2,1,0:T(8,128)(2,1)}), bf16[4,80,1024]{2,1,0:T(8,128)(2,1)S(1)}, u32[]{:S(2)}, u32[]{:S(2)}) %all-to-all-start.5) | async-done | bytes 655392 | tf_op jit(solution)/shard_map/all_to_all | solution.py:18
  185.0 4.7 %all-to-all-start.6 = ((bf16[16,200,256]{2,1,0:T(8,128)(2,1)}), bf16[16,200,256]{2,1,0:T(8,128)(2,1)S(1)}, u32[]{:S(2)}, u32[]{:S(2)}) async-start(bf16[16,200,256]{2,1,0:T(8,128)(2,1)} %maximum_maximum_fusion), calls=%async_computation.7 | async-start | bytes 3276800 | tf_op jit(solution)/shard_map/all_to_all | solution.py:18
  189.7 23.6 %reduce-scatter.5.cloned.1.call-done = bf16[304,128]{1,0:T(8,128)(2,1)} async-done(((bf16[2432,128]{1,0:T(8,128)(2,1)}), bf16[304,128]{1,0:T(8,128)(2,1)}) %reduce-scatter.5.cloned.1.call-update) | async-done | bytes 77840 | tf_op jit(solution)/shard_map/reduce_scatter | solution.py:182
  216.1 8.2 %all-to-all-start.7 = ((bf16[64,15,128]{2,1,0:T(8,128)(2,1)}), bf16[64,15,128]{2,1,0:T(8,128)(2,1)S(1)}, u32[]{:S(2)}, u32[]{:S(2)}) async-start(bf16[64,15,128]{2,1,0:T(8,128)(2,1)} %pad_maximum_fusion.4), calls=%async_computation.9 | async-start | bytes 524288 | tf_op jit(solution)/shard_map/all_to_all | solution.py:18
  224.4 3.4 %copy.250 = bf16[4,800,320]{1,0,2:T(4,128)(2,1)S(1)} copy(bf16[4,800,320]{1,2,0:T(8,128)(2,1)} %all-gather.6.cloned.1.call-done) | data formatting | bytes 4096000 | tf_op jit(solution)/shard_map/all_gather | solution.py:69
  227.8 2.9 %reshape.431 = bf16[3200,320]{0,1:T(8,128)(2,1)} reshape(bf16[4,800,320]{1,0,2:T(4,128)(2,1)S(1)} %copy.250) | data formatting | bytes 4096000
  230.7 2.8 %convolution_convert_fusion.2 = bf16[320,256]{1,0:T(8,128)(2,1)S(1)} fusion(bf16[3200,320]{0,1:T(8,128)(2,1)} %reshape.431, bf16[3200,256]{1,0:T(8,128)(2,1)} %bitcast.159), kind=kOutput, calls=%fused_computation.8 | convolution fusion | flops 524369920 | bytes 3850240 | tf_op jit(solution)/shard_map/dot_general | solution.py:14
  233.5 13.9 %all_gather.19 = bf16[320,1024]{1,0:T(8,128)(2,1)S(1)} all-gather(bf16[320,256]{1,0:T(8,128)(2,1)S(1)} %convolution_convert_fusion.2), channel_id=1, replica_groups=mesh['zl'=4,'x'=4,'y'=4,'zh'=4,'c'=2] {'y'}, dimensions={1}, use_global_device_ids=true | all-gather | bytes 819200 | tf_op jit(solution)/shard_map/all_gather | solution.py:220
  (211 shorter events, 39.2 us)
Async XLA Ops:
  8.0 25.7 %copy-start = (bf16[320,1024]{1,0:T(8,128)(2,1)S(1)}, bf16[320,1024]{1,0:T(8,128)(2,1)}, u32[]{:S(2)}) copy-start(bf16[320,1024]{1,0:T(8,128)(2,1)} %param.13) | copy-start | bytes 1966084
  10.1 30.2 %collective-permute-start.1 = (bf16[640,128]{1,0:T(8,128)(2,1)S(1)}, bf16[640,128]{1,0:T(8,128)(2,1)S(1)}, u32[]{:S(2)}, u32[]{:S(2)}) collective-permute-start(bf16[640,128]{1,0:T(8,128)(2,1)S(1)} %get-tuple-element.21), channel_id=1, source_target_pairs={{0,16},{8,24},{16,0},{24,8},{1,17},{9,25},{17,1},{25,9},{2,18},{10... | collective-permute-start | bytes 491528 | tf_op jit(solution)/shard_map/ppermute | solution.py:110
  15.2 25.1 %collective-permute-start.2 = (bf16[640,128]{1,0:T(8,128)(2,1)S(1)}, bf16[640,128]{1,0:T(8,128)(2,1)S(1)}, u32[]{:S(2)}, u32[]{:S(2)}) collective-permute-start(bf16[640,128]{1,0:T(8,128)(2,1)S(1)} %get-tuple-element.22), channel_id=1, source_target_pairs={{0,24},{8,0},{16,8},{24,16},{1,25},{9,1},{17,9},{25,17},{2,26},{10... | collective-permute-start | bytes 491528 | tf_op jit(solution)/shard_map/ppermute | solution.py:110
  18.2 22.1 %collective-permute-start = (bf16[640,128]{1,0:T(8,128)(2,1)S(1)}, bf16[640,128]{1,0:T(8,128)(2,1)S(1)}, u32[]{:S(2)}, u32[]{:S(2)}) collective-permute-start(bf16[640,128]{1,0:T(8,128)(2,1)S(1)} %get-tuple-element.20), channel_id=1, source_target_pairs={{0,8},{8,16},{16,24},{24,0},{1,9},{9,17},{17,25},{25,1},{2,10},{10... | collective-permute-start | bytes 491528 | tf_op jit(solution)/shard_map/ppermute | solution.py:110
  24.3 15.7 %all-to-all-start.1 = ((bf16[16,6,128]{2,1,0:T(8,128)(2,1)}), bf16[16,6,128]{2,1,0:T(8,128)(2,1)S(1)}, u32[]{:S(2)}, u32[]{:S(2)}) async-start(bf16[16,6,128]{2,1,0:T(8,128)(2,1)} %reshape.405), calls=%async_computation.2 | async-start | bytes 65536 | tf_op jit(solution)/shard_map/all_to_all | solution.py:18
  33.2 57.8 %reduce-scatter.3.cloned.1.call-start = ((), (), s32[]{:S(2)}) async-start(), calls=%async_computation.10 | async-start | bytes 1966080 | tf_op jit(solution)/shard_map/reduce_scatter | solution.py:67
  35.8 97.4 %all-gather.4.cloned.1.call-start = ((), (), s32[]{:S(2)}) async-start(), calls=%async_computation.11 | async-start | bytes 2621440 | tf_op jit(solution)/shard_map/all_gather | solution.py:157
  40.9 35.6 %copy-start.8 = (bf16[1,512,128]{2,1,0:T(8,128)(2,1)}, bf16[1,512,128]{2,1,0:T(8,128)(2,1)S(1)}, u32[]{:S(2)}) copy-start(bf16[1,512,128]{2,1,0:T(8,128)(2,1)S(1)} %constant_dynamic-slice_fusion.2) | copy-start | bytes 393220
  91.0 25.6 %copy-start.1 = (bf16[4,64,1024]{2,1,0:T(8,128)(2,1)S(1)}, bf16[4,64,1024]{2,1,0:T(8,128)(2,1)}, u32[]{:S(2)}) copy-start(bf16[4,64,1024]{2,1,0:T(8,128)(2,1)} %slice.141) | copy-start | bytes 1572868
  91.1 24.2 %all-to-all-start = ((bf16[4,48,1024]{2,1,0:T(8,128)(2,1)}), bf16[4,48,1024]{2,1,0:T(8,128)(2,1)S(1)}, u32[]{:S(2)}, u32[]{:S(2)}) async-start(bf16[4,48,1024]{2,1,0:T(8,128)(2,1)} %bitcast.172), calls=%async_computation.1 | async-start | bytes 786432 | tf_op jit(solution)/shard_map/all_to_all | solution.py:18
  100.2 27.2 %copy-start.9 = (bf16[1,512,128]{2,1,0:T(8,128)(2,1)S(1)}, bf16[1,512,128]{2,1,0:T(8,128)(2,1)}, u32[]{:S(2)}) copy-start(bf16[1,512,128]{2,1,0:T(8,128)(2,1)} %copy-done.8) | copy-start | bytes 393220
  117.6 9.8 %all-to-all-start.3 = ((bf16[4,48,256]{2,1,0:T(8,128)(2,1)}), bf16[4,48,256]{2,1,0:T(8,128)(2,1)S(1)}, u32[]{:S(2)}, u32[]{:S(2)}) async-start(bf16[4,48,256]{2,1,0:T(8,128)(2,1)} %bitcast.28), calls=%async_computation.4 | async-start | bytes 196608 | tf_op jit(solution)/shard_map/all_to_all | solution.py:18
  129.0 23.7 %all-to-all-start.4 = ((bf16[8,88,128]{2,1,0:T(8,128)(2,1)}), bf16[8,88,128]{2,1,0:T(8,128)(2,1)}, u32[]{:S(2)}, u32[]{:S(2)}) async-start(bf16[8,88,128]{2,1,0:T(8,128)(2,1)} %broadcast_in_dim.120), calls=%async_computation.5 | async-start | bytes 360448 | tf_op jit(solution)/shard_map/all_to_all | solution.py:18
  161.2 21.3 %all-to-all-start.5 = ((bf16[4,80,1024]{2,1,0:T(8,128)(2,1)}), bf16[4,80,1024]{2,1,0:T(8,128)(2,1)S(1)}, u32[]{:S(2)}, u32[]{:S(2)}) async-start(bf16[4,80,1024]{2,1,0:T(8,128)(2,1)} %pad_maximum_fusion.2), calls=%async_computation.6 | async-start | bytes 1310720 | tf_op jit(solution)/shard_map/all_to_all | solution.py:18
  164.8 48.5 %reduce-scatter.5.cloned.1.call-start = ((), (), s32[]{:S(2)}) async-start(), calls=%async_computation.12 | async-start | bytes 700416 | tf_op jit(solution)/shard_map/reduce_scatter | solution.py:182
  165.5 58.9 %all-gather.6.cloned.1.call-start = ((), (), s32[]{:S(2)}) async-start(), calls=%async_computation.13 | async-start | bytes 2867200 | tf_op jit(solution)/shard_map/all_gather | solution.py:69
  185.0 28.3 %copy-start.13 = (f32[256,64]{1,0:T(8,128)S(1)}, f32[256,64]{1,0:T(8,128)}, u32[]{:S(2)}) copy-start(f32[256,64]{1,0:T(8,128)} %copy-done.12) | copy-start | bytes 196612
  185.0 28.3 %copy-start.17 = (bf16[64,128]{1,0:T(8,128)(2,1)S(1)}, bf16[64,128]{1,0:T(8,128)(2,1)}, u32[]{:S(2)}) copy-start(bf16[64,128]{1,0:T(8,128)(2,1)} %param.18) | copy-start | bytes 49156
  185.0 28.3 %copy-start.19 = (f32[48,64]{1,0:T(8,128)S(1)}, f32[48,64]{1,0:T(8,128)}, u32[]{:S(2)}) copy-start(f32[48,64]{1,0:T(8,128)} %copy-done.18) | copy-start | bytes 36868
  185.0 29.4 %copy-start.29 = (s32[96]{0:T(128)S(1)}, s32[96]{0:T(128)}, u32[]{:S(2)}) copy-start(s32[96]{0:T(128)} %get-tuple-element.39) | copy-start | bytes 1156
  185.0 29.4 %copy-start.30 = (pred[96]{0:T(512)(128)(4,1)S(1)}, pred[96]{0:T(512)(128)(4,1)}, u32[]{:S(2)}) copy-start(pred[96]{0:T(512)(128)(4,1)} %get-tuple-element.37) | copy-start | bytes 292
  185.0 29.9 %all-to-all-start.6 = ((bf16[16,200,256]{2,1,0:T(8,128)(2,1)}), bf16[16,200,256]{2,1,0:T(8,128)(2,1)S(1)}, u32[]{:S(2)}, u32[]{:S(2)}) async-start(bf16[16,200,256]{2,1,0:T(8,128)(2,1)} %maximum_maximum_fusion), calls=%async_computation.7 | async-start | bytes 3276800 | tf_op jit(solution)/shard_map/all_to_all | solution.py:18
  189.7 34.6 %copy-start.11 = (pred[256,16,6]{0,2,1:T(8,128)(4,1)S(1)}, pred[256,16,6]{0,2,1:T(8,128)(4,1)}, u32[]{:S(2)}) copy-start(pred[256,16,6]{0,2,1:T(8,128)(4,1)} %get-tuple-element.29) | copy-start | bytes 73732
  216.1 32.6 %all-to-all-start.7 = ((bf16[64,15,128]{2,1,0:T(8,128)(2,1)}), bf16[64,15,128]{2,1,0:T(8,128)(2,1)S(1)}, u32[]{:S(2)}, u32[]{:S(2)}) async-start(bf16[64,15,128]{2,1,0:T(8,128)(2,1)} %pad_maximum_fusion.4), calls=%async_computation.9 | async-start | bytes 524288 | tf_op jit(solution)/shard_map/all_to_all | solution.py:18
  (21 other events, 209.0 us)
Sparse Core Ops, SparseCore 0:
  36.9 33.1 reduce-scatter.2
  168.5 44.7 reduce-scatter.4
Sparse Core Ops, SparseCore 1:
  91.1 34.4 all-gather.3
  168.1 49.6 all-gather.5
